TPU v7x, 128 devices: a whole 4x4x4 slice. The times are simulated.
128 devices in a mesh: dom: 16 (over z, y_hi, core), rot: 8 (over y_lo, x).
Axes of the slice: x: 4, y: 4 (y_hi: 2, y_lo: 2; y = y_hi * 2 + y_lo), z: 4, core: 2. Of those that a mesh axis runs over, the one named last changes fastest.
Arguments:
- particles: bfloat16 [128, 64, 4096], P('dom'), may hold values from -6 to 6
- references: bfloat16 [32, 64, 4096], P('rot', 'dom'), may hold values from -6 to 6
- part_class: int32 [128, 1], P('dom'), may hold values from 0 to 7; in each aligned block of 8 rows (0 to 7, 8 to 15, ...) at most 4 rows name the same one
- part_rot: int32 [128], P('dom'), may hold values from 0 to 3
- bucket: int32 [128], P('dom'), may hold values from 0 to 7
- bucket_weights: bfloat16 [8], replicated, may hold values from 0.25 to 2
- live_count: int32 [16], P('dom'), may hold values from 4 to 8, as said below
Outputs:
- scores: float32 [128, 512], P('dom')
- sums: float32 [64, 32, 64, 128], P('dom', 'rot')
Inputs may be any that keep to these rules, and one draw needn't show every extreme that they name: `part_class`: among the 8 particles of one index of dom no class is named more than 4 times, and some class is named 4 times in some such block. `live_count`: some block has all 8 particles in use.
All inputs are finite; a program needn't handle non-finite values.
Results may differ from a plain program's by a relative error of at most 0.014.
Values may be sent and summed in bfloat16 or wider, within the bound.
No kernel may reach another device: no remote copies, remote signals or barrier semaphores. Data moves between devices by JAX's collectives and lax.ppermute only.
A program may use at most 192 MiB of HBM per device.

v0:
```python
import math

import jax
import jax.numpy as jnp
import numpy as np
from jax import lax
from jax.experimental import pallas as pl
from jax.experimental.pallas import tpu as pltpu
from jax.sharding import PartitionSpec as P

BOX = 64
SHIFTS = 8
ROT_CLS = 4
CAP = 4
HALF = 33
KXP = 48
KXV = 40
PAIRS = BOX // 2
DOM = 16
CHIPS = DOM // 2
SAME_CORE = [[2 * chip + core for chip in range(CHIPS)] for core in range(2)]
BF = jnp.bfloat16
F32 = jnp.float32


def grid_cos_sin(rows, cols):
    theta = ((rows[:, None] * cols[None, :]) % BOX).astype(np.float64) * (2.0 * math.pi / BOX)
    return np.cos(theta), np.sin(theta)


def x_half_table():
    c, s = grid_cos_sin(np.arange(BOX), np.arange(BOX))
    out = np.zeros((2, KXP, BOX))
    out[0, :HALF] = c[:HALF]
    out[1, :HALF] = -s[:HALF]
    return out.reshape(2 * KXP, BOX)


def z_complex_table():
    c, s = grid_cos_sin(np.arange(BOX), np.arange(BOX))
    two = np.eye(2)
    return np.block([[np.kron(two, c), np.kron(two, -s)], [np.kron(two, s), np.kron(two, c)]])


def shift_tables():
    c, s = grid_cos_sin(np.arange(SHIFTS) - SHIFTS // 2, np.arange(BOX))
    fold = np.zeros((KXV,))
    fold[:HALF] = 2.0
    fold[0] = fold[HALF - 1] = 1.0
    ex = np.zeros((2 * SHIFTS, KXV))
    ex[:SHIFTS, :HALF] = c[:, :HALF]
    ex[SHIFTS:, :HALF] = s[:, :HALF]
    ex = ex * fold[None, :]
    wz = np.zeros((2, 4 * BOX, 128))
    wz[0, :, :SHIFTS] = np.concatenate([c.T, c.T, -s.T, -s.T], axis=0)
    wz[1, :, :SHIFTS] = np.concatenate([-s.T, -s.T, -c.T, -c.T], axis=0)
    return ex, wz.reshape(8 * BOX, 128)


def z_real_table():
    c, s = grid_cos_sin(np.arange(BOX), np.arange(BOX))
    return np.kron(np.eye(2), np.concatenate([c, -s], axis=1))


def y_table():
    c, s = grid_cos_sin(np.arange(BOX), np.arange(BOX))
    return np.concatenate([c, s], axis=0)


def x_rows_table():
    c, s = grid_cos_sin(np.arange(BOX), np.arange(BOX))
    full = []
    for table in (c, s):
        spread = np.einsum(
            "rq,kdx->rkdqx", np.eye(ROT_CLS), table.reshape(BOX, DOM, BOX // DOM)
        ).reshape(ROT_CLS * BOX, ROT_CLS * BOX)
        high = spread.astype(np.float32).astype(BF)
        low = (spread.astype(np.float32) - high.astype(np.float32)).astype(BF)
        full += [high, low]
    return np.stack(full)


def z_stage(src, table, start, count):
    parts = []
    for j in range(start, start + count):
        lanes = slice(128 * j, 128 * (j + 1))
        parts.append(jnp.concatenate([src[0:KXP, lanes], src[KXP : 2 * KXP, lanes]], axis=1))
    return jnp.dot(jnp.concatenate(parts, axis=0), table, preferred_element_type=F32)


STEP = 8
CHUNK = 4
PLANES = BOX // DOM
PER_CHIP = ROT_CLS * PLANES
SEND = CHIPS * PER_CHIP


LANES = 1024


def slot_copies(flat_hbm, flat_s, sems, rows_of):
    return [
        pltpu.make_async_copy(
            flat_hbm.at[pl.ds(pl.multiple_of(rows_of(slot) * BOX, BOX), BOX)],
            flat_s.at[slot * BOX : (slot + 1) * BOX],
            sems.at[slot],
        )
        for slot in range(CAP)
    ]


def send_kernel(
    class_ref,
    rot_ref,
    bucket_ref,
    live_ref,
    level_ref,
    flat_hbm,
    send_out,
    own_out,
    count_out,
    slot_rot_out,
    slot_row_out,
    flat_s,
    spread_s,
    sems,
):
    owner = lax.axis_index("rot")
    core = lax.axis_index("dom") & 1
    count = jnp.int32(0)
    slot_row = [jnp.int32(0) for _ in range(CAP)]
    slot_rot = [jnp.int32(-1) for _ in range(CAP)]
    slot_bucket = [jnp.int32(-1) for _ in range(CAP)]
    for p in range(class_ref.shape[0]):
        mine = (class_ref[p] == owner) & (p < live_ref[0])
        for slot in range(CAP):
            here = mine & (count == slot)
            slot_row[slot] = jnp.where(here, p, slot_row[slot])
            slot_rot[slot] = jnp.where(here, rot_ref[p], slot_rot[slot])
            slot_bucket[slot] = jnp.where(here, bucket_ref[p], slot_bucket[slot])
        count = count + mine.astype(jnp.int32)
    copies = slot_copies(flat_hbm, flat_s, sems, lambda slot: slot_row[slot])
    for copy in copies:
        copy.start()
    count_out[0] = count
    for slot in range(CAP):
        slot_rot_out[slot] = slot_rot[slot]
        slot_row_out[slot] = slot_row[slot]
    columns = CAP * BOX
    lane = lax.broadcasted_iota(jnp.int32, (1, columns), 1)
    col_slot, col_x = lane >> 6, lane & (BOX - 1)
    col_rot = jnp.full((1, columns), -1, jnp.int32)
    col_bucket = jnp.full((1, columns), -1, jnp.int32)
    for slot in range(CAP):
        col_rot = jnp.where(col_slot == slot, slot_rot[slot], col_rot)
        col_bucket = jnp.where(col_slot == slot, slot_bucket[slot], col_bucket)
    levels = level_ref[...].astype(F32)
    col_weight = jnp.zeros((1, columns), F32)
    for level in range(levels.shape[1]):
        value = jnp.broadcast_to(levels[:, level : level + 1], (1, columns))
        col_weight = jnp.where(col_bucket == level, value, col_weight)
    row = lax.broadcasted_iota(jnp.int32, (SEND, columns), 0)
    base = (row // PER_CHIP) * (2 * PLANES) + (row & (PLANES - 1))
    right = ((row // PLANES) & (ROT_CLS - 1)) == col_rot
    for half, to_core in enumerate((core, 1 - core)):
        hit = right & (base + to_core * PLANES == col_x)
        spread_s[half * SEND : (half + 1) * SEND] = jnp.where(hit, col_weight, 0.0).astype(BF)
    for copy in copies:
        copy.wait()
    for start in range(0, BOX * BOX, LANES):
        lanes = slice(start, start + LANES)
        part = jnp.dot(spread_s[...], flat_s[:, lanes], preferred_element_type=F32)
        own_out[:, lanes] = part[:SEND].astype(BF)
        send_out[:, lanes] = part[SEND:].astype(BF)


def pair_kernel(own_ref, other_ref, out_ref):
    out_ref[...] = (own_ref[...].astype(F32) + other_ref[...].astype(F32)).astype(BF)


def spectra_kernel(slot_row_ref, x_ref, flat_hbm, table_ref, spectra_out, flat_s, sems):
    chunk = pl.program_id(0)

    @pl.when(chunk == 0)
    def _():
        copies = slot_copies(flat_hbm, flat_s, sems, lambda slot: slot_row_ref[slot])
        for copy in copies:
            copy.start()
        for copy in copies:
            copy.wait()

    lanes = pl.ds(pl.multiple_of(chunk * 128 * CHUNK, 128 * CHUNK), 128 * CHUNK)
    along_x = jnp.dot(x_ref[...], flat_s[:, lanes], preferred_element_type=F32).astype(BF)
    table = table_ref[...]
    for slot in range(CAP):
        part = z_stage(along_x[slot * 2 * KXP : (slot + 1) * 2 * KXP], table, 0, CHUNK)
        spectra_out[slot] = part.astype(BF)


def score_kernel(
    count_ref,
    slot_rot_ref,
    zp_ref,
    x_ref,
    own_ref,
    other_ref,
    table_ref,
    ex_ref,
    wz_ref,
    out_ref,
    pick_s,
    x_s,
    p_s,
    r_s,
    a_s,
):
    slot = pl.program_id(0)

    @pl.when((slot == 0) & (count_ref[0] > 0))
    def _():
        core = lax.axis_index("dom") & 1
        ref_lane = lax.broadcasted_iota(jnp.int32, (1, SEND), 1)
        ref_rot = (ref_lane // PLANES) & (ROT_CLS - 1)
        for to in range(CAP):
            rows = slice(to * 2 * KXP, (to + 1) * 2 * KXP)
            wanted = ref_rot == slot_rot_ref[to]
            pick_s[0, rows] = jnp.where(wanted, x_ref[core], 0.0).astype(BF)
            pick_s[1, rows] = jnp.where(wanted, x_ref[1 - core], 0.0).astype(BF)
        for start in range(0, BOX * BOX, 512):
            lanes = slice(start, start + 512)
            part = jnp.dot(pick_s[0], own_ref[:, lanes], preferred_element_type=F32)
            part = part + jnp.dot(pick_s[1], other_ref[:, lanes], preferred_element_type=F32)
            x_s[:, :, lanes] = part.astype(BF).reshape(CAP, 2 * KXP, 512)

    @pl.when(slot < count_ref[0])
    def _():
        table = table_ref[...]
        xr = x_s.at[slot]
        for start in range(0, PAIRS, STEP):
            part = z_stage(xr, table, start, STEP)
            part = part.astype(BF).astype(F32).reshape(STEP, KXP, 4 * BOX)
            r_s[start : start + STEP] = part[:, :KXV, :]
            mine = zp_ref[start * KXP : (start + STEP) * KXP, :].astype(F32)
            p_s[start : start + STEP] = mine.reshape(STEP, KXP, 4 * BOX)[:, :KXV, :]
        first = lax.broadcasted_iota(jnp.int32, (8, 128), 1) < BOX

        def column(col, carry):
            rows = pl.ds(pl.multiple_of(col * 8, 8), 8)

            def pair(m):
                return r_s[m % PAIRS, rows, 0:128], r_s[m % PAIRS, rows, 128:256]

            def shifted(before, now):
                return tuple(
                    pltpu.roll(jnp.where(first, n, b), BOX, 1) for b, n in zip(before, now)
                )

            def three(re, im):
                return re, im, re - im

            tiles = {m: pair(m) for m in range(-2, 2)}
            even = {m: three(*tiles[m]) for m in range(-1, 2)}
            odd = {m: three(*shifted(tiles[m - 1], tiles[m])) for m in range(-1, 2)}
            last = tiles[1]
            sums = [[jnp.zeros((8, 128), F32) for _ in range(3)] for _ in range(SHIFTS)]
            for j in range(PAIRS):
                new = pair(j + 2)
                even[j + 2] = three(*new)
                odd[j + 2] = three(*shifted(last, new))
                last = new
                pr = p_s[j, rows, 0:128]
                pi = p_s[j, rows, 128:256]
                both = pr + pi
                for u in range(-2, 2):
                    for parity, held in ((0, even), (1, odd)):
                        t = 2 * u + parity + SHIFTS // 2
                        rr, ri, rd = held[j - u]
                        sums[t][0] = sums[t][0] + pr * rr
                        sums[t][1] = sums[t][1] + pi * ri
                        sums[t][2] = sums[t][2] + both * rd
                del even[j - 1], odd[j - 1]
            for t in range(SHIFTS):
                one, two, mix = sums[t]
                a_s[t, rows, 0:128] = one + two
                a_s[t, rows, 128:256] = mix - one + two
            return carry

        lax.fori_loop(0, KXV // 8, column, 0)
        ex = ex_ref[...]
        along_x = [
            jnp.dot(ex, a_s[t].astype(BF), preferred_element_type=F32) for t in range(SHIFTS)
        ]
        cos_rows = jnp.concatenate([u[:SHIFTS] for u in along_x], axis=0).astype(BF)
        sin_rows = jnp.concatenate([u[SHIFTS:] for u in along_x], axis=0).astype(BF)
        both_rows = jnp.concatenate([cos_rows, sin_rows], axis=1)
        final = jnp.dot(both_rows, wz_ref[...], preferred_element_type=F32)
        out_ref[...] = final * (float(BOX) ** -3.5)

    @pl.when(slot >= count_ref[0])
    def _():
        out_ref[...] = jnp.zeros_like(out_ref)


def yz_kernel(parts_ref, table_hbm, out_ref, z_s, g_s, table_ref, sem):
    copy = pltpu.make_async_copy(table_hbm, table_ref, sem)
    copy.start()
    total = parts_ref[0:PER_CHIP].astype(F32)
    for chip in range(1, CHIPS):
        total = total + parts_ref[chip * PER_CHIP : (chip + 1) * PER_CHIP].astype(F32)
    total = total.astype(BF)
    copy.wait()
    z_ref, y_ref = table_ref[: 2 * BOX], table_ref[2 * BOX :, :BOX]
    stacked = jnp.concatenate([total[:, 128 * j : 128 * (j + 1)] for j in range(PAIRS)], axis=0)
    z_part = jnp.dot(stacked, z_ref, preferred_element_type=F32)
    for j in range(PAIRS):
        for half in range(2):
            start = (2 * j + half) * PER_CHIP
            z_s[start : start + PER_CHIP] = z_part[
                j * PER_CHIP : (j + 1) * PER_CHIP, 128 * half : 128 * (half + 1)
            ]
    by_y = [z_s[pl.ds(n, BOX, stride=PER_CHIP), :].astype(BF) for n in range(PER_CHIP)]
    y_part = jnp.dot(y_ref, jnp.concatenate(by_y, axis=1), preferred_element_type=F32)
    first = lax.broadcasted_iota(jnp.int32, (BOX, 128), 1) < BOX
    for n in range(PER_CHIP):
        lanes = slice(128 * n, 128 * (n + 1))
        turned = pltpu.roll(y_part[BOX:, lanes], BOX, 1)
        g_s[pl.ds(n, BOX, stride=PER_CHIP), :] = y_part[:BOX, lanes] + jnp.where(first, turned, -turned)
    out_ref[...] = g_s[...].astype(BF)


def x_rows_kernel(rows_ref, table_hbm, out_ref, table_ref, sem):
    copy = pltpu.make_async_copy(table_hbm, table_ref, sem)
    copy.start()
    copy.wait()
    rows = ROT_CLS * (BOX // DOM)
    first = lax.broadcasted_iota(jnp.int32, (ROT_CLS * BOX, 128), 1) < BOX
    for ky in range(BOX // DOM):
        grid = rows_ref[:, ky * rows : (ky + 1) * rows, :].reshape(ROT_CLS * BOX, 128)
        cos_part = jnp.dot(table_ref[0], grid, preferred_element_type=F32)
        cos_part = cos_part + jnp.dot(table_ref[1], grid, preferred_element_type=F32)
        sin_part = jnp.dot(table_ref[2], grid, preferred_element_type=F32)
        sin_part = sin_part + jnp.dot(table_ref[3], grid, preferred_element_type=F32)
        turned = pltpu.roll(sin_part, BOX, 1)
        total = (cos_part + jnp.where(first, turned, -turned)) * (float(BOX) ** -1.5)
        out_ref[ky] = total.reshape(ROT_CLS, BOX, 128)


VMEM = pl.BlockSpec(memory_space=pltpu.VMEM)
HBM = pl.BlockSpec(memory_space=pltpu.HBM)
SMEM = pl.BlockSpec(memory_space=pltpu.SMEM)


def params(mib):
    return pltpu.CompilerParams(vmem_limit_bytes=mib * 1024 * 1024)


def cost(flops, moved):
    return pl.CostEstimate(flops=flops, bytes_accessed=moved, transcendentals=0)


def shards(particles, references, part_class, part_rot, bucket, bucket_weights, live_count):
    block_size = particles.shape[0]
    voxels = BOX * BOX
    columns = block_size * BOX
    to_other = [(i, i ^ 1) for i in range(DOM)]

    mine_refs = jnp.tile(references.reshape(PER_CHIP, voxels), (CHIPS, 1))

    flat = particles.reshape(columns, voxels)
    classes = part_class.reshape(block_size)
    x_half = x_half_table()
    by_core = x_half.reshape(2 * KXP, CHIPS, 2, 1, PLANES)
    by_core = np.broadcast_to(by_core, (2 * KXP, CHIPS, 2, ROT_CLS, PLANES))
    by_core = by_core.transpose(2, 0, 1, 3, 4).reshape(2, 2 * KXP, SEND)
    held = [
        pltpu.VMEM((CAP * BOX, voxels), BF),
        pltpu.SemaphoreType.DMA((CAP,)),
    ]

    def whole(*shape):
        return pl.BlockSpec(shape, lambda s: (0,) * len(shape))

    to_send, own, count, slot_rot, slot_row = pl.pallas_call(
        send_kernel,
        out_shape=(
            jax.ShapeDtypeStruct((SEND, voxels), BF),
            jax.ShapeDtypeStruct((SEND, voxels), BF),
            jax.ShapeDtypeStruct((1,), jnp.int32),
            jax.ShapeDtypeStruct((CAP,), jnp.int32),
            jax.ShapeDtypeStruct((CAP,), jnp.int32),
        ),
        in_specs=[SMEM, SMEM, SMEM, SMEM, VMEM, HBM],
        out_specs=(VMEM, VMEM, SMEM, SMEM, SMEM),
        scratch_shapes=[held[0], pltpu.VMEM((2 * SEND, CAP * BOX), BF), held[1]],
        compiler_params=params(54),
        cost_estimate=cost(1024, 1024),
        name="send",
    )(
        classes,
        part_rot,
        bucket,
        live_count,
        bucket_weights.reshape(1, -1),
        flat,
    )
    other = lax.ppermute(to_send, "dom", to_other)
    refs_own = lax.all_to_all(
        mine_refs, "dom", 0, 0, tiled=True, axis_index_groups=SAME_CORE
    )
    pair_sum = pl.pallas_call(
        pair_kernel,
        out_shape=jax.ShapeDtypeStruct((SEND, voxels), BF),
        in_specs=[VMEM, VMEM],
        out_specs=VMEM,
        compiler_params=params(50),
        cost_estimate=cost(1024, 1024),
        name="pair",
    )(own, other)
    arrived = lax.all_to_all(pair_sum, "dom", 0, 0, tiled=True, axis_index_groups=SAME_CORE)

    z_table = jnp.asarray(z_complex_table().astype(BF))
    spectra = pl.pallas_call(
        spectra_kernel,
        out_shape=jax.ShapeDtypeStruct((CAP, PAIRS * KXP, 4 * BOX), BF),
        grid=(PAIRS // CHUNK,),
        in_specs=[
            SMEM,
            whole(CAP * 2 * KXP, CAP * BOX),
            HBM,
            whole(4 * BOX, 4 * BOX),
        ],
        out_specs=pl.BlockSpec((CAP, CHUNK * KXP, 4 * BOX), lambda i: (0, i, 0)),
        scratch_shapes=held,
        compiler_params=params(54),
        cost_estimate=cost(1024, 1024),
        name="spectra",
    )(slot_row, jnp.asarray(np.kron(np.eye(CAP), x_half).astype(BF)), flat, z_table)

    refs_own, spectra = lax.optimization_barrier((refs_own, spectra))
    refs_other = lax.ppermute(refs_own, "dom", to_other)
    ex, wz = shift_tables()

    slots = pl.pallas_call(
        score_kernel,
        out_shape=jax.ShapeDtypeStruct((CAP, SHIFTS * SHIFTS, 128), F32),
        grid=(CAP,),
        in_specs=[
            SMEM,
            SMEM,
            pl.BlockSpec((None, PAIRS * KXP, 4 * BOX), lambda s: (s, 0, 0)),
            whole(2, 2 * KXP, SEND),
            whole(SEND, voxels),
            whole(SEND, voxels),
            whole(4 * BOX, 4 * BOX),
            whole(2 * SHIFTS, KXV),
            whole(8 * BOX, 128),
        ],
        out_specs=pl.BlockSpec((None, SHIFTS * SHIFTS, 128), lambda s: (s, 0, 0)),
        scratch_shapes=[
            pltpu.VMEM((2, CAP * 2 * KXP, SEND), BF),
            pltpu.VMEM((CAP, 2 * KXP, voxels), BF),
            pltpu.VMEM((PAIRS, KXV, 4 * BOX), F32),
            pltpu.VMEM((PAIRS, KXV, 4 * BOX), F32),
            pltpu.VMEM((SHIFTS, KXV, 4 * BOX), F32),
        ],
        compiler_params=params(50),
        cost_estimate=cost(1024, 1024),
        name="slot_scores",
    )(
        count,
        slot_rot,
        spectra,
        jnp.asarray(by_core, F32),
        refs_own,
        refs_other,
        z_table,
        jnp.asarray(ex.astype(BF)),
        jnp.asarray(wz.astype(BF)),
    )
    slot_scores = slots[:, :, :SHIFTS].reshape(CAP, SHIFTS, SHIFTS, SHIFTS)
    slot_scores = slot_scores.transpose(0, 2, 1, 3).reshape(CAP, SHIFTS**3)
    everywhere = slot_scores
    for bit in (1, 2, 4):
        held_there = lax.ppermute(everywhere, "rot", [(i, i ^ bit) for i in range(8)])
        everywhere = jnp.concatenate([everywhere, held_there], axis=0)
    rows_all = jnp.arange(block_size, dtype=jnp.int32)
    alive = rows_all < live_count[0]
    before = (classes[:, None] == classes[None, :]) & (rows_all[None, :] < rows_all[:, None])
    place = (classes ^ lax.axis_index("rot")) * CAP + jnp.sum(before.astype(jnp.int32), axis=1)
    found = (place[:, None] == jnp.arange(8 * CAP, dtype=jnp.int32)[None, :]) & alive[:, None]
    scores = jnp.sum(jnp.where(found[:, :, None], everywhere[None, :, :], 0.0), axis=1)

    yz_table = np.zeros((4 * BOX, 4 * BOX))
    yz_table[: 2 * BOX] = z_real_table()
    yz_table[2 * BOX :, :BOX] = y_table()
    grids = pl.pallas_call(
        yz_kernel,
        out_shape=jax.ShapeDtypeStruct((BOX * PER_CHIP, 2 * BOX), BF),
        in_specs=[VMEM, HBM],
        out_specs=VMEM,
        scratch_shapes=[
            pltpu.VMEM((BOX * PER_CHIP, 128), F32),
            pltpu.VMEM((BOX * PER_CHIP, 128), F32),
            pltpu.VMEM((4 * BOX, 4 * BOX), BF),
            pltpu.SemaphoreType.DMA,
        ],
        compiler_params=params(50),
        cost_estimate=cost(1024, 1024),
        name="yz_planes",
    )(arrived, jnp.asarray(yz_table.astype(BF)))
    by_rows = lax.all_to_all(grids, "dom", 0, 0, tiled=True)
    sums = pl.pallas_call(
        x_rows_kernel,
        out_shape=jax.ShapeDtypeStruct((BOX // DOM, ROT_CLS, BOX, 2 * BOX), F32),
        in_specs=[VMEM, HBM],
        out_specs=VMEM,
        scratch_shapes=[
            pltpu.VMEM((4, ROT_CLS * BOX, ROT_CLS * BOX), BF),
            pltpu.SemaphoreType.DMA,
        ],
        compiler_params=params(50),
        name="x_rows",
    )(by_rows.reshape(DOM, PLANES * PER_CHIP, 2 * BOX), jnp.asarray(x_rows_table()))
    return (scores, sums)


def solution(mesh):
    return jax.shard_map(
        shards,
        mesh=mesh,
        in_specs=(
            P("dom", None, None),
            P("rot", "dom", None),
            P("dom", None),
            P("dom"),
            P("dom"),
            P(),
            P("dom"),
        ),
        out_specs=(P("dom", None), P("dom", "rot", None, None)),
        check_vma=False,
    )
```

profile of v0, /device:TPU:1, one launch (start us, length us, event | category | flops | bytes accessed | tf_op | source)
XLA Modules:
  0.0 68.0 jit_solution(604376049838095667)
XLA Ops:
  0.6 0.9 %tile.8 = bf16[16,4096]{1,0:T(8,128)(2,1)S(1)} reshape(bf16[4,4,4096]{2,1,0:T(4,128)(2,1)} %param.15) | data formatting | bytes 262144 | tf_op jit(solution)/shard_map/tile | solution.py:367
  1.6 1.1 %tile.9 = bf16[8,16,4096]{2,1,0:T(8,128)(2,1)} broadcast(bf16[16,4096]{1,0:T(8,128)(2,1)S(1)} %tile.8), dimensions={1,2} | broadcast | bytes 1179648 | tf_op jit(solution)/shard_map/tile | solution.py:367
  2.7 8.5 %all-to-all-start = ((bf16[8,16,4096]{2,1,0:T(8,128)(2,1)}), bf16[8,16,4096]{2,1,0:T(8,128)(2,1)S(1)}, u32[]{:S(2)}, u32[]{:S(2)}) async-start(bf16[8,16,4096]{2,1,0:T(8,128)(2,1)} %tile.9), calls=%async_computation | async-start | bytes 2097152 | tf_op jit(solution)/shard_map/all_to_all | solution.py:407
  11.8 4.7 %send.1 = (bf16[128,4096]{1,0:T(8,128)(2,1)}, bf16[128,4096]{1,0:T(8,128)(2,1)}, s32[1]{0:T(128)}, s32[4]{0:T(128)}, s32[4]{0:T(128)}) custom-call(s32[8]{0:T(128)} %bitcast.28, s32[8]{0:T(128)} %rot_ref.1, s32[8]{0:T(128)} %bucket_ref.1, s32[1]{0:T(128)} %copy.20.live_ref, bf16[1,8]{1,0:T(2,128)(2,1)} %bitcast.30, bf16[512,4096]{1,0:T(8,128)(2,1)} %bitcast.25), custom_call_target="tpu_custom_call" | custom-call | flops 1024 | bytes 1024 | tf_op jit(solution)/shard_map/send/pallas_call | solution.py:383
  16.6 0.9 %collective-permute-start.4 = (bf16[128,4096]{1,0:T(8,128)(2,1)}, bf16[128,4096]{1,0:T(8,128)(2,1)S(1)}, u32[]{:S(2)}, u32[]{:S(2)}) collective-permute-start(bf16[128,4096]{1,0:T(8,128)(2,1)} %get-tuple-element.15), channel_id=1, source_target_pairs={{0,8},{8,0},{16,24},{24,16},{32,40},{40,32},{48,56},{56,48},{64,72... | collective-permute-start | bytes 3145736 | tf_op jit(solution)/shard_map/ppermute | solution.py:406
  17.5 8.3 %spectra.1.zp_ref = bf16[4,1536,256]{2,1,0:T(8,128)(2,1)} custom-call(s32[4]{0:T(128)} %get-tuple-element.11.slot_row_ref, bf16[384,256]{1,0:T(8,128)(2,1)} %constant.25.clone.x_ref, bf16[512,4096]{1,0:T(8,128)(2,1)} %bitcast.26, bf16[256,256]{1,0:T(8,128)(2,1)} %constant.24.clone.table_ref), custom_call_target="tpu_custom_call" | custom-call | flops 1024 | bytes 1024 | tf_op jit(solution)/shard_map/spectra/pallas_call | solution.py:422
  25.8 0.0 copy-start.8
  25.8 0.0 copy-start.1
  25.8 0.0 copy-start.3
  25.9 0.0 copy-start.5
  25.9 0.0 copy-start.6
  25.9 1.3 %all-to-all-done = bf16[8,16,4096]{2,1,0:T(8,128)(2,1)S(1)} async-done(((bf16[8,16,4096]{2,1,0:T(8,128)(2,1)}), bf16[8,16,4096]{2,1,0:T(8,128)(2,1)S(1)}, u32[]{:S(2)}, u32[]{:S(2)}) %all-to-all-start) | async-done | bytes 1048608 | tf_op jit(solution)/shard_map/all_to_all | solution.py:407
  27.2 2.2 %collective-permute-start = (bf16[128,4096]{1,0:T(8,128)(2,1)S(1)}, bf16[128,4096]{1,0:T(8,128)(2,1)}, u32[]{:S(2)}, u32[]{:S(2)}) collective-permute-start(bf16[128,4096]{1,0:T(8,128)(2,1)S(1)} %bitcast.23), channel_id=1, source_target_pairs={{0,8},{8,0},{16,24},{24,16},{32,40},{40,32},{48,56},{56,48},{64,72... | collective-permute-start | bytes 3145736 | tf_op jit(solution)/shard_map/ppermute | solution.py:440
  29.3 0.0 collective-permute-done.4.other_ref
  29.3 1.2 %pair.1 = bf16[128,4096]{1,0:T(8,128)(2,1)} custom-call(bf16[128,4096]{1,0:T(8,128)(2,1)S(1)} %copy-done, bf16[128,4096]{1,0:T(8,128)(2,1)S(1)} %collective-permute-done.4.other_ref), custom_call_target="tpu_custom_call" | custom-call | flops 1024 | bytes 1024 | tf_op jit(solution)/shard_map/pair/pallas_call | solution.py:410
  30.6 3.7 %all-to-all-start.1 = ((bf16[8,16,4096]{2,1,0:T(8,128)(2,1)}), bf16[8,16,4096]{2,1,0:T(8,128)(2,1)S(1)}, u32[]{:S(2)}, u32[]{:S(2)}) async-start(bf16[8,16,4096]{2,1,0:T(8,128)(2,1)} %bitcast.9), calls=%async_computation.1 | async-start | bytes 2097152 | tf_op jit(solution)/shard_map/all_to_all | solution.py:419
  34.3 0.2 convert_reduce_fusion
  34.5 0.0 copy-start.2
  34.5 3.7 %slot_scores.1 = f32[4,64,128]{2,1,0:T(8,128)S(1)} custom-call(s32[1]{0:T(128)} %get-tuple-element.9.count_ref, s32[4]{0:T(128)S(1)} %copy-done.7, bf16[4,1536,256]{2,1,0:T(8,128)(2,1)} %spectra.1.zp_ref, f32[2,96,128]{2,1,0:T(8,128)S(1)} %copy-done.5, bf16[128,4096]{1,0:T(8,128)(2,1)S(1)} %bitcast.24, bf16[128,4096]{1,0:T(8,128)(2,1)} %collective-permute-done.other_ref, ...), custom_call_target="tpu_custom_call" | custom-call | flops 1024 | bytes 1024 | tf_op jit(solution)/shard_map/slot_scores/pallas_call | solution.py:443
  38.3 0.1 reshape.77
  38.4 1.3 %collective-permute-start.1 = (f32[4,512]{1,0:T(4,128)S(1)}, f32[4,512]{1,0:T(4,128)S(1)}, u32[]{:S(2)}, u32[]{:S(2)}) collective-permute-start(f32[4,512]{1,0:T(4,128)S(1)} %reshape.77), channel_id=1, source_target_pairs={{0,1},{1,0},{2,3},{3,2},{4,5},{5,4},{6,7},{7,6},{8,9},{9,8},{10,11... | collective-permute-start | bytes 24584 | tf_op jit(solution)/shard_map/ppermute | solution.py:484
  39.7 1.6 %collective-permute-done.1 = f32[4,512]{1,0:T(4,128)S(1)} collective-permute-done((f32[4,512]{1,0:T(4,128)S(1)}, f32[4,512]{1,0:T(4,128)S(1)}, u32[]{:S(2)}, u32[]{:S(2)}) %collective-permute-start.1) | collective-permute-done | bytes 8224 | tf_op jit(solution)/shard_map/ppermute | solution.py:484
  41.3 3.0 %collective-permute-start.2 = (f32[8,512]{1,0:T(8,128)S(1)}, f32[8,512]{1,0:T(8,128)S(1)}, u32[]{:S(2)}, u32[]{:S(2)}) collective-permute-start(f32[8,512]{1,0:T(8,128)S(1)} %pad_maximum_fusion.2), channel_id=1, source_target_pairs={{0,2},{1,3},{2,0},{3,1},{4,6},{5,7},{6,4},{7,5},{8,10},{9,11},{10,... | collective-permute-start | bytes 49160 | tf_op jit(solution)/shard_map/ppermute | solution.py:484
  44.4 6.4 %all-to-all-done.1 = bf16[8,16,4096]{2,1,0:T(8,128)(2,1)S(1)} async-done(((bf16[8,16,4096]{2,1,0:T(8,128)(2,1)}), bf16[8,16,4096]{2,1,0:T(8,128)(2,1)S(1)}, u32[]{:S(2)}, u32[]{:S(2)}) %all-to-all-start.1) | async-done | bytes 1048608 | tf_op jit(solution)/shard_map/all_to_all | solution.py:419
  50.8 1.8 %yz_planes.1 = bf16[1024,128]{1,0:T(8,128)(2,1)} custom-call(bf16[128,4096]{1,0:T(8,128)(2,1)S(1)} %bitcast.22, bf16[256,256]{1,0:T(8,128)(2,1)S(1)} %copy-done.4), custom_call_target="tpu_custom_call" | custom-call | flops 1024 | bytes 1024 | tf_op jit(solution)/shard_map/yz_planes/pallas_call | solution.py:496
  52.6 5.0 %all-to-all-start.2 = ((bf16[16,64,128]{2,1,0:T(8,128)(2,1)}), bf16[16,64,128]{2,1,0:T(8,128)(2,1)S(1)}, u32[]{:S(2)}, u32[]{:S(2)}) async-start(bf16[16,64,128]{2,1,0:T(8,128)(2,1)} %bitcast.11), calls=%async_computation.2 | async-start | bytes 524288 | tf_op jit(solution)/shard_map/all_to_all | solution.py:511
  57.7 1.2 %collective-permute-start.3 = (f32[16,512]{1,0:T(8,128)S(1)}, f32[16,512]{1,0:T(8,128)S(1)}, u32[]{:S(2)}, u32[]{:S(2)}) collective-permute-start(f32[16,512]{1,0:T(8,128)S(1)} %pad_maximum_fusion.1), channel_id=1, source_target_pairs={{0,4},{1,5},{2,6},{3,7},{4,0},{5,1},{6,2},{7,3},{8,12},{9,13},{10,... | collective-permute-start | bytes 98312 | tf_op jit(solution)/shard_map/ppermute | solution.py:484
  58.8 0.1 fusion.1
  58.9 4.6 %collective-permute-done.3 = f32[16,512]{1,0:T(8,128)S(1)} collective-permute-done((f32[16,512]{1,0:T(8,128)S(1)}, f32[16,512]{1,0:T(8,128)S(1)}, u32[]{:S(2)}, u32[]{:S(2)}) %collective-permute-start.3) | collective-permute-done | bytes 32800 | tf_op jit(solution)/shard_map/ppermute | solution.py:484
  63.5 0.7 %select_reduce_fusion = f32[8,512]{1,0:T(8,128)} fusion(f32[32,512]{1,0:T(8,128)S(1)} %pad_maximum_fusion, pred[8,32]{1,0:T(8,128)(4,1)S(1)} %fusion.1), kind=kLoop, calls=%fused_computation | loop fusion | flops 258048 | bytes 82176 | tf_op jit(solution)/shard_map/reduce_sum | solution.py:491
  64.2 2.2 %all-to-all-done.2.rows_ref = bf16[16,64,128]{2,1,0:T(8,128)(2,1)S(1)} async-done(((bf16[16,64,128]{2,1,0:T(8,128)(2,1)}), bf16[16,64,128]{2,1,0:T(8,128)(2,1)S(1)}, u32[]{:S(2)}, u32[]{:S(2)}) %all-to-all-start.2) | async-done | bytes 262176 | tf_op jit(solution)/shard_map/all_to_all | solution.py:511
  66.4 1.6 %x_rows.1 = f32[4,4,64,128]{3,2,1,0:T(8,128)} custom-call(bf16[16,64,128]{2,1,0:T(8,128)(2,1)S(1)} %all-to-all-done.2.rows_ref, bf16[4,256,256]{2,1,0:T(8,128)(2,1)S(1)} %copy-done.2), custom_call_target="tpu_custom_call" | custom-call | tf_op jit(solution)/shard_map/x_rows/pallas_call | solution.py:512
  (21 shorter events, 0.1 us)
Async XLA Ops:
  2.7 24.5 %all-to-all-start = ((bf16[8,16,4096]{2,1,0:T(8,128)(2,1)}), bf16[8,16,4096]{2,1,0:T(8,128)(2,1)S(1)}, u32[]{:S(2)}, u32[]{:S(2)}) async-start(bf16[8,16,4096]{2,1,0:T(8,128)(2,1)} %tile.9), calls=%async_computation | async-start | bytes 2097152 | tf_op jit(solution)/shard_map/all_to_all | solution.py:407
  16.6 12.8 %copy-start = (bf16[128,4096]{1,0:T(8,128)(2,1)S(1)}, bf16[128,4096]{1,0:T(8,128)(2,1)}, u32[]{:S(2)}) copy-start(bf16[128,4096]{1,0:T(8,128)(2,1)} %get-tuple-element.14.own_ref) | copy-start | bytes 3145732
  16.6 12.8 %collective-permute-start.4 = (bf16[128,4096]{1,0:T(8,128)(2,1)}, bf16[128,4096]{1,0:T(8,128)(2,1)S(1)}, u32[]{:S(2)}, u32[]{:S(2)}) collective-permute-start(bf16[128,4096]{1,0:T(8,128)(2,1)} %get-tuple-element.15), channel_id=1, source_target_pairs={{0,8},{8,0},{16,24},{24,16},{32,40},{40,32},{48,56},{56,48},{64,72... | collective-permute-start | bytes 3145736 | tf_op jit(solution)/shard_map/ppermute | solution.py:406
  25.8 8.5 %copy-start.8 = (s32[8,1]{0,1:T(1,128)S(1)}, s32[8,1]{0,1:T(1,128)}, u32[]{:S(2)}) copy-start(s32[8,1]{0,1:T(1,128)} %param.16) | copy-start | bytes 100
  25.8 8.6 %copy-start.1 = (bf16[256,256]{1,0:T(8,128)(2,1)S(1)}, bf16[256,256]{1,0:T(8,128)(2,1)}, u32[]{:S(2)}) copy-start(bf16[256,256]{1,0:T(8,128)(2,1)} %constant.24.clone.table_ref) | copy-start | bytes 393220
  25.8 8.6 %copy-start.3 = (bf16[512,128]{1,0:T(8,128)(2,1)S(1)}, bf16[512,128]{1,0:T(8,128)(2,1)}, u32[]{:S(2)}) copy-start(bf16[512,128]{1,0:T(8,128)(2,1)} %constant.28.clone.wz_ref) | copy-start | bytes 393220
  25.9 8.6 %copy-start.5 = (f32[2,96,128]{2,1,0:T(8,128)S(1)}, f32[2,96,128]{2,1,0:T(8,128)}, u32[]{:S(2)}) copy-start(f32[2,96,128]{2,1,0:T(8,128)} %constant.26.clone.x_ref) | copy-start | bytes 294916
  25.9 8.6 %copy-start.6 = (bf16[16,40]{1,0:T(8,128)(2,1)S(1)}, bf16[16,40]{1,0:T(8,128)(2,1)}, u32[]{:S(2)}) copy-start(bf16[16,40]{1,0:T(8,128)(2,1)} %constant.27.clone.ex_ref) | copy-start | bytes 3844
  25.9 8.6 %copy-start.7 = (s32[4]{0:T(128)S(1)}, s32[4]{0:T(128)}, u32[]{:S(2)}) copy-start(s32[4]{0:T(128)} %get-tuple-element.10.slot_rot_ref) | copy-start | bytes 52
  27.2 7.3 %collective-permute-start = (bf16[128,4096]{1,0:T(8,128)(2,1)S(1)}, bf16[128,4096]{1,0:T(8,128)(2,1)}, u32[]{:S(2)}, u32[]{:S(2)}) collective-permute-start(bf16[128,4096]{1,0:T(8,128)(2,1)S(1)} %bitcast.23), channel_id=1, source_target_pairs={{0,8},{8,0},{16,24},{24,16},{32,40},{40,32},{48,56},{56,48},{64,72... | collective-permute-start | bytes 3145736 | tf_op jit(solution)/shard_map/ppermute | solution.py:440
  30.6 20.2 %copy-start.4 = (bf16[256,256]{1,0:T(8,128)(2,1)S(1)}, bf16[256,256]{1,0:T(8,128)(2,1)}, u32[]{:S(2)}) copy-start(bf16[256,256]{1,0:T(8,128)(2,1)} %constant.29.clone.table_hbm) | copy-start | bytes 393220
  30.6 20.2 %all-to-all-start.1 = ((bf16[8,16,4096]{2,1,0:T(8,128)(2,1)}), bf16[8,16,4096]{2,1,0:T(8,128)(2,1)S(1)}, u32[]{:S(2)}, u32[]{:S(2)}) async-start(bf16[8,16,4096]{2,1,0:T(8,128)(2,1)} %bitcast.9), calls=%async_computation.1 | async-start | bytes 2097152 | tf_op jit(solution)/shard_map/all_to_all | solution.py:419
  34.5 31.8 %copy-start.2 = (bf16[4,256,256]{2,1,0:T(8,128)(2,1)S(1)}, bf16[4,256,256]{2,1,0:T(8,128)(2,1)}, u32[]{:S(2)}) copy-start(bf16[4,256,256]{2,1,0:T(8,128)(2,1)} %constant.30.clone.table_hbm) | copy-start | bytes 1572868
  38.4 2.9 %collective-permute-start.1 = (f32[4,512]{1,0:T(4,128)S(1)}, f32[4,512]{1,0:T(4,128)S(1)}, u32[]{:S(2)}, u32[]{:S(2)}) collective-permute-start(f32[4,512]{1,0:T(4,128)S(1)} %reshape.77), channel_id=1, source_target_pairs={{0,1},{1,0},{2,3},{3,2},{4,5},{5,4},{6,7},{7,6},{8,9},{9,8},{10,11... | collective-permute-start | bytes 24584 | tf_op jit(solution)/shard_map/ppermute | solution.py:484
  41.3 16.3 %collective-permute-start.2 = (f32[8,512]{1,0:T(8,128)S(1)}, f32[8,512]{1,0:T(8,128)S(1)}, u32[]{:S(2)}, u32[]{:S(2)}) collective-permute-start(f32[8,512]{1,0:T(8,128)S(1)} %pad_maximum_fusion.2), channel_id=1, source_target_pairs={{0,2},{1,3},{2,0},{3,1},{4,6},{5,7},{6,4},{7,5},{8,10},{9,11},{10,... | collective-permute-start | bytes 49160 | tf_op jit(solution)/shard_map/ppermute | solution.py:484
  52.6 13.8 %all-to-all-start.2 = ((bf16[16,64,128]{2,1,0:T(8,128)(2,1)}), bf16[16,64,128]{2,1,0:T(8,128)(2,1)S(1)}, u32[]{:S(2)}, u32[]{:S(2)}) async-start(bf16[16,64,128]{2,1,0:T(8,128)(2,1)} %bitcast.11), calls=%async_computation.2 | async-start | bytes 524288 | tf_op jit(solution)/shard_map/all_to_all | solution.py:511
  57.7 5.8 %collective-permute-start.3 = (f32[16,512]{1,0:T(8,128)S(1)}, f32[16,512]{1,0:T(8,128)S(1)}, u32[]{:S(2)}, u32[]{:S(2)}) collective-permute-start(f32[16,512]{1,0:T(8,128)S(1)} %pad_maximum_fusion.1), channel_id=1, source_target_pairs={{0,4},{1,5},{2,6},{3,7},{4,0},{5,1},{6,2},{7,3},{8,12},{9,13},{10,... | collective-permute-start | bytes 98312 | tf_op jit(solution)/shard_map/ppermute | solution.py:484
where the time goes:
time: 69 us; the launch traced here: 68 us
  starting transfers between devices  25.8 us (37%)
  Pallas kernels  21.4 us (31%)
  waiting for transfers between devices  16 us (23%)
  local copies, waits for them, and re-layouts  2.25 us (3%)
  between operations  1.48 us (2%)
  other arithmetic  1.04 us (2%)
    all_to_all x1, starting transfers between devices, shards(): lax.all_to_all(mine_refs, 'dom', 0, 0, tiled=True, axis_index_groups=SAME...  8.49 us
    pallas_call x1, Pallas kernels, shards(): pl.pallas_call(spectra_kernel, out_shape=jax.ShapeDtypeStruct((CAP, PAIRS...  8.32 us
    all_to_all x1, waiting for transfers between devices, shards(): lax.all_to_all(pair_sum, 'dom', 0, 0, tiled=True, axis_index_groups=SAME_...  6.43 us
    ppermute x3, waiting for transfers between devices, shards(): lax.ppermute(everywhere, 'rot', [(i, i ^ bit) for i in range(8)])  6.14 us
    ppermute x3, starting transfers between devices, shards(): lax.ppermute(everywhere, 'rot', [(i, i ^ bit) for i in range(8)])  5.49 us
    all_to_all x1, starting transfers between devices, shards(): by_rows = lax.all_to_all(grids, 'dom', 0, 0, tiled=True)  5.02 us
    pallas_call x1, Pallas kernels, shards(): pl.pallas_call(send_kernel, out_shape=(jax.ShapeDtypeStruct((SEND, voxels...  4.74 us
    pallas_call x1, Pallas kernels, shards(): pl.pallas_call(score_kernel, out_shape=jax.ShapeDtypeStruct((CAP, SHIFTS...  3.71 us
  transfers between devices with their start and end apart: 8, of which 5 were waited for; matrix products, arithmetic and copies ran while one was open for 2% of the time, Pallas kernels for 22%

commit v1 on v0

--- a/solution.py
+++ b/solution.py
@@ -178,23 +178,34 @@
     out_ref[...] = (own_ref[...].astype(F32) + other_ref[...].astype(F32)).astype(BF)
 
 
-def spectra_kernel(slot_row_ref, x_ref, flat_hbm, table_ref, spectra_out, flat_s, sems):
-    chunk = pl.program_id(0)
-
-    @pl.when(chunk == 0)
+def spectra_kernel(slot_row_ref, count_ref, x_ref, flat_hbm, table_ref, spectra_out, flat_s, sems):
+    now = pl.program_id(0)
+    copies = slot_copies(flat_hbm, flat_s, sems, lambda slot: slot_row_ref[slot])
+    for slot, copy in enumerate(copies):
+
+        @pl.when((now == 0) & (slot < count_ref[0]))
+        def _():
+            copy.start()
+
+    for slot, copy in enumerate(copies):
+
+        @pl.when((now == slot) & (slot < count_ref[0]))
+        def _():
+            copy.wait()
+
+    @pl.when(now < count_ref[0])
     def _():
-        copies = slot_copies(flat_hbm, flat_s, sems, lambda slot: slot_row_ref[slot])
-        for copy in copies:
-            copy.start()
-        for copy in copies:
-            copy.wait()
-
-    lanes = pl.ds(pl.multiple_of(chunk * 128 * CHUNK, 128 * CHUNK), 128 * CHUNK)
-    along_x = jnp.dot(x_ref[...], flat_s[:, lanes], preferred_element_type=F32).astype(BF)
-    table = table_ref[...]
-    for slot in range(CAP):
-        part = z_stage(along_x[slot * 2 * KXP : (slot + 1) * 2 * KXP], table, 0, CHUNK)
-        spectra_out[slot] = part.astype(BF)
+        table = table_ref[...]
+        rows = pl.ds(pl.multiple_of(now * BOX, BOX), BOX)
+        for start in range(0, PAIRS, CHUNK):
+            lanes = slice(128 * start, 128 * (start + CHUNK))
+            along_x = jnp.dot(x_ref[...], flat_s[rows, lanes], preferred_element_type=F32)
+            part = z_stage(along_x.astype(BF), table, 0, CHUNK)
+            spectra_out[start * KXP : (start + CHUNK) * KXP, :] = part.astype(BF)
+
+    @pl.when(now >= count_ref[0])
+    def _():
+        spectra_out[...] = jnp.zeros_like(spectra_out)
 
 
 def score_kernel(
@@ -416,27 +427,22 @@
         cost_estimate=cost(1024, 1024),
         name="pair",
     )(own, other)
-    arrived = lax.all_to_all(pair_sum, "dom", 0, 0, tiled=True, axis_index_groups=SAME_CORE)
 
     z_table = jnp.asarray(z_complex_table().astype(BF))
     spectra = pl.pallas_call(
         spectra_kernel,
         out_shape=jax.ShapeDtypeStruct((CAP, PAIRS * KXP, 4 * BOX), BF),
-        grid=(PAIRS // CHUNK,),
-        in_specs=[
-            SMEM,
-            whole(CAP * 2 * KXP, CAP * BOX),
-            HBM,
-            whole(4 * BOX, 4 * BOX),
-        ],
-        out_specs=pl.BlockSpec((CAP, CHUNK * KXP, 4 * BOX), lambda i: (0, i, 0)),
+        grid=(CAP,),
+        in_specs=[SMEM, SMEM, whole(2 * KXP, BOX), HBM, whole(4 * BOX, 4 * BOX)],
+        out_specs=pl.BlockSpec((None, PAIRS * KXP, 4 * BOX), lambda i: (i, 0, 0)),
         scratch_shapes=held,
         compiler_params=params(54),
-        cost_estimate=cost(1024, 1024),
+        cost_estimate=cost(20 * 10**9, 1024),
         name="spectra",
-    )(slot_row, jnp.asarray(np.kron(np.eye(CAP), x_half).astype(BF)), flat, z_table)
-
-    refs_own, spectra = lax.optimization_barrier((refs_own, spectra))
+    )(slot_row, count, jnp.asarray(x_half.astype(BF)), flat, z_table)
+
+    refs_own, spectra, pair_sum = lax.optimization_barrier((refs_own, spectra, pair_sum))
+    arrived = lax.all_to_all(pair_sum, "dom", 0, 0, tiled=True, axis_index_groups=SAME_CORE)
     refs_other = lax.ppermute(refs_own, "dom", to_other)
     ex, wz = shift_tables()
 

time: 69 us -> 70.8 us (1.026)
  the two profiles are of different devices: /device:TPU:1 before, /device:TPU:6 now
where the time goes in v1:
time: 70.8 us; the launch traced here: 70.7 us
  starting transfers between devices  25.5 us (36%)
  waiting for transfers between devices  21.8 us (31%)
  Pallas kernels  16.6 us (23%)
  local copies, waits for them, and re-layouts  4.17 us (6%)
  between operations  1.51 us (2%)
  other arithmetic  1.04 us (1%)
    all_to_all x1, starting transfers between devices, shards(): lax.all_to_all(mine_refs, 'dom', 0, 0, tiled=True, axis_index_groups=SAME...  7.94 us
    ppermute x3, starting transfers between devices, shards(): lax.ppermute(everywhere, 'rot', [(i, i ^ bit) for i in range(8)])  7.2 us
    all_to_all x1, starting transfers between devices, shards(): by_rows = lax.all_to_all(grids, 'dom', 0, 0, tiled=True)  6.61 us
    all_to_all x1, waiting for transfers between devices, shards(): lax.all_to_all(mine_refs, 'dom', 0, 0, tiled=True, axis_index_groups=SAME...  6.5 us
    ppermute x3, waiting for transfers between devices, shards(): lax.ppermute(everywhere, 'rot', [(i, i ^ bit) for i in range(8)])  5.95 us
    all_to_all x1, waiting for transfers between devices, shards(): lax.all_to_all(pair_sum, 'dom', 0, 0, tiled=True, axis_index_groups=SAME_...  4.75 us
    pallas_call x1, Pallas kernels, shards(): pl.pallas_call(send_kernel, out_shape=(jax.ShapeDtypeStruct((SEND, voxels...  4.66 us
    all_to_all x1, waiting for transfers between devices, shards(): by_rows = lax.all_to_all(grids, 'dom', 0, 0, tiled=True)  4.63 us
  transfers between devices with their start and end apart: 8, of which 5 were waited for; matrix products, arithmetic and copies ran while one was open for 2% of the time, Pallas kernels for 15%

profile of v1, /device:TPU:6, one launch (start us, length us, event | category | flops | bytes accessed | tf_op | source)
XLA Modules:
  0.0 70.7 jit_solution(4957075800188596674)
XLA Ops:
  0.6 0.9 %tile.8 = bf16[16,4096]{1,0:T(8,128)(2,1)S(1)} reshape(bf16[4,4,4096]{2,1,0:T(4,128)(2,1)} %param.15) | data formatting | bytes 262144 | tf_op jit(solution)/shard_map/tile | solution.py:378
  1.6 1.1 %tile.9 = bf16[8,16,4096]{2,1,0:T(8,128)(2,1)} broadcast(bf16[16,4096]{1,0:T(8,128)(2,1)S(1)} %tile.8), dimensions={1,2} | broadcast | bytes 1179648 | tf_op jit(solution)/shard_map/tile | solution.py:378
  2.7 7.9 %all-to-all-start = ((bf16[8,16,4096]{2,1,0:T(8,128)(2,1)}), bf16[8,16,4096]{2,1,0:T(8,128)(2,1)S(1)}, u32[]{:S(2)}, u32[]{:S(2)}) async-start(bf16[8,16,4096]{2,1,0:T(8,128)(2,1)} %tile.9), calls=%async_computation | async-start | bytes 2097152 | tf_op jit(solution)/shard_map/all_to_all | solution.py:418
  11.3 4.7 %send.1 = (bf16[128,4096]{1,0:T(8,128)(2,1)}, bf16[128,4096]{1,0:T(8,128)(2,1)}, s32[1]{0:T(128)}, s32[4]{0:T(128)}, s32[4]{0:T(128)}) custom-call(s32[8]{0:T(128)} %bitcast.28, s32[8]{0:T(128)} %rot_ref.1, s32[8]{0:T(128)} %bucket_ref.1, s32[1]{0:T(128)} %copy.20.live_ref, bf16[1,8]{1,0:T(2,128)(2,1)} %bitcast.30, bf16[512,4096]{1,0:T(8,128)(2,1)} %bitcast.25), custom_call_target="tpu_custom_call" | custom-call | flops 1024 | bytes 1024 | tf_op jit(solution)/shard_map/send/pallas_call | solution.py:394
  15.9 0.1 collective-permute-start
  16.0 4.0 %spectra.1.zp_ref = bf16[4,1536,256]{2,1,0:T(8,128)(2,1)} custom-call(s32[4]{0:T(128)} %get-tuple-element.12.slot_row_ref, s32[1]{0:T(128)} %get-tuple-element.10.count_ref, bf16[96,64]{1,0:T(8,128)(2,1)} %constant.25.clone.x_ref, bf16[512,4096]{1,0:T(8,128)(2,1)} %bitcast.26, bf16[256,256]{1,0:T(8,128)(2,1)} %constant.24.clone.table_ref), custom_call_target="tpu_custom_call" | custom-call | flops 20000000000 | bytes 1024 | tf_op jit(solution)/shard_map/spectra/pallas_call | solution.py:432
  20.0 0.0 copy-start.8
  20.0 0.0 copy-start.2
  20.1 0.0 copy-start.3
  20.1 0.0 copy-start.6
  20.1 0.0 collective-permute-done.other_ref
  20.1 1.2 %pair.1 = bf16[128,4096]{1,0:T(8,128)(2,1)} custom-call(bf16[128,4096]{1,0:T(8,128)(2,1)S(1)} %copy-done, bf16[128,4096]{1,0:T(8,128)(2,1)S(1)} %collective-permute-done.other_ref), custom_call_target="tpu_custom_call" | custom-call | flops 1024 | bytes 1024 | tf_op jit(solution)/shard_map/pair/pallas_call | solution.py:421
  21.3 6.5 %all-to-all-done = bf16[8,16,4096]{2,1,0:T(8,128)(2,1)S(1)} async-done(((bf16[8,16,4096]{2,1,0:T(8,128)(2,1)}), bf16[8,16,4096]{2,1,0:T(8,128)(2,1)S(1)}, u32[]{:S(2)}, u32[]{:S(2)}) %all-to-all-start) | async-done | bytes 1048608 | tf_op jit(solution)/shard_map/all_to_all | solution.py:418
  27.8 3.7 %all-to-all-start.1 = ((bf16[8,16,4096]{2,1,0:T(8,128)(2,1)}), bf16[8,16,4096]{2,1,0:T(8,128)(2,1)S(1)}, u32[]{:S(2)}, u32[]{:S(2)}) async-start(bf16[8,16,4096]{2,1,0:T(8,128)(2,1)} %bitcast.9), calls=%async_computation.1 | async-start | bytes 2097152 | tf_op jit(solution)/shard_map/all_to_all | solution.py:445
  31.5 0.2 convert_reduce_fusion
  31.8 0.0 copy-start.5
  31.8 0.9 %copy-done.5 = f32[2,96,128]{2,1,0:T(8,128)S(1)} copy-done((f32[2,96,128]{2,1,0:T(8,128)S(1)}, f32[2,96,128]{2,1,0:T(8,128)}, u32[]{:S(2)}) %copy-start.5) | copy-done | bytes 98328
  32.7 3.3 %slot_scores.1 = f32[4,64,128]{2,1,0:T(8,128)S(1)} custom-call(s32[1]{0:T(128)} %get-tuple-element.10.count_ref, s32[4]{0:T(128)S(1)} %copy-done.7, bf16[4,1536,256]{2,1,0:T(8,128)(2,1)} %spectra.1.zp_ref, f32[2,96,128]{2,1,0:T(8,128)S(1)} %copy-done.5, bf16[128,4096]{1,0:T(8,128)(2,1)S(1)} %bitcast.24, ...), custom_call_target="tpu_custom_call" | custom-call | flops 1024 | bytes 1024 | tf_op jit(solution)/shard_map/slot_scores/pallas_call | solution.py:449
  36.0 0.1 reshape.77
  36.1 4.4 %collective-permute-start.2 = (f32[4,512]{1,0:T(4,128)S(1)}, f32[4,512]{1,0:T(4,128)S(1)}, u32[]{:S(2)}, u32[]{:S(2)}) collective-permute-start(f32[4,512]{1,0:T(4,128)S(1)} %reshape.77), channel_id=1, source_target_pairs={{0,1},{1,0},{2,3},{3,2},{4,5},{5,4},{6,7},{7,6},{8,9},{9,8},{10,11... | collective-permute-start | bytes 24584 | tf_op jit(solution)/shard_map/ppermute | solution.py:490
  40.6 1.6 %collective-permute-done.2 = f32[4,512]{1,0:T(4,128)S(1)} collective-permute-done((f32[4,512]{1,0:T(4,128)S(1)}, f32[4,512]{1,0:T(4,128)S(1)}, u32[]{:S(2)}, u32[]{:S(2)}) %collective-permute-start.2) | collective-permute-done | bytes 8224 | tf_op jit(solution)/shard_map/ppermute | solution.py:490
  42.2 2.7 %collective-permute-start.3 = (f32[8,512]{1,0:T(8,128)S(1)}, f32[8,512]{1,0:T(8,128)S(1)}, u32[]{:S(2)}, u32[]{:S(2)}) collective-permute-start(f32[8,512]{1,0:T(8,128)S(1)} %pad_maximum_fusion.2), channel_id=1, source_target_pairs={{0,2},{1,3},{2,0},{3,1},{4,6},{5,7},{6,4},{7,5},{8,10},{9,11},{10,... | collective-permute-start | bytes 49160 | tf_op jit(solution)/shard_map/ppermute | solution.py:490
  44.9 4.7 %all-to-all-done.1 = bf16[8,16,4096]{2,1,0:T(8,128)(2,1)S(1)} async-done(((bf16[8,16,4096]{2,1,0:T(8,128)(2,1)}), bf16[8,16,4096]{2,1,0:T(8,128)(2,1)S(1)}, u32[]{:S(2)}, u32[]{:S(2)}) %all-to-all-start.1) | async-done | bytes 1048608 | tf_op jit(solution)/shard_map/all_to_all | solution.py:445
  49.7 1.8 %yz_planes.1 = bf16[1024,128]{1,0:T(8,128)(2,1)} custom-call(bf16[128,4096]{1,0:T(8,128)(2,1)S(1)} %bitcast.22, bf16[256,256]{1,0:T(8,128)(2,1)S(1)} %copy-done.4), custom_call_target="tpu_custom_call" | custom-call | flops 1024 | bytes 1024 | tf_op jit(solution)/shard_map/yz_planes/pallas_call | solution.py:502
  51.5 6.6 %all-to-all-start.2 = ((bf16[16,64,128]{2,1,0:T(8,128)(2,1)}), bf16[16,64,128]{2,1,0:T(8,128)(2,1)S(1)}, u32[]{:S(2)}, u32[]{:S(2)}) async-start(bf16[16,64,128]{2,1,0:T(8,128)(2,1)} %bitcast.11), calls=%async_computation.2 | async-start | bytes 524288 | tf_op jit(solution)/shard_map/all_to_all | solution.py:517
  58.1 0.1 collective-permute-start.4
  58.2 0.1 fusion.1
  58.3 4.3 %collective-permute-done.4 = f32[16,512]{1,0:T(8,128)S(1)} collective-permute-done((f32[16,512]{1,0:T(8,128)S(1)}, f32[16,512]{1,0:T(8,128)S(1)}, u32[]{:S(2)}, u32[]{:S(2)}) %collective-permute-start.4) | collective-permute-done | bytes 32800 | tf_op jit(solution)/shard_map/ppermute | solution.py:490
  62.6 0.7 %select_reduce_fusion = f32[8,512]{1,0:T(8,128)} fusion(f32[32,512]{1,0:T(8,128)S(1)} %pad_maximum_fusion, pred[8,32]{1,0:T(8,128)(4,1)S(1)} %fusion.1), kind=kLoop, calls=%fused_computation | loop fusion | flops 258048 | bytes 82176 | tf_op jit(solution)/shard_map/reduce_sum | solution.py:497
  63.4 4.6 %all-to-all-done.2.rows_ref = bf16[16,64,128]{2,1,0:T(8,128)(2,1)S(1)} async-done(((bf16[16,64,128]{2,1,0:T(8,128)(2,1)}), bf16[16,64,128]{2,1,0:T(8,128)(2,1)S(1)}, u32[]{:S(2)}, u32[]{:S(2)}) %all-to-all-start.2) | async-done | bytes 262176 | tf_op jit(solution)/shard_map/all_to_all | solution.py:517
  68.0 1.0 %copy-done.1 = bf16[4,256,256]{2,1,0:T(8,128)(2,1)S(1)} copy-done((bf16[4,256,256]{2,1,0:T(8,128)(2,1)S(1)}, bf16[4,256,256]{2,1,0:T(8,128)(2,1)}, u32[]{:S(2)}) %copy-start.1) | copy-done | bytes 524312
  69.1 1.6 %x_rows.1 = f32[4,4,64,128]{3,2,1,0:T(8,128)} custom-call(bf16[16,64,128]{2,1,0:T(8,128)(2,1)S(1)} %all-to-all-done.2.rows_ref, bf16[4,256,256]{2,1,0:T(8,128)(2,1)S(1)} %copy-done.1), custom_call_target="tpu_custom_call" | custom-call | tf_op jit(solution)/shard_map/x_rows/pallas_call | solution.py:518
  (21 shorter events, 0.1 us)
Async XLA Ops:
  2.7 25.1 %all-to-all-start = ((bf16[8,16,4096]{2,1,0:T(8,128)(2,1)}), bf16[8,16,4096]{2,1,0:T(8,128)(2,1)S(1)}, u32[]{:S(2)}, u32[]{:S(2)}) async-start(bf16[8,16,4096]{2,1,0:T(8,128)(2,1)} %tile.9), calls=%async_computation | async-start | bytes 2097152 | tf_op jit(solution)/shard_map/all_to_all | solution.py:418
  15.9 4.2 %collective-permute-start = (bf16[128,4096]{1,0:T(8,128)(2,1)}, bf16[128,4096]{1,0:T(8,128)(2,1)S(1)}, u32[]{:S(2)}, u32[]{:S(2)}) collective-permute-start(bf16[128,4096]{1,0:T(8,128)(2,1)} %get-tuple-element.14), channel_id=1, source_target_pairs={{0,8},{8,0},{16,24},{24,16},{32,40},{40,32},{48,56},{56,48},{64,72... | collective-permute-start | bytes 3145736 | tf_op jit(solution)/shard_map/ppermute | solution.py:417
  16.0 4.1 %copy-start = (bf16[128,4096]{1,0:T(8,128)(2,1)S(1)}, bf16[128,4096]{1,0:T(8,128)(2,1)}, u32[]{:S(2)}) copy-start(bf16[128,4096]{1,0:T(8,128)(2,1)} %get-tuple-element.13.own_ref) | copy-start | bytes 3145732
  20.0 11.5 %copy-start.8 = (s32[8,1]{0,1:T(1,128)S(1)}, s32[8,1]{0,1:T(1,128)}, u32[]{:S(2)}) copy-start(s32[8,1]{0,1:T(1,128)} %param.16) | copy-start | bytes 100
  20.0 11.7 %copy-start.2 = (bf16[256,256]{1,0:T(8,128)(2,1)S(1)}, bf16[256,256]{1,0:T(8,128)(2,1)}, u32[]{:S(2)}) copy-start(bf16[256,256]{1,0:T(8,128)(2,1)} %constant.24.clone.table_ref) | copy-start | bytes 393220
  20.1 11.7 %copy-start.3 = (bf16[512,128]{1,0:T(8,128)(2,1)S(1)}, bf16[512,128]{1,0:T(8,128)(2,1)}, u32[]{:S(2)}) copy-start(bf16[512,128]{1,0:T(8,128)(2,1)} %constant.28.clone.wz_ref) | copy-start | bytes 393220
  20.1 11.7 %copy-start.6 = (bf16[16,40]{1,0:T(8,128)(2,1)S(1)}, bf16[16,40]{1,0:T(8,128)(2,1)}, u32[]{:S(2)}) copy-start(bf16[16,40]{1,0:T(8,128)(2,1)} %constant.27.clone.ex_ref) | copy-start | bytes 3844
  20.1 11.7 %copy-start.7 = (s32[4]{0:T(128)S(1)}, s32[4]{0:T(128)}, u32[]{:S(2)}) copy-start(s32[4]{0:T(128)} %get-tuple-element.11.slot_rot_ref) | copy-start | bytes 52
  27.8 3.9 %collective-permute-start.1 = (bf16[128,4096]{1,0:T(8,128)(2,1)S(1)}, bf16[128,4096]{1,0:T(8,128)(2,1)S(1)}, u32[]{:S(2)}, u32[]{:S(2)}) collective-permute-start(bf16[128,4096]{1,0:T(8,128)(2,1)S(1)} %bitcast.23), channel_id=1, source_target_pairs={{0,8},{8,0},{16,24},{24,16},{32,40},{40,32},{48,56},{56,48},{64,72... | collective-permute-start | bytes 3145736 | tf_op jit(solution)/shard_map/ppermute | solution.py:446
  27.8 21.8 %copy-start.4 = (bf16[256,256]{1,0:T(8,128)(2,1)S(1)}, bf16[256,256]{1,0:T(8,128)(2,1)}, u32[]{:S(2)}) copy-start(bf16[256,256]{1,0:T(8,128)(2,1)} %constant.29.clone.table_hbm) | copy-start | bytes 393220
  27.8 21.8 %all-to-all-start.1 = ((bf16[8,16,4096]{2,1,0:T(8,128)(2,1)}), bf16[8,16,4096]{2,1,0:T(8,128)(2,1)S(1)}, u32[]{:S(2)}, u32[]{:S(2)}) async-start(bf16[8,16,4096]{2,1,0:T(8,128)(2,1)} %bitcast.9), calls=%async_computation.1 | async-start | bytes 2097152 | tf_op jit(solution)/shard_map/all_to_all | solution.py:445
  31.8 0.9 %copy-start.5 = (f32[2,96,128]{2,1,0:T(8,128)S(1)}, f32[2,96,128]{2,1,0:T(8,128)}, u32[]{:S(2)}) copy-start(f32[2,96,128]{2,1,0:T(8,128)} %constant.26.clone.x_ref) | copy-start | bytes 294916
  36.1 6.1 %collective-permute-start.2 = (f32[4,512]{1,0:T(4,128)S(1)}, f32[4,512]{1,0:T(4,128)S(1)}, u32[]{:S(2)}, u32[]{:S(2)}) collective-permute-start(f32[4,512]{1,0:T(4,128)S(1)} %reshape.77), channel_id=1, source_target_pairs={{0,1},{1,0},{2,3},{3,2},{4,5},{5,4},{6,7},{7,6},{8,9},{9,8},{10,11... | collective-permute-start | bytes 24584 | tf_op jit(solution)/shard_map/ppermute | solution.py:490
  42.2 15.9 %collective-permute-start.3 = (f32[8,512]{1,0:T(8,128)S(1)}, f32[8,512]{1,0:T(8,128)S(1)}, u32[]{:S(2)}, u32[]{:S(2)}) collective-permute-start(f32[8,512]{1,0:T(8,128)S(1)} %pad_maximum_fusion.2), channel_id=1, source_target_pairs={{0,2},{1,3},{2,0},{3,1},{4,6},{5,7},{6,4},{7,5},{8,10},{9,11},{10,... | collective-permute-start | bytes 49160 | tf_op jit(solution)/shard_map/ppermute | solution.py:490
  51.5 16.5 %all-to-all-start.2 = ((bf16[16,64,128]{2,1,0:T(8,128)(2,1)}), bf16[16,64,128]{2,1,0:T(8,128)(2,1)S(1)}, u32[]{:S(2)}, u32[]{:S(2)}) async-start(bf16[16,64,128]{2,1,0:T(8,128)(2,1)} %bitcast.11), calls=%async_computation.2 | async-start | bytes 524288 | tf_op jit(solution)/shard_map/all_to_all | solution.py:517
  58.1 4.5 %collective-permute-start.4 = (f32[16,512]{1,0:T(8,128)S(1)}, f32[16,512]{1,0:T(8,128)S(1)}, u32[]{:S(2)}, u32[]{:S(2)}) collective-permute-start(f32[16,512]{1,0:T(8,128)S(1)} %pad_maximum_fusion.1), channel_id=1, source_target_pairs={{0,4},{1,5},{2,6},{3,7},{4,0},{5,1},{6,2},{7,3},{8,12},{9,13},{10,... | collective-permute-start | bytes 98312 | tf_op jit(solution)/shard_map/ppermute | solution.py:490
  68.0 1.0 %copy-start.1 = (bf16[4,256,256]{2,1,0:T(8,128)(2,1)S(1)}, bf16[4,256,256]{2,1,0:T(8,128)(2,1)}, u32[]{:S(2)}) copy-start(bf16[4,256,256]{2,1,0:T(8,128)(2,1)} %constant.30.clone.table_hbm) | copy-start | bytes 1572868

commit v2 on v1

--- a/solution.py
+++ b/solution.py
@@ -69,15 +69,14 @@
 
 def x_rows_table():
     c, s = grid_cos_sin(np.arange(BOX), np.arange(BOX))
-    full = []
-    for table in (c, s):
-        spread = np.einsum(
-            "rq,kdx->rkdqx", np.eye(ROT_CLS), table.reshape(BOX, DOM, BOX // DOM)
-        ).reshape(ROT_CLS * BOX, ROT_CLS * BOX)
-        high = spread.astype(np.float32).astype(BF)
-        low = (spread.astype(np.float32) - high.astype(np.float32)).astype(BF)
-        full += [high, low]
-    return np.stack(full)
+    return np.stack(
+        [
+            np.einsum(
+                "rq,kdx->rkdqx", np.eye(ROT_CLS), table.reshape(BOX, DOM, BOX // DOM)
+            ).reshape(ROT_CLS * BOX, ROT_CLS * BOX)
+            for table in (c, s)
+        ]
+    )
 
 
 def z_stage(src, table, start, count):
@@ -93,6 +92,22 @@
 PLANES = BOX // DOM
 PER_CHIP = ROT_CLS * PLANES
 SEND = CHIPS * PER_CHIP
+
+
+def fan_kernel(refs_ref, out_hbm, wide_s, block_s, sems):
+    for rot in range(ROT_CLS):
+        wide_s[rot * PLANES : (rot + 1) * PLANES] = refs_ref[rot].astype(F32)
+    block_s[...] = wide_s[...].astype(BF)
+    copies = [
+        pltpu.make_async_copy(
+            block_s, out_hbm.at[chip * PER_CHIP : (chip + 1) * PER_CHIP], sems.at[chip]
+        )
+        for chip in range(CHIPS)
+    ]
+    for copy in copies:
+        copy.start()
+    for copy in copies:
+        copy.wait()
 
 
 LANES = 1024
@@ -235,12 +250,12 @@
         for to in range(CAP):
             rows = slice(to * 2 * KXP, (to + 1) * 2 * KXP)
             wanted = ref_rot == slot_rot_ref[to]
-            pick_s[0, rows] = jnp.where(wanted, x_ref[core], 0.0).astype(BF)
-            pick_s[1, rows] = jnp.where(wanted, x_ref[1 - core], 0.0).astype(BF)
+            pick_s[rows, :SEND] = jnp.where(wanted, x_ref[core], 0.0).astype(BF)
+            pick_s[rows, SEND:] = jnp.where(wanted, x_ref[1 - core], 0.0).astype(BF)
         for start in range(0, BOX * BOX, 512):
             lanes = slice(start, start + 512)
-            part = jnp.dot(pick_s[0], own_ref[:, lanes], preferred_element_type=F32)
-            part = part + jnp.dot(pick_s[1], other_ref[:, lanes], preferred_element_type=F32)
+            planes = jnp.concatenate([own_ref[:, lanes], other_ref[:, lanes]], axis=0)
+            part = jnp.dot(pick_s[...], planes, preferred_element_type=F32)
             x_s[:, :, lanes] = part.astype(BF).reshape(CAP, 2 * KXP, 512)
 
     @pl.when(slot < count_ref[0])
@@ -312,14 +327,11 @@
         out_ref[...] = jnp.zeros_like(out_ref)
 
 
-def yz_kernel(parts_ref, table_hbm, out_ref, z_s, g_s, table_ref, sem):
-    copy = pltpu.make_async_copy(table_hbm, table_ref, sem)
-    copy.start()
+def yz_kernel(parts_ref, table_ref, out_ref, z_s, g_s):
     total = parts_ref[0:PER_CHIP].astype(F32)
     for chip in range(1, CHIPS):
         total = total + parts_ref[chip * PER_CHIP : (chip + 1) * PER_CHIP].astype(F32)
     total = total.astype(BF)
-    copy.wait()
     z_ref, y_ref = table_ref[: 2 * BOX], table_ref[2 * BOX :, :BOX]
     stacked = jnp.concatenate([total[:, 128 * j : 128 * (j + 1)] for j in range(PAIRS)], axis=0)
     z_part = jnp.dot(stacked, z_ref, preferred_element_type=F32)
@@ -339,18 +351,13 @@
     out_ref[...] = g_s[...].astype(BF)
 
 
-def x_rows_kernel(rows_ref, table_hbm, out_ref, table_ref, sem):
-    copy = pltpu.make_async_copy(table_hbm, table_ref, sem)
-    copy.start()
-    copy.wait()
+def x_rows_kernel(rows_ref, table_ref, out_ref):
     rows = ROT_CLS * (BOX // DOM)
     first = lax.broadcasted_iota(jnp.int32, (ROT_CLS * BOX, 128), 1) < BOX
     for ky in range(BOX // DOM):
         grid = rows_ref[:, ky * rows : (ky + 1) * rows, :].reshape(ROT_CLS * BOX, 128)
         cos_part = jnp.dot(table_ref[0], grid, preferred_element_type=F32)
-        cos_part = cos_part + jnp.dot(table_ref[1], grid, preferred_element_type=F32)
-        sin_part = jnp.dot(table_ref[2], grid, preferred_element_type=F32)
-        sin_part = sin_part + jnp.dot(table_ref[3], grid, preferred_element_type=F32)
+        sin_part = jnp.dot(table_ref[1], grid, preferred_element_type=F32)
         turned = pltpu.roll(sin_part, BOX, 1)
         total = (cos_part + jnp.where(first, turned, -turned)) * (float(BOX) ** -1.5)
         out_ref[ky] = total.reshape(ROT_CLS, BOX, 128)
@@ -375,7 +382,20 @@
     columns = block_size * BOX
     to_other = [(i, i ^ 1) for i in range(DOM)]
 
-    mine_refs = jnp.tile(references.reshape(PER_CHIP, voxels), (CHIPS, 1))
+    mine_refs = pl.pallas_call(
+        fan_kernel,
+        out_shape=jax.ShapeDtypeStruct((SEND, voxels), BF),
+        in_specs=[VMEM],
+        out_specs=HBM,
+        scratch_shapes=[
+            pltpu.VMEM((PER_CHIP, voxels), F32),
+            pltpu.VMEM((PER_CHIP, voxels), BF),
+            pltpu.SemaphoreType.DMA((CHIPS,)),
+        ],
+        compiler_params=params(54),
+        cost_estimate=cost(1024, 1024),
+        name="fan",
+    )(references)
 
     flat = particles.reshape(columns, voxels)
     classes = part_class.reshape(block_size)
@@ -463,13 +483,13 @@
         ],
         out_specs=pl.BlockSpec((None, SHIFTS * SHIFTS, 128), lambda s: (s, 0, 0)),
         scratch_shapes=[
-            pltpu.VMEM((2, CAP * 2 * KXP, SEND), BF),
+            pltpu.VMEM((CAP * 2 * KXP, 2 * SEND), BF),
             pltpu.VMEM((CAP, 2 * KXP, voxels), BF),
             pltpu.VMEM((PAIRS, KXV, 4 * BOX), F32),
             pltpu.VMEM((PAIRS, KXV, 4 * BOX), F32),
             pltpu.VMEM((SHIFTS, KXV, 4 * BOX), F32),
         ],
-        compiler_params=params(50),
+        compiler_params=params(52),
         cost_estimate=cost(1024, 1024),
         name="slot_scores",
     )(
@@ -502,14 +522,9 @@
     grids = pl.pallas_call(
         yz_kernel,
         out_shape=jax.ShapeDtypeStruct((BOX * PER_CHIP, 2 * BOX), BF),
-        in_specs=[VMEM, HBM],
+        in_specs=[VMEM, VMEM],
         out_specs=VMEM,
-        scratch_shapes=[
-            pltpu.VMEM((BOX * PER_CHIP, 128), F32),
-            pltpu.VMEM((BOX * PER_CHIP, 128), F32),
-            pltpu.VMEM((4 * BOX, 4 * BOX), BF),
-            pltpu.SemaphoreType.DMA,
-        ],
+        scratch_shapes=[pltpu.VMEM((BOX * PER_CHIP, 128), F32)] * 2,
         compiler_params=params(50),
         cost_estimate=cost(1024, 1024),
         name="yz_planes",
@@ -518,15 +533,11 @@
     sums = pl.pallas_call(
         x_rows_kernel,
         out_shape=jax.ShapeDtypeStruct((BOX // DOM, ROT_CLS, BOX, 2 * BOX), F32),
-        in_specs=[VMEM, HBM],
+        in_specs=[VMEM, VMEM],
         out_specs=VMEM,
-        scratch_shapes=[
-            pltpu.VMEM((4, ROT_CLS * BOX, ROT_CLS * BOX), BF),
-            pltpu.SemaphoreType.DMA,
-        ],
         compiler_params=params(50),
         name="x_rows",
-    )(by_rows.reshape(DOM, PLANES * PER_CHIP, 2 * BOX), jnp.asarray(x_rows_table()))
+    )(by_rows.reshape(DOM, PLANES * PER_CHIP, 2 * BOX), jnp.asarray(x_rows_table().astype(BF)))
     return (scores, sums)
 
 

time: 70.8 us -> 66.5 us (0.939)
  the two profiles are of different devices: /device:TPU:6 before, /device:TPU:1 now
where the time goes in v2:
time: 66.5 us; the launch traced here: 66 us
  starting transfers between devices  25.5 us (38%)
  Pallas kernels  22.5 us (34%)
  waiting for transfers between devices  15.2 us (23%)
  between operations  1.49 us (2%)
  other arithmetic  1.04 us (2%)
    all_to_all x1, starting transfers between devices, shards(): lax.all_to_all(mine_refs, 'dom', 0, 0, tiled=True, axis_index_groups=SAME...  8.51 us
    pallas_call x1, Pallas kernels, shards(): pl.pallas_call(score_kernel, out_shape=jax.ShapeDtypeStruct((CAP, SHIFTS...  6.44 us
    ppermute x3, waiting for transfers between devices, shards(): lax.ppermute(everywhere, 'rot', [(i, i ^ bit) for i in range(8)])  6.14 us
    ppermute x3, starting transfers between devices, shards(): lax.ppermute(everywhere, 'rot', [(i, i ^ bit) for i in range(8)])  5.8 us
    pallas_call x1, Pallas kernels, shards(): pl.pallas_call(spectra_kernel, out_shape=jax.ShapeDtypeStruct((CAP, PAIRS...  5.58 us
    all_to_all x1, waiting for transfers between devices, shards(): lax.all_to_all(pair_sum, 'dom', 0, 0, tiled=True, axis_index_groups=SAME_...  4.71 us
    pallas_call x1, Pallas kernels, shards(): pl.pallas_call(send_kernel, out_shape=(jax.ShapeDtypeStruct((SEND, voxels...  4.5 us
    all_to_all x1, starting transfers between devices, shards(): by_rows = lax.all_to_all(grids, 'dom', 0, 0, tiled=True)  4.15 us
  transfers between devices with their start and end apart: 8, of which 5 were waited for; matrix products, arithmetic and copies ran while one was open for 2% of the time, Pallas kernels for 22%

profile of v2, /device:TPU:1, one launch (start us, length us, event | category | flops | bytes accessed | tf_op | source)
XLA Modules:
  0.0 66.0 jit_solution(11192729801045006532)
XLA Ops:
  0.6 2.0 %fan.1 = bf16[128,4096]{1,0:T(8,128)(2,1)} custom-call(bf16[4,4,4096]{2,1,0:T(4,128)(2,1)} %refs_ref.1), custom_call_target="tpu_custom_call" | custom-call | flops 1024 | bytes 1024 | tf_op jit(solution)/shard_map/fan/pallas_call | solution.py:385
  2.7 8.5 %all-to-all-start = ((bf16[8,16,4096]{2,1,0:T(8,128)(2,1)}), bf16[8,16,4096]{2,1,0:T(8,128)(2,1)S(1)}, u32[]{:S(2)}, u32[]{:S(2)}) async-start(bf16[8,16,4096]{2,1,0:T(8,128)(2,1)} %bitcast.28), calls=%async_computation | async-start | bytes 2097152 | tf_op jit(solution)/shard_map/all_to_all | solution.py:438
  11.8 4.5 %send.1 = (bf16[128,4096]{1,0:T(8,128)(2,1)}, bf16[128,4096]{1,0:T(8,128)(2,1)}, s32[1]{0:T(128)}, s32[4]{0:T(128)}, s32[4]{0:T(128)}) custom-call(s32[8]{0:T(128)} %bitcast.30, s32[8]{0:T(128)} %rot_ref.1, s32[8]{0:T(128)} %bucket_ref.1, s32[1]{0:T(128)} %copy.20.live_ref, bf16[1,8]{1,0:T(2,128)(2,1)} %bitcast.32, bf16[512,4096]{1,0:T(8,128)(2,1)} %bitcast.26), custom_call_target="tpu_custom_call" | custom-call | flops 1024 | bytes 1024 | tf_op jit(solution)/shard_map/send/pallas_call | solution.py:414
  16.3 1.2 %collective-permute-start = (bf16[128,4096]{1,0:T(8,128)(2,1)}, bf16[128,4096]{1,0:T(8,128)(2,1)S(1)}, u32[]{:S(2)}, u32[]{:S(2)}) collective-permute-start(bf16[128,4096]{1,0:T(8,128)(2,1)} %get-tuple-element.14), channel_id=1, source_target_pairs={{0,8},{8,0},{16,24},{24,16},{32,40},{40,32},{48,56},{56,48},{64,72... | collective-permute-start | bytes 3145736 | tf_op jit(solution)/shard_map/ppermute | solution.py:437
  17.5 5.6 %spectra.1.zp_ref = bf16[4,1536,256]{2,1,0:T(8,128)(2,1)} custom-call(s32[4]{0:T(128)} %get-tuple-element.12.slot_row_ref, s32[1]{0:T(128)} %get-tuple-element.10.count_ref, bf16[96,64]{1,0:T(8,128)(2,1)} %constant.25.clone.x_ref, bf16[512,4096]{1,0:T(8,128)(2,1)} %bitcast.27, bf16[256,256]{1,0:T(8,128)(2,1)} %constant.24.clone.table_ref), custom_call_target="tpu_custom_call" | custom-call | flops 20000000000 | bytes 1024 | tf_op jit(solution)/shard_map/spectra/pallas_call | solution.py:452
  23.1 0.0 copy-start.8
  23.1 0.0 copy-start.2
  23.1 0.0 copy-start.3
  23.2 0.0 copy-start.5
  23.2 0.0 copy-start.6
  23.2 0.0 collective-permute-done.other_ref
  23.2 1.2 %pair.1 = bf16[128,4096]{1,0:T(8,128)(2,1)} custom-call(bf16[128,4096]{1,0:T(8,128)(2,1)S(1)} %copy-done, bf16[128,4096]{1,0:T(8,128)(2,1)S(1)} %collective-permute-done.other_ref), custom_call_target="tpu_custom_call" | custom-call | flops 1024 | bytes 1024 | tf_op jit(solution)/shard_map/pair/pallas_call | solution.py:441
  24.4 2.7 %all-to-all-done = bf16[8,16,4096]{2,1,0:T(8,128)(2,1)S(1)} async-done(((bf16[8,16,4096]{2,1,0:T(8,128)(2,1)}), bf16[8,16,4096]{2,1,0:T(8,128)(2,1)S(1)}, u32[]{:S(2)}, u32[]{:S(2)}) %all-to-all-start) | async-done | bytes 1048608 | tf_op jit(solution)/shard_map/all_to_all | solution.py:438
  27.2 2.2 %collective-permute-start.1 = (bf16[128,4096]{1,0:T(8,128)(2,1)S(1)}, bf16[128,4096]{1,0:T(8,128)(2,1)}, u32[]{:S(2)}, u32[]{:S(2)}) collective-permute-start(bf16[128,4096]{1,0:T(8,128)(2,1)S(1)} %bitcast.24), channel_id=1, source_target_pairs={{0,8},{8,0},{16,24},{24,16},{32,40},{40,32},{48,56},{56,48},{64,72... | collective-permute-start | bytes 3145736 | tf_op jit(solution)/shard_map/ppermute | solution.py:466
  29.3 3.7 %all-to-all-start.1 = ((bf16[8,16,4096]{2,1,0:T(8,128)(2,1)}), bf16[8,16,4096]{2,1,0:T(8,128)(2,1)S(1)}, u32[]{:S(2)}, u32[]{:S(2)}) async-start(bf16[8,16,4096]{2,1,0:T(8,128)(2,1)} %bitcast.10), calls=%async_computation.1 | async-start | bytes 2097152 | tf_op jit(solution)/shard_map/all_to_all | solution.py:465
  33.0 0.2 convert_reduce_fusion
  33.3 0.0 copy-start.1
  33.3 6.4 %slot_scores.1 = f32[4,64,128]{2,1,0:T(8,128)S(1)} custom-call(s32[1]{0:T(128)} %get-tuple-element.10.count_ref, s32[4]{0:T(128)S(1)} %copy-done.7, bf16[4,1536,256]{2,1,0:T(8,128)(2,1)} %spectra.1.zp_ref, f32[2,96,128]{2,1,0:T(8,128)S(1)} %copy-done.5, bf16[128,4096]{1,0:T(8,128)(2,1)S(1)} %bitcast.25, bf16[128,4096]{1,0:T(8,128)(2,1)} %collective-permute-done.1.other_ref, ...), custom_call_target="tpu_custom_call" | custom-call | flops 1024 | bytes 1024 | tf_op jit(solution)/shard_map/slot_scores/pallas_call | solution.py:469
  39.8 0.1 reshape.72
  39.9 1.3 %collective-permute-start.2 = (f32[4,512]{1,0:T(4,128)S(1)}, f32[4,512]{1,0:T(4,128)S(1)}, u32[]{:S(2)}, u32[]{:S(2)}) collective-permute-start(f32[4,512]{1,0:T(4,128)S(1)} %reshape.72), channel_id=1, source_target_pairs={{0,1},{1,0},{2,3},{3,2},{4,5},{5,4},{6,7},{7,6},{8,9},{9,8},{10,11... | collective-permute-start | bytes 24584 | tf_op jit(solution)/shard_map/ppermute | solution.py:510
  41.2 1.6 %collective-permute-done.2 = f32[4,512]{1,0:T(4,128)S(1)} collective-permute-done((f32[4,512]{1,0:T(4,128)S(1)}, f32[4,512]{1,0:T(4,128)S(1)}, u32[]{:S(2)}, u32[]{:S(2)}) %collective-permute-start.2) | collective-permute-done | bytes 8224 | tf_op jit(solution)/shard_map/ppermute | solution.py:510
  42.8 2.8 %collective-permute-start.3 = (f32[8,512]{1,0:T(8,128)S(1)}, f32[8,512]{1,0:T(8,128)S(1)}, u32[]{:S(2)}, u32[]{:S(2)}) collective-permute-start(f32[8,512]{1,0:T(8,128)S(1)} %pad_maximum_fusion.2), channel_id=1, source_target_pairs={{0,2},{1,3},{2,0},{3,1},{4,6},{5,7},{6,4},{7,5},{8,10},{9,11},{10,... | collective-permute-start | bytes 49160 | tf_op jit(solution)/shard_map/ppermute | solution.py:510
  45.6 4.7 %all-to-all-done.1 = bf16[8,16,4096]{2,1,0:T(8,128)(2,1)S(1)} async-done(((bf16[8,16,4096]{2,1,0:T(8,128)(2,1)}), bf16[8,16,4096]{2,1,0:T(8,128)(2,1)S(1)}, u32[]{:S(2)}, u32[]{:S(2)}) %all-to-all-start.1) | async-done | bytes 1048608 | tf_op jit(solution)/shard_map/all_to_all | solution.py:465
  50.3 1.5 %yz_planes.1 = bf16[1024,128]{1,0:T(8,128)(2,1)} custom-call(bf16[128,4096]{1,0:T(8,128)(2,1)S(1)} %bitcast.23, bf16[256,256]{1,0:T(8,128)(2,1)S(1)} %copy-done.4), custom_call_target="tpu_custom_call" | custom-call | flops 1024 | bytes 1024 | tf_op jit(solution)/shard_map/yz_planes/pallas_call | solution.py:522
  51.8 4.2 %all-to-all-start.2 = ((bf16[16,64,128]{2,1,0:T(8,128)(2,1)}), bf16[16,64,128]{2,1,0:T(8,128)(2,1)S(1)}, u32[]{:S(2)}, u32[]{:S(2)}) async-start(bf16[16,64,128]{2,1,0:T(8,128)(2,1)} %bitcast.12), calls=%async_computation.2 | async-start | bytes 524288 | tf_op jit(solution)/shard_map/all_to_all | solution.py:532
  56.0 0.0 collective-permute-done.3
  56.0 1.7 %collective-permute-start.4 = (f32[16,512]{1,0:T(8,128)S(1)}, f32[16,512]{1,0:T(8,128)S(1)}, u32[]{:S(2)}, u32[]{:S(2)}) collective-permute-start(f32[16,512]{1,0:T(8,128)S(1)} %pad_maximum_fusion.1), channel_id=1, source_target_pairs={{0,4},{1,5},{2,6},{3,7},{4,0},{5,1},{6,2},{7,3},{8,12},{9,13},{10,... | collective-permute-start | bytes 98312 | tf_op jit(solution)/shard_map/ppermute | solution.py:510
  57.7 0.1 fusion.1
  57.8 4.6 %collective-permute-done.4 = f32[16,512]{1,0:T(8,128)S(1)} collective-permute-done((f32[16,512]{1,0:T(8,128)S(1)}, f32[16,512]{1,0:T(8,128)S(1)}, u32[]{:S(2)}, u32[]{:S(2)}) %collective-permute-start.4) | collective-permute-done | bytes 32800 | tf_op jit(solution)/shard_map/ppermute | solution.py:510
  62.3 0.7 %select_reduce_fusion = f32[8,512]{1,0:T(8,128)} fusion(f32[32,512]{1,0:T(8,128)S(1)} %pad_maximum_fusion, pred[8,32]{1,0:T(8,128)(4,1)S(1)} %fusion.1), kind=kLoop, calls=%fused_computation | loop fusion | flops 258048 | bytes 82176 | tf_op jit(solution)/shard_map/reduce_sum | solution.py:517
  63.1 1.6 %all-to-all-done.2.rows_ref = bf16[16,64,128]{2,1,0:T(8,128)(2,1)S(1)} async-done(((bf16[16,64,128]{2,1,0:T(8,128)(2,1)}), bf16[16,64,128]{2,1,0:T(8,128)(2,1)S(1)}, u32[]{:S(2)}, u32[]{:S(2)}) %all-to-all-start.2) | async-done | bytes 262176 | tf_op jit(solution)/shard_map/all_to_all | solution.py:532
  64.7 1.3 %x_rows.1 = f32[4,4,64,128]{3,2,1,0:T(8,128)} custom-call(bf16[16,64,128]{2,1,0:T(8,128)(2,1)S(1)} %all-to-all-done.2.rows_ref, bf16[2,256,256]{2,1,0:T(8,128)(2,1)S(1)} %copy-done.1), custom_call_target="tpu_custom_call" | custom-call | tf_op jit(solution)/shard_map/x_rows/pallas_call | solution.py:533
  (20 shorter events, 0.1 us)
Async XLA Ops:
  2.7 24.5 %all-to-all-start = ((bf16[8,16,4096]{2,1,0:T(8,128)(2,1)}), bf16[8,16,4096]{2,1,0:T(8,128)(2,1)S(1)}, u32[]{:S(2)}, u32[]{:S(2)}) async-start(bf16[8,16,4096]{2,1,0:T(8,128)(2,1)} %bitcast.28), calls=%async_computation | async-start | bytes 2097152 | tf_op jit(solution)/shard_map/all_to_all | solution.py:438
  16.3 6.9 %collective-permute-start = (bf16[128,4096]{1,0:T(8,128)(2,1)}, bf16[128,4096]{1,0:T(8,128)(2,1)S(1)}, u32[]{:S(2)}, u32[]{:S(2)}) collective-permute-start(bf16[128,4096]{1,0:T(8,128)(2,1)} %get-tuple-element.14), channel_id=1, source_target_pairs={{0,8},{8,0},{16,24},{24,16},{32,40},{40,32},{48,56},{56,48},{64,72... | collective-permute-start | bytes 3145736 | tf_op jit(solution)/shard_map/ppermute | solution.py:437
  17.5 5.7 %copy-start = (bf16[128,4096]{1,0:T(8,128)(2,1)S(1)}, bf16[128,4096]{1,0:T(8,128)(2,1)}, u32[]{:S(2)}) copy-start(bf16[128,4096]{1,0:T(8,128)(2,1)} %get-tuple-element.13.own_ref) | copy-start | bytes 3145732
  23.1 9.9 %copy-start.8 = (s32[8,1]{0,1:T(1,128)S(1)}, s32[8,1]{0,1:T(1,128)}, u32[]{:S(2)}) copy-start(s32[8,1]{0,1:T(1,128)} %param.16) | copy-start | bytes 100
  23.1 10.1 %copy-start.2 = (bf16[256,256]{1,0:T(8,128)(2,1)S(1)}, bf16[256,256]{1,0:T(8,128)(2,1)}, u32[]{:S(2)}) copy-start(bf16[256,256]{1,0:T(8,128)(2,1)} %constant.24.clone.table_ref) | copy-start | bytes 393220
  23.1 10.1 %copy-start.3 = (bf16[512,128]{1,0:T(8,128)(2,1)S(1)}, bf16[512,128]{1,0:T(8,128)(2,1)}, u32[]{:S(2)}) copy-start(bf16[512,128]{1,0:T(8,128)(2,1)} %constant.28.clone.wz_ref) | copy-start | bytes 393220
  23.2 10.1 %copy-start.5 = (f32[2,96,128]{2,1,0:T(8,128)S(1)}, f32[2,96,128]{2,1,0:T(8,128)}, u32[]{:S(2)}) copy-start(f32[2,96,128]{2,1,0:T(8,128)} %constant.26.clone.x_ref) | copy-start | bytes 294916
  23.2 10.1 %copy-start.6 = (bf16[16,40]{1,0:T(8,128)(2,1)S(1)}, bf16[16,40]{1,0:T(8,128)(2,1)}, u32[]{:S(2)}) copy-start(bf16[16,40]{1,0:T(8,128)(2,1)} %constant.27.clone.ex_ref) | copy-start | bytes 3844
  23.2 10.1 %copy-start.7 = (s32[4]{0:T(128)S(1)}, s32[4]{0:T(128)}, u32[]{:S(2)}) copy-start(s32[4]{0:T(128)} %get-tuple-element.11.slot_rot_ref) | copy-start | bytes 52
  27.2 6.1 %collective-permute-start.1 = (bf16[128,4096]{1,0:T(8,128)(2,1)S(1)}, bf16[128,4096]{1,0:T(8,128)(2,1)}, u32[]{:S(2)}, u32[]{:S(2)}) collective-permute-start(bf16[128,4096]{1,0:T(8,128)(2,1)S(1)} %bitcast.24), channel_id=1, source_target_pairs={{0,8},{8,0},{16,24},{24,16},{32,40},{40,32},{48,56},{56,48},{64,72... | collective-permute-start | bytes 3145736 | tf_op jit(solution)/shard_map/ppermute | solution.py:466
  29.3 21.0 %copy-start.4 = (bf16[256,256]{1,0:T(8,128)(2,1)S(1)}, bf16[256,256]{1,0:T(8,128)(2,1)}, u32[]{:S(2)}) copy-start(bf16[256,256]{1,0:T(8,128)(2,1)} %constant.29.clone.table_ref) | copy-start | bytes 393220
  29.3 21.0 %all-to-all-start.1 = ((bf16[8,16,4096]{2,1,0:T(8,128)(2,1)}), bf16[8,16,4096]{2,1,0:T(8,128)(2,1)S(1)}, u32[]{:S(2)}, u32[]{:S(2)}) async-start(bf16[8,16,4096]{2,1,0:T(8,128)(2,1)} %bitcast.10), calls=%async_computation.1 | async-start | bytes 2097152 | tf_op jit(solution)/shard_map/all_to_all | solution.py:465
  33.3 31.4 %copy-start.1 = (bf16[2,256,256]{2,1,0:T(8,128)(2,1)S(1)}, bf16[2,256,256]{2,1,0:T(8,128)(2,1)}, u32[]{:S(2)}) copy-start(bf16[2,256,256]{2,1,0:T(8,128)(2,1)} %constant.30.clone.table_ref) | copy-start | bytes 786436
  39.9 2.9 %collective-permute-start.2 = (f32[4,512]{1,0:T(4,128)S(1)}, f32[4,512]{1,0:T(4,128)S(1)}, u32[]{:S(2)}, u32[]{:S(2)}) collective-permute-start(f32[4,512]{1,0:T(4,128)S(1)} %reshape.72), channel_id=1, source_target_pairs={{0,1},{1,0},{2,3},{3,2},{4,5},{5,4},{6,7},{7,6},{8,9},{9,8},{10,11... | collective-permute-start | bytes 24584 | tf_op jit(solution)/shard_map/ppermute | solution.py:510
  42.8 13.2 %collective-permute-start.3 = (f32[8,512]{1,0:T(8,128)S(1)}, f32[8,512]{1,0:T(8,128)S(1)}, u32[]{:S(2)}, u32[]{:S(2)}) collective-permute-start(f32[8,512]{1,0:T(8,128)S(1)} %pad_maximum_fusion.2), channel_id=1, source_target_pairs={{0,2},{1,3},{2,0},{3,1},{4,6},{5,7},{6,4},{7,5},{8,10},{9,11},{10,... | collective-permute-start | bytes 49160 | tf_op jit(solution)/shard_map/ppermute | solution.py:510
  51.8 12.9 %all-to-all-start.2 = ((bf16[16,64,128]{2,1,0:T(8,128)(2,1)}), bf16[16,64,128]{2,1,0:T(8,128)(2,1)S(1)}, u32[]{:S(2)}, u32[]{:S(2)}) async-start(bf16[16,64,128]{2,1,0:T(8,128)(2,1)} %bitcast.12), calls=%async_computation.2 | async-start | bytes 524288 | tf_op jit(solution)/shard_map/all_to_all | solution.py:532
  56.0 6.3 %collective-permute-start.4 = (f32[16,512]{1,0:T(8,128)S(1)}, f32[16,512]{1,0:T(8,128)S(1)}, u32[]{:S(2)}, u32[]{:S(2)}) collective-permute-start(f32[16,512]{1,0:T(8,128)S(1)} %pad_maximum_fusion.1), channel_id=1, source_target_pairs={{0,4},{1,5},{2,6},{3,7},{4,0},{5,1},{6,2},{7,3},{8,12},{9,13},{10,... | collective-permute-start | bytes 98312 | tf_op jit(solution)/shard_map/ppermute | solution.py:510

commit v3 on v2

--- a/solution.py
+++ b/solution.py
@@ -226,7 +226,7 @@
 def score_kernel(
     count_ref,
     slot_rot_ref,
-    zp_ref,
+    zp_hbm,
     x_ref,
     own_ref,
     other_ref,
@@ -236,13 +236,21 @@
     out_ref,
     pick_s,
     x_s,
+    zp_s,
     p_s,
     r_s,
     a_s,
+    sems,
 ):
-    slot = pl.program_id(0)
-
-    @pl.when((slot == 0) & (count_ref[0] > 0))
+    for slot in range(CAP):
+
+        @pl.when(slot < count_ref[0])
+        def _():
+            pltpu.make_async_copy(zp_hbm.at[slot], zp_s.at[slot], sems.at[slot]).start()
+
+    out_ref[...] = jnp.zeros_like(out_ref)
+
+    @pl.when(count_ref[0] > 0)
     def _():
         core = lax.axis_index("dom") & 1
         ref_lane = lax.broadcasted_iota(jnp.int32, (1, SEND), 1)
@@ -258,15 +266,15 @@
             part = jnp.dot(pick_s[...], planes, preferred_element_type=F32)
             x_s[:, :, lanes] = part.astype(BF).reshape(CAP, 2 * KXP, 512)
 
-    @pl.when(slot < count_ref[0])
-    def _():
+    def one_slot(slot, carry):
+        pltpu.make_async_copy(zp_hbm.at[slot], zp_s.at[slot], sems.at[slot]).wait()
         table = table_ref[...]
         xr = x_s.at[slot]
         for start in range(0, PAIRS, STEP):
             part = z_stage(xr, table, start, STEP)
             part = part.astype(BF).astype(F32).reshape(STEP, KXP, 4 * BOX)
             r_s[start : start + STEP] = part[:, :KXV, :]
-            mine = zp_ref[start * KXP : (start + STEP) * KXP, :].astype(F32)
+            mine = zp_s[slot, start * KXP : (start + STEP) * KXP, :].astype(F32)
             p_s[start : start + STEP] = mine.reshape(STEP, KXP, 4 * BOX)[:, :KXV, :]
         first = lax.broadcasted_iota(jnp.int32, (8, 128), 1) < BOX
 
@@ -320,11 +328,10 @@
         sin_rows = jnp.concatenate([u[SHIFTS:] for u in along_x], axis=0).astype(BF)
         both_rows = jnp.concatenate([cos_rows, sin_rows], axis=1)
         final = jnp.dot(both_rows, wz_ref[...], preferred_element_type=F32)
-        out_ref[...] = final * (float(BOX) ** -3.5)
-
-    @pl.when(slot >= count_ref[0])
-    def _():
-        out_ref[...] = jnp.zeros_like(out_ref)
+        out_ref[slot] = final * (float(BOX) ** -3.5)
+        return carry
+
+    lax.fori_loop(0, count_ref[0], one_slot, 0)
 
 
 def yz_kernel(parts_ref, table_ref, out_ref, z_s, g_s):
@@ -469,25 +476,16 @@
     slots = pl.pallas_call(
         score_kernel,
         out_shape=jax.ShapeDtypeStruct((CAP, SHIFTS * SHIFTS, 128), F32),
-        grid=(CAP,),
-        in_specs=[
-            SMEM,
-            SMEM,
-            pl.BlockSpec((None, PAIRS * KXP, 4 * BOX), lambda s: (s, 0, 0)),
-            whole(2, 2 * KXP, SEND),
-            whole(SEND, voxels),
-            whole(SEND, voxels),
-            whole(4 * BOX, 4 * BOX),
-            whole(2 * SHIFTS, KXV),
-            whole(8 * BOX, 128),
-        ],
-        out_specs=pl.BlockSpec((None, SHIFTS * SHIFTS, 128), lambda s: (s, 0, 0)),
+        in_specs=[SMEM, SMEM, HBM] + [VMEM] * 6,
+        out_specs=VMEM,
         scratch_shapes=[
             pltpu.VMEM((CAP * 2 * KXP, 2 * SEND), BF),
             pltpu.VMEM((CAP, 2 * KXP, voxels), BF),
+            pltpu.VMEM((CAP, PAIRS * KXP, 4 * BOX), BF),
             pltpu.VMEM((PAIRS, KXV, 4 * BOX), F32),
             pltpu.VMEM((PAIRS, KXV, 4 * BOX), F32),
             pltpu.VMEM((SHIFTS, KXV, 4 * BOX), F32),
+            pltpu.SemaphoreType.DMA((CAP,)),
         ],
         compiler_params=params(52),
         cost_estimate=cost(1024, 1024),

time: 66.5 us -> 66.5 us (level)
  waiting for transfers between devices: 15.2 us -> 18.8 us
  starting transfers between devices: 25.5 us -> 23.5 us
  Pallas kernels: 22.5 us -> 21 us
    all_to_all x1, waiting for transfers between devices: 4.71 us -> 6.73 us  [shards(): lax.all_to_all(pair_sum, 'dom', 0, 0, tiled=True, axis_index_groups=SAME_...]
    ppermute x3, starting transfers between devices: 5.8 us -> 4.04 us  [shards(): lax.ppermute(everywhere, 'rot', [(i, i ^ bit) for i in range(8)])]
    pallas_call x1, Pallas kernels: 6.44 us -> 4.97 us  [shards(): pl.pallas_call(score_kernel, out_shape=jax.ShapeDtypeStruct((CAP, SHIFTS...]
    all_to_all x1, waiting for transfers between devices: 1.62 us -> 2.92 us  [shards(): by_rows = lax.all_to_all(grids, 'dom', 0, 0, tiled=True)]
  transfers between devices with their start and end apart: 8 -> 8, of which waited for: 5 -> 5; matrix products, arithmetic and copies ran while one was open for 2% -> 2% of each run, Pallas kernels for 22% -> 20%
where the time goes in v3:
time: 66.5 us; the launch traced here: 66 us
  starting transfers between devices  23.5 us (35%)
  Pallas kernels  21 us (32%)
  waiting for transfers between devices  18.8 us (28%)
  between operations  1.49 us (2%)
  other arithmetic  1.04 us (2%)
    all_to_all x1, starting transfers between devices, shards(): lax.all_to_all(mine_refs, 'dom', 0, 0, tiled=True, axis_index_groups=SAME...  8.51 us
    all_to_all x1, waiting for transfers between devices, shards(): lax.all_to_all(pair_sum, 'dom', 0, 0, tiled=True, axis_index_groups=SAME_...  6.73 us
    ppermute x3, waiting for transfers between devices, shards(): lax.ppermute(everywhere, 'rot', [(i, i ^ bit) for i in range(8)])  6.06 us
    pallas_call x1, Pallas kernels, shards(): pl.pallas_call(spectra_kernel, out_shape=jax.ShapeDtypeStruct((CAP, PAIRS...  5.58 us
    pallas_call x1, Pallas kernels, shards(): pl.pallas_call(score_kernel, out_shape=jax.ShapeDtypeStruct((CAP, SHIFTS...  4.97 us
    pallas_call x1, Pallas kernels, shards(): pl.pallas_call(send_kernel, out_shape=(jax.ShapeDtypeStruct((SEND, voxels...  4.44 us
    all_to_all x1, starting transfers between devices, shards(): by_rows = lax.all_to_all(grids, 'dom', 0, 0, tiled=True)  4.15 us
    ppermute x3, starting transfers between devices, shards(): lax.ppermute(everywhere, 'rot', [(i, i ^ bit) for i in range(8)])  4.04 us
  transfers between devices with their start and end apart: 8, of which 5 were waited for; matrix products, arithmetic and copies ran while one was open for 2% of the time, Pallas kernels for 20%

profile of v3, /device:TPU:1, one launch (start us, length us, event | category | flops | bytes accessed | tf_op | source)
XLA Modules:
  0.0 66.0 jit_solution(1496178615374913532)
XLA Ops:
  0.6 2.0 %fan.1 = bf16[128,4096]{1,0:T(8,128)(2,1)} custom-call(bf16[4,4,4096]{2,1,0:T(4,128)(2,1)} %refs_ref.1), custom_call_target="tpu_custom_call" | custom-call | flops 1024 | bytes 1024 | tf_op jit(solution)/shard_map/fan/pallas_call | solution.py:392
  2.7 8.5 %all-to-all-start = ((bf16[8,16,4096]{2,1,0:T(8,128)(2,1)}), bf16[8,16,4096]{2,1,0:T(8,128)(2,1)S(1)}, u32[]{:S(2)}, u32[]{:S(2)}) async-start(bf16[8,16,4096]{2,1,0:T(8,128)(2,1)} %bitcast.28), calls=%async_computation | async-start | bytes 2097152 | tf_op jit(solution)/shard_map/all_to_all | solution.py:445
  11.8 4.4 %send.1 = (bf16[128,4096]{1,0:T(8,128)(2,1)}, bf16[128,4096]{1,0:T(8,128)(2,1)}, s32[1]{0:T(128)}, s32[4]{0:T(128)}, s32[4]{0:T(128)}) custom-call(s32[8]{0:T(128)} %bitcast.30, s32[8]{0:T(128)} %rot_ref.1, s32[8]{0:T(128)} %bucket_ref.1, s32[1]{0:T(128)} %copy.20.live_ref, bf16[1,8]{1,0:T(2,128)(2,1)} %bitcast.32, bf16[512,4096]{1,0:T(8,128)(2,1)} %bitcast.26), custom_call_target="tpu_custom_call" | custom-call | flops 1024 | bytes 1024 | tf_op jit(solution)/shard_map/send/pallas_call | solution.py:421
  16.3 0.9 %collective-permute-start = (bf16[128,4096]{1,0:T(8,128)(2,1)}, bf16[128,4096]{1,0:T(8,128)(2,1)S(1)}, u32[]{:S(2)}, u32[]{:S(2)}) collective-permute-start(bf16[128,4096]{1,0:T(8,128)(2,1)} %get-tuple-element.14), channel_id=1, source_target_pairs={{0,8},{8,0},{16,24},{24,16},{32,40},{40,32},{48,56},{56,48},{64,72... | collective-permute-start | bytes 3145736 | tf_op jit(solution)/shard_map/ppermute | solution.py:444
  17.2 5.6 %spectra.1.zp_hbm = bf16[4,1536,256]{2,1,0:T(8,128)(2,1)} custom-call(s32[4]{0:T(128)} %get-tuple-element.12.slot_row_ref, s32[1]{0:T(128)} %get-tuple-element.10.count_ref, bf16[96,64]{1,0:T(8,128)(2,1)} %constant.25.clone.x_ref, bf16[512,4096]{1,0:T(8,128)(2,1)} %bitcast.27, bf16[256,256]{1,0:T(8,128)(2,1)} %constant.24.clone.table_ref), custom_call_target="tpu_custom_call" | custom-call | flops 20000000000 | bytes 1024 | tf_op jit(solution)/shard_map/spectra/pallas_call | solution.py:459
  22.8 0.0 copy-start.8
  22.8 0.0 copy-start.2
  22.8 0.0 copy-start.3
  22.8 0.0 copy-start.5
  22.8 0.0 copy-start.6
  22.9 0.0 collective-permute-done.other_ref
  22.9 1.2 %pair.1 = bf16[128,4096]{1,0:T(8,128)(2,1)} custom-call(bf16[128,4096]{1,0:T(8,128)(2,1)S(1)} %copy-done, bf16[128,4096]{1,0:T(8,128)(2,1)S(1)} %collective-permute-done.other_ref), custom_call_target="tpu_custom_call" | custom-call | flops 1024 | bytes 1024 | tf_op jit(solution)/shard_map/pair/pallas_call | solution.py:448
  24.1 3.1 %all-to-all-done = bf16[8,16,4096]{2,1,0:T(8,128)(2,1)S(1)} async-done(((bf16[8,16,4096]{2,1,0:T(8,128)(2,1)}), bf16[8,16,4096]{2,1,0:T(8,128)(2,1)S(1)}, u32[]{:S(2)}, u32[]{:S(2)}) %all-to-all-start) | async-done | bytes 1048608 | tf_op jit(solution)/shard_map/all_to_all | solution.py:445
  27.2 2.2 %collective-permute-start.1 = (bf16[128,4096]{1,0:T(8,128)(2,1)S(1)}, bf16[128,4096]{1,0:T(8,128)(2,1)}, u32[]{:S(2)}, u32[]{:S(2)}) collective-permute-start(bf16[128,4096]{1,0:T(8,128)(2,1)S(1)} %bitcast.24), channel_id=1, source_target_pairs={{0,8},{8,0},{16,24},{24,16},{32,40},{40,32},{48,56},{56,48},{64,72... | collective-permute-start | bytes 3145736 | tf_op jit(solution)/shard_map/ppermute | solution.py:473
  29.3 3.7 %all-to-all-start.1 = ((bf16[8,16,4096]{2,1,0:T(8,128)(2,1)}), bf16[8,16,4096]{2,1,0:T(8,128)(2,1)S(1)}, u32[]{:S(2)}, u32[]{:S(2)}) async-start(bf16[8,16,4096]{2,1,0:T(8,128)(2,1)} %bitcast.10), calls=%async_computation.1 | async-start | bytes 2097152 | tf_op jit(solution)/shard_map/all_to_all | solution.py:472
  33.0 0.2 convert_reduce_fusion
  33.3 0.0 copy-start.1
  33.3 5.0 %slot_scores.1 = f32[4,64,128]{2,1,0:T(8,128)S(1)} custom-call(s32[1]{0:T(128)} %get-tuple-element.10.count_ref, s32[4]{0:T(128)S(1)} %copy-done.7, bf16[4,1536,256]{2,1,0:T(8,128)(2,1)} %spectra.1.zp_hbm, f32[2,96,128]{2,1,0:T(8,128)S(1)} %copy-done.5, bf16[128,4096]{1,0:T(8,128)(2,1)S(1)} %bitcast.25, bf16[128,4096]{1,0:T(8,128)(2,1)} %collective-permute-done.1.other_ref, ...), custom_call_target="tpu_custom_call" | custom-call | flops 1024 | bytes 1024 | tf_op jit(solution)/shard_map/slot_scores/pallas_call | solution.py:476
  38.3 0.1 reshape.72
  38.4 1.3 %collective-permute-start.2 = (f32[4,512]{1,0:T(4,128)S(1)}, f32[4,512]{1,0:T(4,128)S(1)}, u32[]{:S(2)}, u32[]{:S(2)}) collective-permute-start(f32[4,512]{1,0:T(4,128)S(1)} %reshape.72), channel_id=1, source_target_pairs={{0,1},{1,0},{2,3},{3,2},{4,5},{5,4},{6,7},{7,6},{8,9},{9,8},{10,11... | collective-permute-start | bytes 24584 | tf_op jit(solution)/shard_map/ppermute | solution.py:508
  39.7 1.6 %collective-permute-done.2 = f32[4,512]{1,0:T(4,128)S(1)} collective-permute-done((f32[4,512]{1,0:T(4,128)S(1)}, f32[4,512]{1,0:T(4,128)S(1)}, u32[]{:S(2)}, u32[]{:S(2)}) %collective-permute-start.2) | collective-permute-done | bytes 8224 | tf_op jit(solution)/shard_map/ppermute | solution.py:508
  41.3 2.3 %collective-permute-start.3 = (f32[8,512]{1,0:T(8,128)S(1)}, f32[8,512]{1,0:T(8,128)S(1)}, u32[]{:S(2)}, u32[]{:S(2)}) collective-permute-start(f32[8,512]{1,0:T(8,128)S(1)} %pad_maximum_fusion.2), channel_id=1, source_target_pairs={{0,2},{1,3},{2,0},{3,1},{4,6},{5,7},{6,4},{7,5},{8,10},{9,11},{10,... | collective-permute-start | bytes 49160 | tf_op jit(solution)/shard_map/ppermute | solution.py:508
  43.6 6.7 %all-to-all-done.1 = bf16[8,16,4096]{2,1,0:T(8,128)(2,1)S(1)} async-done(((bf16[8,16,4096]{2,1,0:T(8,128)(2,1)}), bf16[8,16,4096]{2,1,0:T(8,128)(2,1)S(1)}, u32[]{:S(2)}, u32[]{:S(2)}) %all-to-all-start.1) | async-done | bytes 1048608 | tf_op jit(solution)/shard_map/all_to_all | solution.py:472
  50.3 1.5 %yz_planes.1 = bf16[1024,128]{1,0:T(8,128)(2,1)} custom-call(bf16[128,4096]{1,0:T(8,128)(2,1)S(1)} %bitcast.23, bf16[256,256]{1,0:T(8,128)(2,1)S(1)} %copy-done.4), custom_call_target="tpu_custom_call" | custom-call | flops 1024 | bytes 1024 | tf_op jit(solution)/shard_map/yz_planes/pallas_call | solution.py:520
  51.8 4.2 %all-to-all-start.2 = ((bf16[16,64,128]{2,1,0:T(8,128)(2,1)}), bf16[16,64,128]{2,1,0:T(8,128)(2,1)S(1)}, u32[]{:S(2)}, u32[]{:S(2)}) async-start(bf16[16,64,128]{2,1,0:T(8,128)(2,1)} %bitcast.12), calls=%async_computation.2 | async-start | bytes 524288 | tf_op jit(solution)/shard_map/all_to_all | solution.py:530
  56.0 0.0 collective-permute-done.3
  56.0 0.5 collective-permute-start.4
  56.5 0.1 fusion.1
  56.6 4.5 %collective-permute-done.4 = f32[16,512]{1,0:T(8,128)S(1)} collective-permute-done((f32[16,512]{1,0:T(8,128)S(1)}, f32[16,512]{1,0:T(8,128)S(1)}, u32[]{:S(2)}, u32[]{:S(2)}) %collective-permute-start.4) | collective-permute-done | bytes 32800 | tf_op jit(solution)/shard_map/ppermute | solution.py:508
  61.0 0.7 %select_reduce_fusion = f32[8,512]{1,0:T(8,128)} fusion(f32[32,512]{1,0:T(8,128)S(1)} %pad_maximum_fusion, pred[8,32]{1,0:T(8,128)(4,1)S(1)} %fusion.1), kind=kLoop, calls=%fused_computation | loop fusion | flops 258048 | bytes 82176 | tf_op jit(solution)/shard_map/reduce_sum | solution.py:515
  61.8 2.9 %all-to-all-done.2.rows_ref = bf16[16,64,128]{2,1,0:T(8,128)(2,1)S(1)} async-done(((bf16[16,64,128]{2,1,0:T(8,128)(2,1)}), bf16[16,64,128]{2,1,0:T(8,128)(2,1)S(1)}, u32[]{:S(2)}, u32[]{:S(2)}) %all-to-all-start.2) | async-done | bytes 262176 | tf_op jit(solution)/shard_map/all_to_all | solution.py:530
  64.7 1.3 %x_rows.1 = f32[4,4,64,128]{3,2,1,0:T(8,128)} custom-call(bf16[16,64,128]{2,1,0:T(8,128)(2,1)S(1)} %all-to-all-done.2.rows_ref, bf16[2,256,256]{2,1,0:T(8,128)(2,1)S(1)} %copy-done.1), custom_call_target="tpu_custom_call" | custom-call | tf_op jit(solution)/shard_map/x_rows/pallas_call | solution.py:531
  (20 shorter events, 0.1 us)
Async XLA Ops:
  2.7 24.5 %all-to-all-start = ((bf16[8,16,4096]{2,1,0:T(8,128)(2,1)}), bf16[8,16,4096]{2,1,0:T(8,128)(2,1)S(1)}, u32[]{:S(2)}, u32[]{:S(2)}) async-start(bf16[8,16,4096]{2,1,0:T(8,128)(2,1)} %bitcast.28), calls=%async_computation | async-start | bytes 2097152 | tf_op jit(solution)/shard_map/all_to_all | solution.py:445
  16.3 6.6 %collective-permute-start = (bf16[128,4096]{1,0:T(8,128)(2,1)}, bf16[128,4096]{1,0:T(8,128)(2,1)S(1)}, u32[]{:S(2)}, u32[]{:S(2)}) collective-permute-start(bf16[128,4096]{1,0:T(8,128)(2,1)} %get-tuple-element.14), channel_id=1, source_target_pairs={{0,8},{8,0},{16,24},{24,16},{32,40},{40,32},{48,56},{56,48},{64,72... | collective-permute-start | bytes 3145736 | tf_op jit(solution)/shard_map/ppermute | solution.py:444
  17.2 5.7 %copy-start = (bf16[128,4096]{1,0:T(8,128)(2,1)S(1)}, bf16[128,4096]{1,0:T(8,128)(2,1)}, u32[]{:S(2)}) copy-start(bf16[128,4096]{1,0:T(8,128)(2,1)} %get-tuple-element.13.own_ref) | copy-start | bytes 3145732
  22.8 10.2 %copy-start.8 = (s32[8,1]{0,1:T(1,128)S(1)}, s32[8,1]{0,1:T(1,128)}, u32[]{:S(2)}) copy-start(s32[8,1]{0,1:T(1,128)} %param.16) | copy-start | bytes 100
  22.8 10.4 %copy-start.2 = (bf16[256,256]{1,0:T(8,128)(2,1)S(1)}, bf16[256,256]{1,0:T(8,128)(2,1)}, u32[]{:S(2)}) copy-start(bf16[256,256]{1,0:T(8,128)(2,1)} %constant.24.clone.table_ref) | copy-start | bytes 393220
  22.8 10.4 %copy-start.3 = (bf16[512,128]{1,0:T(8,128)(2,1)S(1)}, bf16[512,128]{1,0:T(8,128)(2,1)}, u32[]{:S(2)}) copy-start(bf16[512,128]{1,0:T(8,128)(2,1)} %constant.28.clone.wz_ref) | copy-start | bytes 393220
  22.8 10.4 %copy-start.5 = (f32[2,96,128]{2,1,0:T(8,128)S(1)}, f32[2,96,128]{2,1,0:T(8,128)}, u32[]{:S(2)}) copy-start(f32[2,96,128]{2,1,0:T(8,128)} %constant.26.clone.x_ref) | copy-start | bytes 294916
  22.8 10.4 %copy-start.6 = (bf16[16,40]{1,0:T(8,128)(2,1)S(1)}, bf16[16,40]{1,0:T(8,128)(2,1)}, u32[]{:S(2)}) copy-start(bf16[16,40]{1,0:T(8,128)(2,1)} %constant.27.clone.ex_ref) | copy-start | bytes 3844
  22.9 10.4 %copy-start.7 = (s32[4]{0:T(128)S(1)}, s32[4]{0:T(128)}, u32[]{:S(2)}) copy-start(s32[4]{0:T(128)} %get-tuple-element.11.slot_rot_ref) | copy-start | bytes 52
  27.2 6.1 %collective-permute-start.1 = (bf16[128,4096]{1,0:T(8,128)(2,1)S(1)}, bf16[128,4096]{1,0:T(8,128)(2,1)}, u32[]{:S(2)}, u32[]{:S(2)}) collective-permute-start(bf16[128,4096]{1,0:T(8,128)(2,1)S(1)} %bitcast.24), channel_id=1, source_target_pairs={{0,8},{8,0},{16,24},{24,16},{32,40},{40,32},{48,56},{56,48},{64,72... | collective-permute-start | bytes 3145736 | tf_op jit(solution)/shard_map/ppermute | solution.py:473
  29.3 21.0 %copy-start.4 = (bf16[256,256]{1,0:T(8,128)(2,1)S(1)}, bf16[256,256]{1,0:T(8,128)(2,1)}, u32[]{:S(2)}) copy-start(bf16[256,256]{1,0:T(8,128)(2,1)} %constant.29.clone.table_ref) | copy-start | bytes 393220
  29.3 21.0 %all-to-all-start.1 = ((bf16[8,16,4096]{2,1,0:T(8,128)(2,1)}), bf16[8,16,4096]{2,1,0:T(8,128)(2,1)S(1)}, u32[]{:S(2)}, u32[]{:S(2)}) async-start(bf16[8,16,4096]{2,1,0:T(8,128)(2,1)} %bitcast.10), calls=%async_computation.1 | async-start | bytes 2097152 | tf_op jit(solution)/shard_map/all_to_all | solution.py:472
  33.3 31.4 %copy-start.1 = (bf16[2,256,256]{2,1,0:T(8,128)(2,1)S(1)}, bf16[2,256,256]{2,1,0:T(8,128)(2,1)}, u32[]{:S(2)}) copy-start(bf16[2,256,256]{2,1,0:T(8,128)(2,1)} %constant.30.clone.table_ref) | copy-start | bytes 786436
  38.4 2.9 %collective-permute-start.2 = (f32[4,512]{1,0:T(4,128)S(1)}, f32[4,512]{1,0:T(4,128)S(1)}, u32[]{:S(2)}, u32[]{:S(2)}) collective-permute-start(f32[4,512]{1,0:T(4,128)S(1)} %reshape.72), channel_id=1, source_target_pairs={{0,1},{1,0},{2,3},{3,2},{4,5},{5,4},{6,7},{7,6},{8,9},{9,8},{10,11... | collective-permute-start | bytes 24584 | tf_op jit(solution)/shard_map/ppermute | solution.py:508
  41.3 14.7 %collective-permute-start.3 = (f32[8,512]{1,0:T(8,128)S(1)}, f32[8,512]{1,0:T(8,128)S(1)}, u32[]{:S(2)}, u32[]{:S(2)}) collective-permute-start(f32[8,512]{1,0:T(8,128)S(1)} %pad_maximum_fusion.2), channel_id=1, source_target_pairs={{0,2},{1,3},{2,0},{3,1},{4,6},{5,7},{6,4},{7,5},{8,10},{9,11},{10,... | collective-permute-start | bytes 49160 | tf_op jit(solution)/shard_map/ppermute | solution.py:508
  51.8 12.9 %all-to-all-start.2 = ((bf16[16,64,128]{2,1,0:T(8,128)(2,1)}), bf16[16,64,128]{2,1,0:T(8,128)(2,1)S(1)}, u32[]{:S(2)}, u32[]{:S(2)}) async-start(bf16[16,64,128]{2,1,0:T(8,128)(2,1)} %bitcast.12), calls=%async_computation.2 | async-start | bytes 524288 | tf_op jit(solution)/shard_map/all_to_all | solution.py:530
  56.0 5.0 %collective-permute-start.4 = (f32[16,512]{1,0:T(8,128)S(1)}, f32[16,512]{1,0:T(8,128)S(1)}, u32[]{:S(2)}, u32[]{:S(2)}) collective-permute-start(f32[16,512]{1,0:T(8,128)S(1)} %pad_maximum_fusion.1), channel_id=1, source_target_pairs={{0,4},{1,5},{2,6},{3,7},{4,0},{5,1},{6,2},{7,3},{8,12},{9,13},{10,... | collective-permute-start | bytes 98312 | tf_op jit(solution)/shard_map/ppermute | solution.py:508

commit v4 on v3

--- a/solution.py
+++ b/solution.py
@@ -18,6 +18,8 @@
 PAIRS = BOX // 2
 DOM = 16
 CHIPS = DOM // 2
+LINE = DOM // 4
+SAME_LINE = [[LINE * z + i for z in range(LINE)] for i in range(4)]
 SAME_CORE = [[2 * chip + core for chip in range(CHIPS)] for core in range(2)]
 BF = jnp.bfloat16
 F32 = jnp.float32
@@ -102,7 +104,7 @@
         pltpu.make_async_copy(
             block_s, out_hbm.at[chip * PER_CHIP : (chip + 1) * PER_CHIP], sems.at[chip]
         )
-        for chip in range(CHIPS)
+        for chip in range(LINE)
     ]
     for copy in copies:
         copy.start()
@@ -228,8 +230,10 @@
     slot_rot_ref,
     zp_hbm,
     x_ref,
-    own_ref,
-    other_ref,
+    part_0_ref,
+    part_1_ref,
+    part_2_ref,
+    part_3_ref,
     table_ref,
     ex_ref,
     wz_ref,
@@ -252,17 +256,18 @@
 
     @pl.when(count_ref[0] > 0)
     def _():
-        core = lax.axis_index("dom") & 1
-        ref_lane = lax.broadcasted_iota(jnp.int32, (1, SEND), 1)
+        place = lax.axis_index("dom") & 3
+        spread = jnp.concatenate([x_ref[place ^ part] for part in (0, 2, 1, 3)], axis=1)
+        ref_lane = lax.broadcasted_iota(jnp.int32, (1, ROT_CLS * BOX), 1)
         ref_rot = (ref_lane // PLANES) & (ROT_CLS - 1)
         for to in range(CAP):
             rows = slice(to * 2 * KXP, (to + 1) * 2 * KXP)
             wanted = ref_rot == slot_rot_ref[to]
-            pick_s[rows, :SEND] = jnp.where(wanted, x_ref[core], 0.0).astype(BF)
-            pick_s[rows, SEND:] = jnp.where(wanted, x_ref[1 - core], 0.0).astype(BF)
+            pick_s[rows] = jnp.where(wanted, spread, 0.0).astype(BF)
+        parts = (part_0_ref, part_1_ref, part_2_ref, part_3_ref)
         for start in range(0, BOX * BOX, 512):
             lanes = slice(start, start + 512)
-            planes = jnp.concatenate([own_ref[:, lanes], other_ref[:, lanes]], axis=0)
+            planes = jnp.concatenate([part[:, lanes] for part in parts], axis=0)
             part = jnp.dot(pick_s[...], planes, preferred_element_type=F32)
             x_s[:, :, lanes] = part.astype(BF).reshape(CAP, 2 * KXP, 512)
 
@@ -391,13 +396,13 @@
 
     mine_refs = pl.pallas_call(
         fan_kernel,
-        out_shape=jax.ShapeDtypeStruct((SEND, voxels), BF),
+        out_shape=jax.ShapeDtypeStruct((LINE * PER_CHIP, voxels), BF),
         in_specs=[VMEM],
         out_specs=HBM,
         scratch_shapes=[
             pltpu.VMEM((PER_CHIP, voxels), F32),
             pltpu.VMEM((PER_CHIP, voxels), BF),
-            pltpu.SemaphoreType.DMA((CHIPS,)),
+            pltpu.SemaphoreType.DMA((LINE,)),
         ],
         compiler_params=params(54),
         cost_estimate=cost(1024, 1024),
@@ -407,9 +412,9 @@
     flat = particles.reshape(columns, voxels)
     classes = part_class.reshape(block_size)
     x_half = x_half_table()
-    by_core = x_half.reshape(2 * KXP, CHIPS, 2, 1, PLANES)
-    by_core = np.broadcast_to(by_core, (2 * KXP, CHIPS, 2, ROT_CLS, PLANES))
-    by_core = by_core.transpose(2, 0, 1, 3, 4).reshape(2, 2 * KXP, SEND)
+    by_place = x_half.reshape(2 * KXP, LINE, 4, 1, PLANES)
+    by_place = np.broadcast_to(by_place, (2 * KXP, LINE, 4, ROT_CLS, PLANES))
+    by_place = by_place.transpose(2, 0, 1, 3, 4).reshape(4, 2 * KXP, BOX)
     held = [
         pltpu.VMEM((CAP * BOX, voxels), BF),
         pltpu.SemaphoreType.DMA((CAP,)),
@@ -442,8 +447,8 @@
         flat,
     )
     other = lax.ppermute(to_send, "dom", to_other)
-    refs_own = lax.all_to_all(
-        mine_refs, "dom", 0, 0, tiled=True, axis_index_groups=SAME_CORE
+    refs_line = lax.all_to_all(
+        mine_refs, "dom", 0, 0, tiled=True, axis_index_groups=SAME_LINE
     )
     pair_sum = pl.pallas_call(
         pair_kernel,
@@ -454,6 +459,10 @@
         cost_estimate=cost(1024, 1024),
         name="pair",
     )(own, other)
+
+    refs_line, slot_row, pair_sum = lax.optimization_barrier((refs_line, slot_row, pair_sum))
+    refs_y = lax.ppermute(refs_line, "dom", [(i, i ^ 2) for i in range(DOM)])
+    arrived = lax.all_to_all(pair_sum, "dom", 0, 0, tiled=True, axis_index_groups=SAME_CORE)
 
     z_table = jnp.asarray(z_complex_table().astype(BF))
     spectra = pl.pallas_call(
@@ -468,15 +477,18 @@
         name="spectra",
     )(slot_row, count, jnp.asarray(x_half.astype(BF)), flat, z_table)
 
-    refs_own, spectra, pair_sum = lax.optimization_barrier((refs_own, spectra, pair_sum))
-    arrived = lax.all_to_all(pair_sum, "dom", 0, 0, tiled=True, axis_index_groups=SAME_CORE)
-    refs_other = lax.ppermute(refs_own, "dom", to_other)
+    parts = (
+        refs_line,
+        refs_y,
+        lax.ppermute(refs_line, "dom", to_other),
+        lax.ppermute(refs_y, "dom", to_other),
+    )
     ex, wz = shift_tables()
 
     slots = pl.pallas_call(
         score_kernel,
         out_shape=jax.ShapeDtypeStruct((CAP, SHIFTS * SHIFTS, 128), F32),
-        in_specs=[SMEM, SMEM, HBM] + [VMEM] * 6,
+        in_specs=[SMEM, SMEM, HBM] + [VMEM] * 8,
         out_specs=VMEM,
         scratch_shapes=[
             pltpu.VMEM((CAP * 2 * KXP, 2 * SEND), BF),
@@ -487,16 +499,15 @@
             pltpu.VMEM((SHIFTS, KXV, 4 * BOX), F32),
             pltpu.SemaphoreType.DMA((CAP,)),
         ],
-        compiler_params=params(52),
+        compiler_params=params(51),
         cost_estimate=cost(1024, 1024),
         name="slot_scores",
     )(
         count,
         slot_rot,
         spectra,
-        jnp.asarray(by_core, F32),
-        refs_own,
-        refs_other,
+        jnp.asarray(by_place, F32),
+        *parts,
         z_table,
         jnp.asarray(ex.astype(BF)),
         jnp.asarray(wz.astype(BF)),

time: 66.5 us -> 77.7 us (1.17)
  the two profiles are of different devices: /device:TPU:1 before, /device:TPU:14 now
where the time goes in v4:
time: 77.7 us; the launch traced here: 76.6 us
  waiting for transfers between devices  28.6 us (37%)
  starting transfers between devices  28.3 us (36%)
  Pallas kernels  15.7 us (20%)
  between operations  1.5 us (2%)
  local copies, waits for them, and re-layouts  1.42 us (2%)
  other arithmetic  1.04 us (1%)
    ppermute x1, waiting for transfers between devices, shards(): refs_y = lax.ppermute(refs_line, 'dom', [(i, i ^ 2) for i in range(DOM)])  10.4 us
    all_to_all x1, starting transfers between devices, shards(): by_rows = lax.all_to_all(grids, 'dom', 0, 0, tiled=True)  9.04 us
    ppermute x3, starting transfers between devices, shards(): lax.ppermute(everywhere, 'rot', [(i, i ^ bit) for i in range(8)])  8.08 us
    all_to_all x1, waiting for transfers between devices, shards(): lax.all_to_all(mine_refs, 'dom', 0, 0, tiled=True, axis_index_groups=SAME...  7.66 us
    ppermute x3, waiting for transfers between devices, shards(): lax.ppermute(everywhere, 'rot', [(i, i ^ bit) for i in range(8)])  5.95 us
    all_to_all x1, starting transfers between devices, shards(): lax.all_to_all(mine_refs, 'dom', 0, 0, tiled=True, axis_index_groups=SAME...  5.32 us
    pallas_call x1, Pallas kernels, shards(): pl.pallas_call(send_kernel, out_shape=(jax.ShapeDtypeStruct((SEND, voxels...  4.68 us
    all_to_all x1, waiting for transfers between devices, shards(): by_rows = lax.all_to_all(grids, 'dom', 0, 0, tiled=True)  4.63 us
  transfers between devices with their start and end apart: 10, of which 5 were waited for; matrix products, arithmetic and copies ran while one was open for 2% of the time, Pallas kernels for 13%

profile of v4, /device:TPU:14, one launch (start us, length us, event | category | flops | bytes accessed | tf_op | source)
XLA Modules:
  0.0 76.6 jit_solution(7687244731921284553)
XLA Ops:
  1.3 4.7 %send.1 = (bf16[128,4096]{1,0:T(8,128)(2,1)}, bf16[128,4096]{1,0:T(8,128)(2,1)}, s32[1]{0:T(128)}, s32[4]{0:T(128)}, s32[4]{0:T(128)}) custom-call(s32[8]{0:T(128)} %bitcast.31, s32[8]{0:T(128)} %rot_ref.1, s32[8]{0:T(128)} %bucket_ref.1, s32[1]{0:T(128)} %copy.20.live_ref, bf16[1,8]{1,0:T(2,128)(2,1)} %bitcast.33, bf16[512,4096]{1,0:T(8,128)(2,1)} %bitcast.27), custom_call_target="tpu_custom_call" | custom-call | flops 1024 | bytes 1024 | tf_op jit(solution)/shard_map/send/pallas_call | solution.py:426
  6.0 0.1 collective-permute-start
  6.1 1.8 %fan.1 = bf16[64,4096]{1,0:T(8,128)(2,1)} custom-call(bf16[4,4,4096]{2,1,0:T(4,128)(2,1)} %refs_ref.1), custom_call_target="tpu_custom_call" | custom-call | flops 1024 | bytes 1024 | tf_op jit(solution)/shard_map/fan/pallas_call | solution.py:397
  7.9 5.3 %all-to-all-start = ((bf16[4,16,4096]{2,1,0:T(8,128)(2,1)}), bf16[4,16,4096]{2,1,0:T(8,128)(2,1)S(1)}, u32[]{:S(2)}, u32[]{:S(2)}) async-start(bf16[4,16,4096]{2,1,0:T(8,128)(2,1)} %bitcast.29), calls=%async_computation | async-start | bytes 1048576 | tf_op jit(solution)/shard_map/all_to_all | solution.py:450
  13.2 0.0 collective-permute-done.other_ref
  13.2 1.2 %copy-done = bf16[128,4096]{1,0:T(8,128)(2,1)S(1)} copy-done((bf16[128,4096]{1,0:T(8,128)(2,1)S(1)}, bf16[128,4096]{1,0:T(8,128)(2,1)}, u32[]{:S(2)}) %copy-start) | copy-done | bytes 1048600
  14.4 1.2 %pair.1 = bf16[128,4096]{1,0:T(8,128)(2,1)} custom-call(bf16[128,4096]{1,0:T(8,128)(2,1)S(1)} %copy-done, bf16[128,4096]{1,0:T(8,128)(2,1)S(1)} %collective-permute-done.other_ref), custom_call_target="tpu_custom_call" | custom-call | flops 1024 | bytes 1024 | tf_op jit(solution)/shard_map/pair/pallas_call | solution.py:453
  15.7 7.7 %all-to-all-done = bf16[4,16,4096]{2,1,0:T(8,128)(2,1)S(1)} async-done(((bf16[4,16,4096]{2,1,0:T(8,128)(2,1)}), bf16[4,16,4096]{2,1,0:T(8,128)(2,1)S(1)}, u32[]{:S(2)}, u32[]{:S(2)}) %all-to-all-start) | async-done | bytes 524320 | tf_op jit(solution)/shard_map/all_to_all | solution.py:450
  23.3 2.1 %collective-permute-start.1 = (bf16[64,4096]{1,0:T(8,128)(2,1)S(1)}, bf16[64,4096]{1,0:T(8,128)(2,1)S(1)}, u32[]{:S(2)}, u32[]{:S(2)}) collective-permute-start(bf16[64,4096]{1,0:T(8,128)(2,1)S(1)} %bitcast.24), channel_id=1, source_target_pairs={{0,16},{8,24},{16,0},{24,8},{32,48},{40,56},{48,32},{56,40},{64,80... | collective-permute-start | bytes 1572872 | tf_op jit(solution)/shard_map/ppermute | solution.py:464
  25.4 0.2 convert_reduce_fusion
  25.6 0.1 collective-permute-start.2
  25.7 3.6 %all-to-all-start.1 = ((bf16[8,16,4096]{2,1,0:T(8,128)(2,1)}), bf16[8,16,4096]{2,1,0:T(8,128)(2,1)S(1)}, u32[]{:S(2)}, u32[]{:S(2)}) async-start(bf16[8,16,4096]{2,1,0:T(8,128)(2,1)} %bitcast.10), calls=%async_computation.1 | async-start | bytes 2097152 | tf_op jit(solution)/shard_map/all_to_all | solution.py:465
  29.3 10.4 %collective-permute-done.1.part_1_ref = bf16[64,4096]{1,0:T(8,128)(2,1)S(1)} collective-permute-done((bf16[64,4096]{1,0:T(8,128)(2,1)S(1)}, bf16[64,4096]{1,0:T(8,128)(2,1)S(1)}, u32[]{:S(2)}, u32[]{:S(2)}) %collective-permute-start.1) | collective-permute-done | bytes 524320 | tf_op jit(solution)/shard_map/ppermute | solution.py:464
  39.7 0.0 copy-start.6
  39.7 3.9 %spectra.1.zp_hbm = bf16[4,1536,256]{2,1,0:T(8,128)(2,1)} custom-call(s32[4]{0:T(128)} %get-tuple-element.15.slot_row_ref, s32[1]{0:T(128)} %get-tuple-element.10.count_ref, bf16[96,64]{1,0:T(8,128)(2,1)} %constant.25.clone.x_ref, bf16[512,4096]{1,0:T(8,128)(2,1)} %bitcast.28, bf16[256,256]{1,0:T(8,128)(2,1)} %constant.24.clone.table_ref), custom_call_target="tpu_custom_call" | custom-call | flops 20000000000 | bytes 1024 | tf_op jit(solution)/shard_map/spectra/pallas_call | solution.py:468
  43.6 0.0 copy-start.5
  43.7 0.0 collective-permute-done.2.part_2_ref
  43.7 0.0 copy-start.1
  43.7 1.3 %slot_scores.1 = f32[4,64,128]{2,1,0:T(8,128)S(1)} custom-call(s32[1]{0:T(128)} %get-tuple-element.10.count_ref, s32[4]{0:T(128)S(1)} %copy-done.7, bf16[4,1536,256]{2,1,0:T(8,128)(2,1)} %spectra.1.zp_hbm, f32[4,96,64]{2,1,0:T(8,128)S(1)} %copy-done.2, bf16[64,4096]{1,0:T(8,128)(2,1)S(1)} %bitcast.26, ...), custom_call_target="tpu_custom_call" | custom-call | flops 1024 | bytes 1024 | tf_op jit(solution)/shard_map/slot_scores/pallas_call | solution.py:488
  45.1 0.1 reshape.72
  45.2 5.3 %collective-permute-start.4 = (f32[4,512]{1,0:T(4,128)S(1)}, f32[4,512]{1,0:T(4,128)S(1)}, u32[]{:S(2)}, u32[]{:S(2)}) collective-permute-start(f32[4,512]{1,0:T(4,128)S(1)} %reshape.72), channel_id=1, source_target_pairs={{0,1},{1,0},{2,3},{3,2},{4,5},{5,4},{6,7},{7,6},{8,9},{9,8},{10,11... | collective-permute-start | bytes 24584 | tf_op jit(solution)/shard_map/ppermute | solution.py:519
  50.5 1.6 %collective-permute-done.4 = f32[4,512]{1,0:T(4,128)S(1)} collective-permute-done((f32[4,512]{1,0:T(4,128)S(1)}, f32[4,512]{1,0:T(4,128)S(1)}, u32[]{:S(2)}, u32[]{:S(2)}) %collective-permute-start.4) | collective-permute-done | bytes 8224 | tf_op jit(solution)/shard_map/ppermute | solution.py:519
  52.1 2.7 %collective-permute-start.5 = (f32[8,512]{1,0:T(8,128)S(1)}, f32[8,512]{1,0:T(8,128)S(1)}, u32[]{:S(2)}, u32[]{:S(2)}) collective-permute-start(f32[8,512]{1,0:T(8,128)S(1)} %pad_maximum_fusion.2), channel_id=1, source_target_pairs={{0,2},{1,3},{2,0},{3,1},{4,6},{5,7},{6,4},{7,5},{8,10},{9,11},{10,... | collective-permute-start | bytes 49160 | tf_op jit(solution)/shard_map/ppermute | solution.py:519
  54.8 1.5 %yz_planes.1 = bf16[1024,128]{1,0:T(8,128)(2,1)} custom-call(bf16[128,4096]{1,0:T(8,128)(2,1)S(1)} %bitcast.23, bf16[256,256]{1,0:T(8,128)(2,1)S(1)} %copy-done.5), custom_call_target="tpu_custom_call" | custom-call | flops 1024 | bytes 1024 | tf_op jit(solution)/shard_map/yz_planes/pallas_call | solution.py:531
  56.3 9.0 %all-to-all-start.2 = ((bf16[16,64,128]{2,1,0:T(8,128)(2,1)}), bf16[16,64,128]{2,1,0:T(8,128)(2,1)S(1)}, u32[]{:S(2)}, u32[]{:S(2)}) async-start(bf16[16,64,128]{2,1,0:T(8,128)(2,1)} %bitcast.12), calls=%async_computation.2 | async-start | bytes 524288 | tf_op jit(solution)/shard_map/all_to_all | solution.py:541
  65.4 0.0 collective-permute-done.5
  65.4 0.1 collective-permute-start.6
  65.5 0.1 fusion.1
  65.6 4.3 %collective-permute-done.6 = f32[16,512]{1,0:T(8,128)S(1)} collective-permute-done((f32[16,512]{1,0:T(8,128)S(1)}, f32[16,512]{1,0:T(8,128)S(1)}, u32[]{:S(2)}, u32[]{:S(2)}) %collective-permute-start.6) | collective-permute-done | bytes 32800 | tf_op jit(solution)/shard_map/ppermute | solution.py:519
  69.9 0.7 select_reduce_fusion
  70.7 4.6 %all-to-all-done.2.rows_ref = bf16[16,64,128]{2,1,0:T(8,128)(2,1)S(1)} async-done(((bf16[16,64,128]{2,1,0:T(8,128)(2,1)}), bf16[16,64,128]{2,1,0:T(8,128)(2,1)S(1)}, u32[]{:S(2)}, u32[]{:S(2)}) %all-to-all-start.2) | async-done | bytes 262176 | tf_op jit(solution)/shard_map/all_to_all | solution.py:541
  75.3 1.3 %x_rows.1 = f32[4,4,64,128]{3,2,1,0:T(8,128)} custom-call(bf16[16,64,128]{2,1,0:T(8,128)(2,1)S(1)} %all-to-all-done.2.rows_ref, bf16[2,256,256]{2,1,0:T(8,128)(2,1)S(1)} %copy-done.1), custom_call_target="tpu_custom_call" | custom-call | tf_op jit(solution)/shard_map/x_rows/pallas_call | solution.py:542
  (24 shorter events, 0.1 us)
Async XLA Ops:
  1.3 24.2 %copy-start.8 = (s32[8,1]{0,1:T(1,128)S(1)}, s32[8,1]{0,1:T(1,128)}, u32[]{:S(2)}) copy-start(s32[8,1]{0,1:T(1,128)} %param.16) | copy-start | bytes 100
  6.0 7.2 %collective-permute-start = (bf16[128,4096]{1,0:T(8,128)(2,1)}, bf16[128,4096]{1,0:T(8,128)(2,1)S(1)}, u32[]{:S(2)}, u32[]{:S(2)}) collective-permute-start(bf16[128,4096]{1,0:T(8,128)(2,1)} %get-tuple-element.14), channel_id=1, source_target_pairs={{0,8},{8,0},{16,24},{24,16},{32,40},{40,32},{48,56},{56,48},{64,72... | collective-permute-start | bytes 3145736 | tf_op jit(solution)/shard_map/ppermute | solution.py:449
  7.9 15.5 %all-to-all-start = ((bf16[4,16,4096]{2,1,0:T(8,128)(2,1)}), bf16[4,16,4096]{2,1,0:T(8,128)(2,1)S(1)}, u32[]{:S(2)}, u32[]{:S(2)}) async-start(bf16[4,16,4096]{2,1,0:T(8,128)(2,1)} %bitcast.29), calls=%async_computation | async-start | bytes 1048576 | tf_op jit(solution)/shard_map/all_to_all | solution.py:450
  13.2 1.2 %copy-start = (bf16[128,4096]{1,0:T(8,128)(2,1)S(1)}, bf16[128,4096]{1,0:T(8,128)(2,1)}, u32[]{:S(2)}) copy-start(bf16[128,4096]{1,0:T(8,128)(2,1)} %get-tuple-element.13.own_ref) | copy-start | bytes 3145732
  23.3 16.4 %collective-permute-start.1 = (bf16[64,4096]{1,0:T(8,128)(2,1)S(1)}, bf16[64,4096]{1,0:T(8,128)(2,1)S(1)}, u32[]{:S(2)}, u32[]{:S(2)}) collective-permute-start(bf16[64,4096]{1,0:T(8,128)(2,1)S(1)} %bitcast.24), channel_id=1, source_target_pairs={{0,16},{8,24},{16,0},{24,8},{32,48},{40,56},{48,32},{56,40},{64,80... | collective-permute-start | bytes 1572872 | tf_op jit(solution)/shard_map/ppermute | solution.py:464
  25.6 18.0 %collective-permute-start.2 = (bf16[64,4096]{1,0:T(8,128)(2,1)S(1)}, bf16[64,4096]{1,0:T(8,128)(2,1)S(1)}, u32[]{:S(2)}, u32[]{:S(2)}) collective-permute-start(bf16[64,4096]{1,0:T(8,128)(2,1)S(1)} %bitcast.25), channel_id=1, source_target_pairs={{0,8},{8,0},{16,24},{24,16},{32,40},{40,32},{48,56},{56,48},{64,72... | collective-permute-start | bytes 1572872 | tf_op jit(solution)/shard_map/ppermute | solution.py:483
  25.7 29.1 %all-to-all-start.1 = ((bf16[8,16,4096]{2,1,0:T(8,128)(2,1)}), bf16[8,16,4096]{2,1,0:T(8,128)(2,1)S(1)}, u32[]{:S(2)}, u32[]{:S(2)}) async-start(bf16[8,16,4096]{2,1,0:T(8,128)(2,1)} %bitcast.10), calls=%async_computation.1 | async-start | bytes 2097152 | tf_op jit(solution)/shard_map/all_to_all | solution.py:465
  39.7 4.0 %collective-permute-start.3 = (bf16[64,4096]{1,0:T(8,128)(2,1)S(1)}, bf16[64,4096]{1,0:T(8,128)(2,1)S(1)}, u32[]{:S(2)}, u32[]{:S(2)}) collective-permute-start(bf16[64,4096]{1,0:T(8,128)(2,1)S(1)} %collective-permute-done.1.part_1_ref), channel_id=1, source_target_pairs={{0,8},{8,0},{16,24},{24,16},{32,40},{40,32},{48,56},{56,48},{64,72... | collective-permute-start | bytes 1572872 | tf_op jit(solution)/shard_map/ppermute | solution.py:484
  39.7 4.0 %copy-start.2 = (f32[4,96,64]{2,1,0:T(8,128)S(1)}, f32[4,96,64]{2,1,0:T(8,128)}, u32[]{:S(2)}) copy-start(f32[4,96,64]{2,1,0:T(8,128)} %constant.26.clone.x_ref) | copy-start | bytes 294916
  39.7 4.0 %copy-start.3 = (bf16[256,256]{1,0:T(8,128)(2,1)S(1)}, bf16[256,256]{1,0:T(8,128)(2,1)}, u32[]{:S(2)}) copy-start(bf16[256,256]{1,0:T(8,128)(2,1)} %constant.24.clone.table_ref) | copy-start | bytes 393220
  39.7 4.0 %copy-start.4 = (bf16[512,128]{1,0:T(8,128)(2,1)S(1)}, bf16[512,128]{1,0:T(8,128)(2,1)}, u32[]{:S(2)}) copy-start(bf16[512,128]{1,0:T(8,128)(2,1)} %constant.28.clone.wz_ref) | copy-start | bytes 393220
  39.7 4.0 %copy-start.6 = (bf16[16,40]{1,0:T(8,128)(2,1)S(1)}, bf16[16,40]{1,0:T(8,128)(2,1)}, u32[]{:S(2)}) copy-start(bf16[16,40]{1,0:T(8,128)(2,1)} %constant.27.clone.ex_ref) | copy-start | bytes 3844
  39.7 4.0 %copy-start.7 = (s32[4]{0:T(128)S(1)}, s32[4]{0:T(128)}, u32[]{:S(2)}) copy-start(s32[4]{0:T(128)} %get-tuple-element.11.slot_rot_ref) | copy-start | bytes 52
  43.6 11.2 %copy-start.5 = (bf16[256,256]{1,0:T(8,128)(2,1)S(1)}, bf16[256,256]{1,0:T(8,128)(2,1)}, u32[]{:S(2)}) copy-start(bf16[256,256]{1,0:T(8,128)(2,1)} %constant.29.clone.table_ref) | copy-start | bytes 393220
  43.7 31.6 %copy-start.1 = (bf16[2,256,256]{2,1,0:T(8,128)(2,1)S(1)}, bf16[2,256,256]{2,1,0:T(8,128)(2,1)}, u32[]{:S(2)}) copy-start(bf16[2,256,256]{2,1,0:T(8,128)(2,1)} %constant.30.clone.table_ref) | copy-start | bytes 786436
  45.2 6.9 %collective-permute-start.4 = (f32[4,512]{1,0:T(4,128)S(1)}, f32[4,512]{1,0:T(4,128)S(1)}, u32[]{:S(2)}, u32[]{:S(2)}) collective-permute-start(f32[4,512]{1,0:T(4,128)S(1)} %reshape.72), channel_id=1, source_target_pairs={{0,1},{1,0},{2,3},{3,2},{4,5},{5,4},{6,7},{7,6},{8,9},{9,8},{10,11... | collective-permute-start | bytes 24584 | tf_op jit(solution)/shard_map/ppermute | solution.py:519
  52.1 13.2 %collective-permute-start.5 = (f32[8,512]{1,0:T(8,128)S(1)}, f32[8,512]{1,0:T(8,128)S(1)}, u32[]{:S(2)}, u32[]{:S(2)}) collective-permute-start(f32[8,512]{1,0:T(8,128)S(1)} %pad_maximum_fusion.2), channel_id=1, source_target_pairs={{0,2},{1,3},{2,0},{3,1},{4,6},{5,7},{6,4},{7,5},{8,10},{9,11},{10,... | collective-permute-start | bytes 49160 | tf_op jit(solution)/shard_map/ppermute | solution.py:519
  56.3 19.0 %all-to-all-start.2 = ((bf16[16,64,128]{2,1,0:T(8,128)(2,1)}), bf16[16,64,128]{2,1,0:T(8,128)(2,1)S(1)}, u32[]{:S(2)}, u32[]{:S(2)}) async-start(bf16[16,64,128]{2,1,0:T(8,128)(2,1)} %bitcast.12), calls=%async_computation.2 | async-start | bytes 524288 | tf_op jit(solution)/shard_map/all_to_all | solution.py:541
  65.4 4.5 %collective-permute-start.6 = (f32[16,512]{1,0:T(8,128)S(1)}, f32[16,512]{1,0:T(8,128)S(1)}, u32[]{:S(2)}, u32[]{:S(2)}) collective-permute-start(f32[16,512]{1,0:T(8,128)S(1)} %pad_maximum_fusion.1), channel_id=1, source_target_pairs={{0,4},{1,5},{2,6},{3,7},{4,0},{5,1},{6,2},{7,3},{8,12},{9,13},{10,... | collective-permute-start | bytes 98312 | tf_op jit(solution)/shard_map/ppermute | solution.py:519

commit v5 on v3

--- a/solution.py
+++ b/solution.py
@@ -95,17 +95,21 @@
 
 
 def fan_kernel(refs_ref, out_hbm, wide_s, block_s, sems):
-    for rot in range(ROT_CLS):
-        wide_s[rot * PLANES : (rot + 1) * PLANES] = refs_ref[rot].astype(F32)
-    block_s[...] = wide_s[...].astype(BF)
-    copies = [
-        pltpu.make_async_copy(
-            block_s, out_hbm.at[chip * PER_CHIP : (chip + 1) * PER_CHIP], sems.at[chip]
-        )
-        for chip in range(CHIPS)
-    ]
-    for copy in copies:
-        copy.start()
+    copies = []
+    for half in range(2):
+        lanes = slice(half * BOX * PAIRS, (half + 1) * BOX * PAIRS)
+        for rot in range(ROT_CLS):
+            wide_s[rot * PLANES : (rot + 1) * PLANES, lanes] = refs_ref[rot, :, lanes].astype(F32)
+        block_s[:, lanes] = wide_s[:, lanes].astype(BF)
+        for chip in range(CHIPS):
+            copies.append(
+                pltpu.make_async_copy(
+                    block_s.at[:, lanes],
+                    out_hbm.at[chip * PER_CHIP : (chip + 1) * PER_CHIP, lanes],
+                    sems.at[half, chip],
+                )
+            )
+            copies[-1].start()
     for copy in copies:
         copy.wait()
 
@@ -358,7 +362,8 @@
     out_ref[...] = g_s[...].astype(BF)
 
 
-def x_rows_kernel(rows_ref, table_ref, out_ref):
+def x_rows_kernel(rows_ref, table_ref, out_hbm, out_s, sems):
+    copies = []
     rows = ROT_CLS * (BOX // DOM)
     first = lax.broadcasted_iota(jnp.int32, (ROT_CLS * BOX, 128), 1) < BOX
     for ky in range(BOX // DOM):
@@ -367,7 +372,11 @@
         sin_part = jnp.dot(table_ref[1], grid, preferred_element_type=F32)
         turned = pltpu.roll(sin_part, BOX, 1)
         total = (cos_part + jnp.where(first, turned, -turned)) * (float(BOX) ** -1.5)
-        out_ref[ky] = total.reshape(ROT_CLS, BOX, 128)
+        out_s[ky] = total.reshape(ROT_CLS, BOX, 128)
+        copies.append(pltpu.make_async_copy(out_s.at[ky], out_hbm.at[ky], sems.at[ky]))
+        copies[-1].start()
+    for copy in copies:
+        copy.wait()
 
 
 VMEM = pl.BlockSpec(memory_space=pltpu.VMEM)
@@ -397,7 +406,7 @@
         scratch_shapes=[
             pltpu.VMEM((PER_CHIP, voxels), F32),
             pltpu.VMEM((PER_CHIP, voxels), BF),
-            pltpu.SemaphoreType.DMA((CHIPS,)),
+            pltpu.SemaphoreType.DMA((2, CHIPS)),
         ],
         compiler_params=params(54),
         cost_estimate=cost(1024, 1024),
@@ -532,7 +541,11 @@
         x_rows_kernel,
         out_shape=jax.ShapeDtypeStruct((BOX // DOM, ROT_CLS, BOX, 2 * BOX), F32),
         in_specs=[VMEM, VMEM],
-        out_specs=VMEM,
+        out_specs=HBM,
+        scratch_shapes=[
+            pltpu.VMEM((BOX // DOM, ROT_CLS, BOX, 2 * BOX), F32),
+            pltpu.SemaphoreType.DMA((BOX // DOM,)),
+        ],
         compiler_params=params(50),
         name="x_rows",
     )(by_rows.reshape(DOM, PLANES * PER_CHIP, 2 * BOX), jnp.asarray(x_rows_table().astype(BF)))

time: 66.5 us -> 66.6 us (level)
    ppermute x3, waiting for transfers between devices: 6.06 us -> 7.25 us  [shards(): lax.ppermute(everywhere, 'rot', [(i, i ^ bit) for i in range(8)])]
    ppermute x3, starting transfers between devices: 4.04 us -> 3.09 us  [shards(): lax.ppermute(everywhere, 'rot', [(i, i ^ bit) for i in range(8)])]
where the time goes in v5:
time: 66.6 us; the launch traced here: 66.2 us
  starting transfers between devices  23.1 us (35%)
  Pallas kernels  21 us (32%)
  waiting for transfers between devices  19.3 us (29%)
  between operations  1.5 us (2%)
  other arithmetic  1.04 us (2%)
    all_to_all x1, starting transfers between devices, shards(): lax.all_to_all(mine_refs, 'dom', 0, 0, tiled=True, axis_index_groups=SAME...  8.51 us
    ppermute x3, waiting for transfers between devices, shards(): lax.ppermute(everywhere, 'rot', [(i, i ^ bit) for i in range(8)])  7.25 us
    all_to_all x1, waiting for transfers between devices, shards(): lax.all_to_all(pair_sum, 'dom', 0, 0, tiled=True, axis_index_groups=SAME_...  6.19 us
    pallas_call x1, Pallas kernels, shards(): pl.pallas_call(spectra_kernel, out_shape=jax.ShapeDtypeStruct((CAP, PAIRS...  5.58 us
    pallas_call x1, Pallas kernels, shards(): pl.pallas_call(score_kernel, out_shape=jax.ShapeDtypeStruct((CAP, SHIFTS...  4.96 us
    pallas_call x1, Pallas kernels, shards(): pl.pallas_call(send_kernel, out_shape=(jax.ShapeDtypeStruct((SEND, voxels...  4.47 us
    all_to_all x1, starting transfers between devices, shards(): by_rows = lax.all_to_all(grids, 'dom', 0, 0, tiled=True)  4.45 us
    all_to_all x1, starting transfers between devices, shards(): lax.all_to_all(pair_sum, 'dom', 0, 0, tiled=True, axis_index_groups=SAME_...  3.69 us
  transfers between devices with their start and end apart: 8, of which 5 were waited for; matrix products, arithmetic and copies ran while one was open for 2% of the time, Pallas kernels for 20%

profile of v5, /device:TPU:1, one launch (start us, length us, event | category | flops | bytes accessed | tf_op | source)
XLA Modules:
  0.0 66.2 jit_solution(10152696593122564095)
XLA Ops:
  0.6 2.1 %fan.1 = bf16[128,4096]{1,0:T(8,128)(2,1)} custom-call(bf16[4,4,4096]{2,1,0:T(4,128)(2,1)} %refs_ref.1), custom_call_target="tpu_custom_call" | custom-call | flops 1024 | bytes 1024 | tf_op jit(solution)/shard_map/fan/pallas_call | solution.py:401
  2.7 8.5 %all-to-all-start = ((bf16[8,16,4096]{2,1,0:T(8,128)(2,1)}), bf16[8,16,4096]{2,1,0:T(8,128)(2,1)S(1)}, u32[]{:S(2)}, u32[]{:S(2)}) async-start(bf16[8,16,4096]{2,1,0:T(8,128)(2,1)} %bitcast.28), calls=%async_computation | async-start | bytes 2097152 | tf_op jit(solution)/shard_map/all_to_all | solution.py:454
  11.9 4.5 %send.1 = (bf16[128,4096]{1,0:T(8,128)(2,1)}, bf16[128,4096]{1,0:T(8,128)(2,1)}, s32[1]{0:T(128)}, s32[4]{0:T(128)}, s32[4]{0:T(128)}) custom-call(s32[8]{0:T(128)} %bitcast.30, s32[8]{0:T(128)} %rot_ref.1, s32[8]{0:T(128)} %bucket_ref.1, s32[1]{0:T(128)} %copy.20.live_ref, bf16[1,8]{1,0:T(2,128)(2,1)} %bitcast.32, bf16[512,4096]{1,0:T(8,128)(2,1)} %bitcast.26), custom_call_target="tpu_custom_call" | custom-call | flops 1024 | bytes 1024 | tf_op jit(solution)/shard_map/send/pallas_call | solution.py:430
  16.4 1.2 %collective-permute-start = (bf16[128,4096]{1,0:T(8,128)(2,1)}, bf16[128,4096]{1,0:T(8,128)(2,1)S(1)}, u32[]{:S(2)}, u32[]{:S(2)}) collective-permute-start(bf16[128,4096]{1,0:T(8,128)(2,1)} %get-tuple-element.14), channel_id=1, source_target_pairs={{0,8},{8,0},{16,24},{24,16},{32,40},{40,32},{48,56},{56,48},{64,72... | collective-permute-start | bytes 3145736 | tf_op jit(solution)/shard_map/ppermute | solution.py:453
  17.6 5.6 %spectra.1.zp_hbm = bf16[4,1536,256]{2,1,0:T(8,128)(2,1)} custom-call(s32[4]{0:T(128)} %get-tuple-element.12.slot_row_ref, s32[1]{0:T(128)} %get-tuple-element.10.count_ref, bf16[96,64]{1,0:T(8,128)(2,1)} %constant.25.clone.x_ref, bf16[512,4096]{1,0:T(8,128)(2,1)} %bitcast.27, bf16[256,256]{1,0:T(8,128)(2,1)} %constant.24.clone.table_ref), custom_call_target="tpu_custom_call" | custom-call | flops 20000000000 | bytes 1024 | tf_op jit(solution)/shard_map/spectra/pallas_call | solution.py:468
  23.2 0.0 copy-start.8
  23.2 0.0 copy-start.2
  23.2 0.0 copy-start.3
  23.2 0.0 copy-start.5
  23.2 0.0 copy-start.6
  23.3 0.0 collective-permute-done.other_ref
  23.3 1.2 %pair.1 = bf16[128,4096]{1,0:T(8,128)(2,1)} custom-call(bf16[128,4096]{1,0:T(8,128)(2,1)S(1)} %copy-done, bf16[128,4096]{1,0:T(8,128)(2,1)S(1)} %collective-permute-done.other_ref), custom_call_target="tpu_custom_call" | custom-call | flops 1024 | bytes 1024 | tf_op jit(solution)/shard_map/pair/pallas_call | solution.py:457
  24.5 2.7 %all-to-all-done = bf16[8,16,4096]{2,1,0:T(8,128)(2,1)S(1)} async-done(((bf16[8,16,4096]{2,1,0:T(8,128)(2,1)}), bf16[8,16,4096]{2,1,0:T(8,128)(2,1)S(1)}, u32[]{:S(2)}, u32[]{:S(2)}) %all-to-all-start) | async-done | bytes 1048608 | tf_op jit(solution)/shard_map/all_to_all | solution.py:454
  27.2 2.2 %collective-permute-start.1 = (bf16[128,4096]{1,0:T(8,128)(2,1)S(1)}, bf16[128,4096]{1,0:T(8,128)(2,1)}, u32[]{:S(2)}, u32[]{:S(2)}) collective-permute-start(bf16[128,4096]{1,0:T(8,128)(2,1)S(1)} %bitcast.24), channel_id=1, source_target_pairs={{0,8},{8,0},{16,24},{24,16},{32,40},{40,32},{48,56},{56,48},{64,72... | collective-permute-start | bytes 3145736 | tf_op jit(solution)/shard_map/ppermute | solution.py:482
  29.4 3.7 %all-to-all-start.1 = ((bf16[8,16,4096]{2,1,0:T(8,128)(2,1)}), bf16[8,16,4096]{2,1,0:T(8,128)(2,1)S(1)}, u32[]{:S(2)}, u32[]{:S(2)}) async-start(bf16[8,16,4096]{2,1,0:T(8,128)(2,1)} %bitcast.10), calls=%async_computation.1 | async-start | bytes 2097152 | tf_op jit(solution)/shard_map/all_to_all | solution.py:481
  33.1 0.2 convert_reduce_fusion
  33.3 0.0 collective-permute-done.1.other_ref
  33.3 0.0 copy-start.1
  33.4 5.0 %slot_scores.1 = f32[4,64,128]{2,1,0:T(8,128)S(1)} custom-call(s32[1]{0:T(128)} %get-tuple-element.10.count_ref, s32[4]{0:T(128)S(1)} %copy-done.7, bf16[4,1536,256]{2,1,0:T(8,128)(2,1)} %spectra.1.zp_hbm, f32[2,96,128]{2,1,0:T(8,128)S(1)} %copy-done.5, bf16[128,4096]{1,0:T(8,128)(2,1)S(1)} %bitcast.25, bf16[128,4096]{1,0:T(8,128)(2,1)} %collective-permute-done.1.other_ref, ...), custom_call_target="tpu_custom_call" | custom-call | flops 1024 | bytes 1024 | tf_op jit(solution)/shard_map/slot_scores/pallas_call | solution.py:485
  38.4 0.1 reshape.72
  38.5 0.1 collective-permute-start.2
  38.6 2.8 %collective-permute-done.2 = f32[4,512]{1,0:T(4,128)S(1)} collective-permute-done((f32[4,512]{1,0:T(4,128)S(1)}, f32[4,512]{1,0:T(4,128)S(1)}, u32[]{:S(2)}, u32[]{:S(2)}) %collective-permute-start.2) | collective-permute-done | bytes 8224 | tf_op jit(solution)/shard_map/ppermute | solution.py:517
  41.4 2.8 %collective-permute-start.3 = (f32[8,512]{1,0:T(8,128)S(1)}, f32[8,512]{1,0:T(8,128)S(1)}, u32[]{:S(2)}, u32[]{:S(2)}) collective-permute-start(f32[8,512]{1,0:T(8,128)S(1)} %pad_maximum_fusion.2), channel_id=1, source_target_pairs={{0,2},{1,3},{2,0},{3,1},{4,6},{5,7},{6,4},{7,5},{8,10},{9,11},{10,... | collective-permute-start | bytes 49160 | tf_op jit(solution)/shard_map/ppermute | solution.py:517
  44.2 6.2 %all-to-all-done.1 = bf16[8,16,4096]{2,1,0:T(8,128)(2,1)S(1)} async-done(((bf16[8,16,4096]{2,1,0:T(8,128)(2,1)}), bf16[8,16,4096]{2,1,0:T(8,128)(2,1)S(1)}, u32[]{:S(2)}, u32[]{:S(2)}) %all-to-all-start.1) | async-done | bytes 1048608 | tf_op jit(solution)/shard_map/all_to_all | solution.py:481
  50.4 1.5 %yz_planes.1 = bf16[1024,128]{1,0:T(8,128)(2,1)} custom-call(bf16[128,4096]{1,0:T(8,128)(2,1)S(1)} %bitcast.23, bf16[256,256]{1,0:T(8,128)(2,1)S(1)} %copy-done.4), custom_call_target="tpu_custom_call" | custom-call | flops 1024 | bytes 1024 | tf_op jit(solution)/shard_map/yz_planes/pallas_call | solution.py:529
  51.9 4.4 %all-to-all-start.2 = ((bf16[16,64,128]{2,1,0:T(8,128)(2,1)}), bf16[16,64,128]{2,1,0:T(8,128)(2,1)S(1)}, u32[]{:S(2)}, u32[]{:S(2)}) async-start(bf16[16,64,128]{2,1,0:T(8,128)(2,1)} %bitcast.12), calls=%async_computation.2 | async-start | bytes 524288 | tf_op jit(solution)/shard_map/all_to_all | solution.py:539
  56.4 0.2 collective-permute-start.4
  56.5 0.1 fusion.1
  56.6 4.5 %collective-permute-done.4 = f32[16,512]{1,0:T(8,128)S(1)} collective-permute-done((f32[16,512]{1,0:T(8,128)S(1)}, f32[16,512]{1,0:T(8,128)S(1)}, u32[]{:S(2)}, u32[]{:S(2)}) %collective-permute-start.4) | collective-permute-done | bytes 32800 | tf_op jit(solution)/shard_map/ppermute | solution.py:517
  61.1 0.7 %select_reduce_fusion = f32[8,512]{1,0:T(8,128)} fusion(f32[32,512]{1,0:T(8,128)S(1)} %pad_maximum_fusion, pred[8,32]{1,0:T(8,128)(4,1)S(1)} %fusion.1), kind=kLoop, calls=%fused_computation | loop fusion | flops 258048 | bytes 82176 | tf_op jit(solution)/shard_map/reduce_sum | solution.py:524
  61.9 3.2 %all-to-all-done.2.rows_ref = bf16[16,64,128]{2,1,0:T(8,128)(2,1)S(1)} async-done(((bf16[16,64,128]{2,1,0:T(8,128)(2,1)}), bf16[16,64,128]{2,1,0:T(8,128)(2,1)S(1)}, u32[]{:S(2)}, u32[]{:S(2)}) %all-to-all-start.2) | async-done | bytes 262176 | tf_op jit(solution)/shard_map/all_to_all | solution.py:539
  65.0 1.2 %x_rows.1 = f32[4,4,64,128]{3,2,1,0:T(8,128)} custom-call(bf16[16,64,128]{2,1,0:T(8,128)(2,1)S(1)} %all-to-all-done.2.rows_ref, bf16[2,256,256]{2,1,0:T(8,128)(2,1)S(1)} %copy-done.1), custom_call_target="tpu_custom_call" | custom-call | tf_op jit(solution)/shard_map/x_rows/pallas_call | solution.py:540
  (20 shorter events, 0.1 us)
Async XLA Ops:
  2.7 24.5 %all-to-all-start = ((bf16[8,16,4096]{2,1,0:T(8,128)(2,1)}), bf16[8,16,4096]{2,1,0:T(8,128)(2,1)S(1)}, u32[]{:S(2)}, u32[]{:S(2)}) async-start(bf16[8,16,4096]{2,1,0:T(8,128)(2,1)} %bitcast.28), calls=%async_computation | async-start | bytes 2097152 | tf_op jit(solution)/shard_map/all_to_all | solution.py:454
  16.4 6.9 %collective-permute-start = (bf16[128,4096]{1,0:T(8,128)(2,1)}, bf16[128,4096]{1,0:T(8,128)(2,1)S(1)}, u32[]{:S(2)}, u32[]{:S(2)}) collective-permute-start(bf16[128,4096]{1,0:T(8,128)(2,1)} %get-tuple-element.14), channel_id=1, source_target_pairs={{0,8},{8,0},{16,24},{24,16},{32,40},{40,32},{48,56},{56,48},{64,72... | collective-permute-start | bytes 3145736 | tf_op jit(solution)/shard_map/ppermute | solution.py:453
  17.6 5.7 %copy-start = (bf16[128,4096]{1,0:T(8,128)(2,1)S(1)}, bf16[128,4096]{1,0:T(8,128)(2,1)}, u32[]{:S(2)}) copy-start(bf16[128,4096]{1,0:T(8,128)(2,1)} %get-tuple-element.13.own_ref) | copy-start | bytes 3145732
  23.2 9.9 %copy-start.8 = (s32[8,1]{0,1:T(1,128)S(1)}, s32[8,1]{0,1:T(1,128)}, u32[]{:S(2)}) copy-start(s32[8,1]{0,1:T(1,128)} %param.16) | copy-start | bytes 100
  23.2 10.1 %copy-start.2 = (bf16[256,256]{1,0:T(8,128)(2,1)S(1)}, bf16[256,256]{1,0:T(8,128)(2,1)}, u32[]{:S(2)}) copy-start(bf16[256,256]{1,0:T(8,128)(2,1)} %constant.24.clone.table_ref) | copy-start | bytes 393220
  23.2 10.1 %copy-start.3 = (bf16[512,128]{1,0:T(8,128)(2,1)S(1)}, bf16[512,128]{1,0:T(8,128)(2,1)}, u32[]{:S(2)}) copy-start(bf16[512,128]{1,0:T(8,128)(2,1)} %constant.28.clone.wz_ref) | copy-start | bytes 393220
  23.2 10.1 %copy-start.5 = (f32[2,96,128]{2,1,0:T(8,128)S(1)}, f32[2,96,128]{2,1,0:T(8,128)}, u32[]{:S(2)}) copy-start(f32[2,96,128]{2,1,0:T(8,128)} %constant.26.clone.x_ref) | copy-start | bytes 294916
  23.2 10.1 %copy-start.6 = (bf16[16,40]{1,0:T(8,128)(2,1)S(1)}, bf16[16,40]{1,0:T(8,128)(2,1)}, u32[]{:S(2)}) copy-start(bf16[16,40]{1,0:T(8,128)(2,1)} %constant.27.clone.ex_ref) | copy-start | bytes 3844
  23.2 10.1 %copy-start.7 = (s32[4]{0:T(128)S(1)}, s32[4]{0:T(128)}, u32[]{:S(2)}) copy-start(s32[4]{0:T(128)} %get-tuple-element.11.slot_rot_ref) | copy-start | bytes 52
  27.2 6.1 %collective-permute-start.1 = (bf16[128,4096]{1,0:T(8,128)(2,1)S(1)}, bf16[128,4096]{1,0:T(8,128)(2,1)}, u32[]{:S(2)}, u32[]{:S(2)}) collective-permute-start(bf16[128,4096]{1,0:T(8,128)(2,1)S(1)} %bitcast.24), channel_id=1, source_target_pairs={{0,8},{8,0},{16,24},{24,16},{32,40},{40,32},{48,56},{56,48},{64,72... | collective-permute-start | bytes 3145736 | tf_op jit(solution)/shard_map/ppermute | solution.py:482
  29.4 21.0 %copy-start.4 = (bf16[256,256]{1,0:T(8,128)(2,1)S(1)}, bf16[256,256]{1,0:T(8,128)(2,1)}, u32[]{:S(2)}) copy-start(bf16[256,256]{1,0:T(8,128)(2,1)} %constant.29.clone.table_ref) | copy-start | bytes 393220
  29.4 21.0 %all-to-all-start.1 = ((bf16[8,16,4096]{2,1,0:T(8,128)(2,1)}), bf16[8,16,4096]{2,1,0:T(8,128)(2,1)S(1)}, u32[]{:S(2)}, u32[]{:S(2)}) async-start(bf16[8,16,4096]{2,1,0:T(8,128)(2,1)} %bitcast.10), calls=%async_computation.1 | async-start | bytes 2097152 | tf_op jit(solution)/shard_map/all_to_all | solution.py:481
  33.3 31.7 %copy-start.1 = (bf16[2,256,256]{2,1,0:T(8,128)(2,1)S(1)}, bf16[2,256,256]{2,1,0:T(8,128)(2,1)}, u32[]{:S(2)}) copy-start(bf16[2,256,256]{2,1,0:T(8,128)(2,1)} %constant.30.clone.table_ref) | copy-start | bytes 786436
  38.5 2.9 %collective-permute-start.2 = (f32[4,512]{1,0:T(4,128)S(1)}, f32[4,512]{1,0:T(4,128)S(1)}, u32[]{:S(2)}, u32[]{:S(2)}) collective-permute-start(f32[4,512]{1,0:T(4,128)S(1)} %reshape.72), channel_id=1, source_target_pairs={{0,1},{1,0},{2,3},{3,2},{4,5},{5,4},{6,7},{7,6},{8,9},{9,8},{10,11... | collective-permute-start | bytes 24584 | tf_op jit(solution)/shard_map/ppermute | solution.py:517
  41.4 15.0 %collective-permute-start.3 = (f32[8,512]{1,0:T(8,128)S(1)}, f32[8,512]{1,0:T(8,128)S(1)}, u32[]{:S(2)}, u32[]{:S(2)}) collective-permute-start(f32[8,512]{1,0:T(8,128)S(1)} %pad_maximum_fusion.2), channel_id=1, source_target_pairs={{0,2},{1,3},{2,0},{3,1},{4,6},{5,7},{6,4},{7,5},{8,10},{9,11},{10,... | collective-permute-start | bytes 49160 | tf_op jit(solution)/shard_map/ppermute | solution.py:517
  51.9 13.1 %all-to-all-start.2 = ((bf16[16,64,128]{2,1,0:T(8,128)(2,1)}), bf16[16,64,128]{2,1,0:T(8,128)(2,1)S(1)}, u32[]{:S(2)}, u32[]{:S(2)}) async-start(bf16[16,64,128]{2,1,0:T(8,128)(2,1)} %bitcast.12), calls=%async_computation.2 | async-start | bytes 524288 | tf_op jit(solution)/shard_map/all_to_all | solution.py:539
  56.4 4.7 %collective-permute-start.4 = (f32[16,512]{1,0:T(8,128)S(1)}, f32[16,512]{1,0:T(8,128)S(1)}, u32[]{:S(2)}, u32[]{:S(2)}) collective-permute-start(f32[16,512]{1,0:T(8,128)S(1)} %pad_maximum_fusion.1), channel_id=1, source_target_pairs={{0,4},{1,5},{2,6},{3,7},{4,0},{5,1},{6,2},{7,3},{8,12},{9,13},{10,... | collective-permute-start | bytes 98312 | tf_op jit(solution)/shard_map/ppermute | solution.py:517

commit v6 on v5

--- a/solution.py
+++ b/solution.py
@@ -276,8 +276,7 @@
         xr = x_s.at[slot]
         for start in range(0, PAIRS, STEP):
             part = z_stage(xr, table, start, STEP)
-            part = part.astype(BF).astype(F32).reshape(STEP, KXP, 4 * BOX)
-            r_s[start : start + STEP] = part[:, :KXV, :]
+            r_s[start : start + STEP] = part.reshape(STEP, KXP, 4 * BOX)[:, :KXV, :]
             mine = zp_s[slot, start * KXP : (start + STEP) * KXP, :].astype(F32)
             p_s[start : start + STEP] = mine.reshape(STEP, KXP, 4 * BOX)[:, :KXV, :]
         first = lax.broadcasted_iota(jnp.int32, (8, 128), 1) < BOX

time: 66.6 us -> 67.5 us (1.014); the launches traced: 66.2 us -> 66.4 us
  starting transfers between devices: 23.1 us -> 26.4 us
  waiting for transfers between devices: 19.3 us -> 16.3 us
    ppermute x3, starting transfers between devices: 3.09 us -> 6.63 us  [shards(): lax.ppermute(everywhere, 'rot', [(i, i ^ bit) for i in range(8)])]
    all_to_all x1, waiting for transfers between devices: 3.16 us -> 0.01 us  [shards(): by_rows = lax.all_to_all(grids, 'dom', 0, 0, tiled=True)]
  transfers between devices with their start and end apart: 8 -> 8, of which waited for: 5 -> 4; matrix products, arithmetic and copies ran while one was open for 2% -> 2% of each run, Pallas kernels for 20% -> 20%
where the time goes in v6:
time: 67.5 us; the launch traced here: 66.4 us
  starting transfers between devices  26.4 us (39%)
  Pallas kernels  20.9 us (31%)
  waiting for transfers between devices  16.3 us (24%)
  between operations  1.5 us (2%)
  other arithmetic  1.04 us (2%)
    all_to_all x1, starting transfers between devices, shards(): lax.all_to_all(mine_refs, 'dom', 0, 0, tiled=True, axis_index_groups=SAME...  8.51 us
    ppermute x3, waiting for transfers between devices, shards(): lax.ppermute(everywhere, 'rot', [(i, i ^ bit) for i in range(8)])  7.36 us
    ppermute x3, starting transfers between devices, shards(): lax.ppermute(everywhere, 'rot', [(i, i ^ bit) for i in range(8)])  6.63 us
    all_to_all x1, waiting for transfers between devices, shards(): lax.all_to_all(pair_sum, 'dom', 0, 0, tiled=True, axis_index_groups=SAME_...  6.19 us
    pallas_call x1, Pallas kernels, shards(): pl.pallas_call(spectra_kernel, out_shape=jax.ShapeDtypeStruct((CAP, PAIRS...  5.58 us
    pallas_call x1, Pallas kernels, shards(): pl.pallas_call(score_kernel, out_shape=jax.ShapeDtypeStruct((CAP, SHIFTS...  4.96 us
    pallas_call x1, Pallas kernels, shards(): pl.pallas_call(send_kernel, out_shape=(jax.ShapeDtypeStruct((SEND, voxels...  4.43 us
    all_to_all x1, starting transfers between devices, shards(): by_rows = lax.all_to_all(grids, 'dom', 0, 0, tiled=True)  4.15 us
  transfers between devices with their start and end apart: 8, of which 4 were waited for; matrix products, arithmetic and copies ran while one was open for 2% of the time, Pallas kernels for 20%

profile of v6, /device:TPU:1, one launch (start us, length us, event | category | flops | bytes accessed | tf_op | source)
XLA Modules:
  0.0 66.4 jit_solution(6692991773942095574)
XLA Ops:
  0.6 2.1 %fan.1 = bf16[128,4096]{1,0:T(8,128)(2,1)} custom-call(bf16[4,4,4096]{2,1,0:T(4,128)(2,1)} %refs_ref.1), custom_call_target="tpu_custom_call" | custom-call | flops 1024 | bytes 1024 | tf_op jit(solution)/shard_map/fan/pallas_call | solution.py:400
  2.7 8.5 %all-to-all-start = ((bf16[8,16,4096]{2,1,0:T(8,128)(2,1)}), bf16[8,16,4096]{2,1,0:T(8,128)(2,1)S(1)}, u32[]{:S(2)}, u32[]{:S(2)}) async-start(bf16[8,16,4096]{2,1,0:T(8,128)(2,1)} %bitcast.28), calls=%async_computation | async-start | bytes 2097152 | tf_op jit(solution)/shard_map/all_to_all | solution.py:453
  11.9 4.4 %send.1 = (bf16[128,4096]{1,0:T(8,128)(2,1)}, bf16[128,4096]{1,0:T(8,128)(2,1)}, s32[1]{0:T(128)}, s32[4]{0:T(128)}, s32[4]{0:T(128)}) custom-call(s32[8]{0:T(128)} %bitcast.30, s32[8]{0:T(128)} %rot_ref.1, s32[8]{0:T(128)} %bucket_ref.1, s32[1]{0:T(128)} %copy.20.live_ref, bf16[1,8]{1,0:T(2,128)(2,1)} %bitcast.32, bf16[512,4096]{1,0:T(8,128)(2,1)} %bitcast.26), custom_call_target="tpu_custom_call" | custom-call | flops 1024 | bytes 1024 | tf_op jit(solution)/shard_map/send/pallas_call | solution.py:429
  16.3 1.3 %collective-permute-start = (bf16[128,4096]{1,0:T(8,128)(2,1)}, bf16[128,4096]{1,0:T(8,128)(2,1)S(1)}, u32[]{:S(2)}, u32[]{:S(2)}) collective-permute-start(bf16[128,4096]{1,0:T(8,128)(2,1)} %get-tuple-element.14), channel_id=1, source_target_pairs={{0,8},{8,0},{16,24},{24,16},{32,40},{40,32},{48,56},{56,48},{64,72... | collective-permute-start | bytes 3145736 | tf_op jit(solution)/shard_map/ppermute | solution.py:452
  17.6 5.6 %spectra.1.zp_hbm = bf16[4,1536,256]{2,1,0:T(8,128)(2,1)} custom-call(s32[4]{0:T(128)} %get-tuple-element.12.slot_row_ref, s32[1]{0:T(128)} %get-tuple-element.10.count_ref, bf16[96,64]{1,0:T(8,128)(2,1)} %constant.25.clone.x_ref, bf16[512,4096]{1,0:T(8,128)(2,1)} %bitcast.27, bf16[256,256]{1,0:T(8,128)(2,1)} %constant.24.clone.table_ref), custom_call_target="tpu_custom_call" | custom-call | flops 20000000000 | bytes 1024 | tf_op jit(solution)/shard_map/spectra/pallas_call | solution.py:467
  23.2 0.0 copy-start.8
  23.2 0.0 copy-start.2
  23.2 0.0 copy-start.3
  23.2 0.0 copy-start.5
  23.2 0.0 copy-start.6
  23.3 0.0 collective-permute-done.other_ref
  23.3 1.2 %pair.1 = bf16[128,4096]{1,0:T(8,128)(2,1)} custom-call(bf16[128,4096]{1,0:T(8,128)(2,1)S(1)} %copy-done, bf16[128,4096]{1,0:T(8,128)(2,1)S(1)} %collective-permute-done.other_ref), custom_call_target="tpu_custom_call" | custom-call | flops 1024 | bytes 1024 | tf_op jit(solution)/shard_map/pair/pallas_call | solution.py:456
  24.5 2.7 %all-to-all-done = bf16[8,16,4096]{2,1,0:T(8,128)(2,1)S(1)} async-done(((bf16[8,16,4096]{2,1,0:T(8,128)(2,1)}), bf16[8,16,4096]{2,1,0:T(8,128)(2,1)S(1)}, u32[]{:S(2)}, u32[]{:S(2)}) %all-to-all-start) | async-done | bytes 1048608 | tf_op jit(solution)/shard_map/all_to_all | solution.py:453
  27.2 2.2 %collective-permute-start.1 = (bf16[128,4096]{1,0:T(8,128)(2,1)S(1)}, bf16[128,4096]{1,0:T(8,128)(2,1)}, u32[]{:S(2)}, u32[]{:S(2)}) collective-permute-start(bf16[128,4096]{1,0:T(8,128)(2,1)S(1)} %bitcast.24), channel_id=1, source_target_pairs={{0,8},{8,0},{16,24},{24,16},{32,40},{40,32},{48,56},{56,48},{64,72... | collective-permute-start | bytes 3145736 | tf_op jit(solution)/shard_map/ppermute | solution.py:481
  29.4 3.7 %all-to-all-start.1 = ((bf16[8,16,4096]{2,1,0:T(8,128)(2,1)}), bf16[8,16,4096]{2,1,0:T(8,128)(2,1)S(1)}, u32[]{:S(2)}, u32[]{:S(2)}) async-start(bf16[8,16,4096]{2,1,0:T(8,128)(2,1)} %bitcast.10), calls=%async_computation.1 | async-start | bytes 2097152 | tf_op jit(solution)/shard_map/all_to_all | solution.py:480
  33.1 0.2 convert_reduce_fusion
  33.3 0.0 collective-permute-done.1.other_ref
  33.3 0.0 copy-start.1
  33.4 5.0 %slot_scores.1 = f32[4,64,128]{2,1,0:T(8,128)S(1)} custom-call(s32[1]{0:T(128)} %get-tuple-element.10.count_ref, s32[4]{0:T(128)S(1)} %copy-done.7, bf16[4,1536,256]{2,1,0:T(8,128)(2,1)} %spectra.1.zp_hbm, f32[2,96,128]{2,1,0:T(8,128)S(1)} %copy-done.5, bf16[128,4096]{1,0:T(8,128)(2,1)S(1)} %bitcast.25, bf16[128,4096]{1,0:T(8,128)(2,1)} %collective-permute-done.1.other_ref, ...), custom_call_target="tpu_custom_call" | custom-call | flops 1024 | bytes 1024 | tf_op jit(solution)/shard_map/slot_scores/pallas_call | solution.py:484
  38.4 0.1 reshape.72
  38.5 0.1 collective-permute-start.2
  38.6 2.8 %collective-permute-done.2 = f32[4,512]{1,0:T(4,128)S(1)} collective-permute-done((f32[4,512]{1,0:T(4,128)S(1)}, f32[4,512]{1,0:T(4,128)S(1)}, u32[]{:S(2)}, u32[]{:S(2)}) %collective-permute-start.2) | collective-permute-done | bytes 8224 | tf_op jit(solution)/shard_map/ppermute | solution.py:516
  41.4 2.8 %collective-permute-start.3 = (f32[8,512]{1,0:T(8,128)S(1)}, f32[8,512]{1,0:T(8,128)S(1)}, u32[]{:S(2)}, u32[]{:S(2)}) collective-permute-start(f32[8,512]{1,0:T(8,128)S(1)} %pad_maximum_fusion.2), channel_id=1, source_target_pairs={{0,2},{1,3},{2,0},{3,1},{4,6},{5,7},{6,4},{7,5},{8,10},{9,11},{10,... | collective-permute-start | bytes 49160 | tf_op jit(solution)/shard_map/ppermute | solution.py:516
  44.2 6.2 %all-to-all-done.1 = bf16[8,16,4096]{2,1,0:T(8,128)(2,1)S(1)} async-done(((bf16[8,16,4096]{2,1,0:T(8,128)(2,1)}), bf16[8,16,4096]{2,1,0:T(8,128)(2,1)S(1)}, u32[]{:S(2)}, u32[]{:S(2)}) %all-to-all-start.1) | async-done | bytes 1048608 | tf_op jit(solution)/shard_map/all_to_all | solution.py:480
  50.4 1.5 %yz_planes.1 = bf16[1024,128]{1,0:T(8,128)(2,1)} custom-call(bf16[128,4096]{1,0:T(8,128)(2,1)S(1)} %bitcast.23, bf16[256,256]{1,0:T(8,128)(2,1)S(1)} %copy-done.4), custom_call_target="tpu_custom_call" | custom-call | flops 1024 | bytes 1024 | tf_op jit(solution)/shard_map/yz_planes/pallas_call | solution.py:528
  51.9 4.2 %all-to-all-start.2 = ((bf16[16,64,128]{2,1,0:T(8,128)(2,1)}), bf16[16,64,128]{2,1,0:T(8,128)(2,1)S(1)}, u32[]{:S(2)}, u32[]{:S(2)}) async-start(bf16[16,64,128]{2,1,0:T(8,128)(2,1)} %bitcast.12), calls=%async_computation.2 | async-start | bytes 524288 | tf_op jit(solution)/shard_map/all_to_all | solution.py:538
  56.1 3.8 %collective-permute-start.4 = (f32[16,512]{1,0:T(8,128)S(1)}, f32[16,512]{1,0:T(8,128)S(1)}, u32[]{:S(2)}, u32[]{:S(2)}) collective-permute-start(f32[16,512]{1,0:T(8,128)S(1)} %pad_maximum_fusion.1), channel_id=1, source_target_pairs={{0,4},{1,5},{2,6},{3,7},{4,0},{5,1},{6,2},{7,3},{8,12},{9,13},{10,... | collective-permute-start | bytes 98312 | tf_op jit(solution)/shard_map/ppermute | solution.py:516
  59.8 0.1 fusion.1
  59.9 4.6 %collective-permute-done.4 = f32[16,512]{1,0:T(8,128)S(1)} collective-permute-done((f32[16,512]{1,0:T(8,128)S(1)}, f32[16,512]{1,0:T(8,128)S(1)}, u32[]{:S(2)}, u32[]{:S(2)}) %collective-permute-start.4) | collective-permute-done | bytes 32800 | tf_op jit(solution)/shard_map/ppermute | solution.py:516
  64.5 0.7 %select_reduce_fusion = f32[8,512]{1,0:T(8,128)} fusion(f32[32,512]{1,0:T(8,128)S(1)} %pad_maximum_fusion, pred[8,32]{1,0:T(8,128)(4,1)S(1)} %fusion.1), kind=kLoop, calls=%fused_computation | loop fusion | flops 258048 | bytes 82176 | tf_op jit(solution)/shard_map/reduce_sum | solution.py:523
  65.2 0.0 all-to-all-done.2.rows_ref
  65.2 1.2 %x_rows.1 = f32[4,4,64,128]{3,2,1,0:T(8,128)} custom-call(bf16[16,64,128]{2,1,0:T(8,128)(2,1)S(1)} %all-to-all-done.2.rows_ref, bf16[2,256,256]{2,1,0:T(8,128)(2,1)S(1)} %copy-done.1), custom_call_target="tpu_custom_call" | custom-call | tf_op jit(solution)/shard_map/x_rows/pallas_call | solution.py:539
  (20 shorter events, 0.1 us)
Async XLA Ops:
  2.7 24.5 %all-to-all-start = ((bf16[8,16,4096]{2,1,0:T(8,128)(2,1)}), bf16[8,16,4096]{2,1,0:T(8,128)(2,1)S(1)}, u32[]{:S(2)}, u32[]{:S(2)}) async-start(bf16[8,16,4096]{2,1,0:T(8,128)(2,1)} %bitcast.28), calls=%async_computation | async-start | bytes 2097152 | tf_op jit(solution)/shard_map/all_to_all | solution.py:453
  16.3 6.9 %collective-permute-start = (bf16[128,4096]{1,0:T(8,128)(2,1)}, bf16[128,4096]{1,0:T(8,128)(2,1)S(1)}, u32[]{:S(2)}, u32[]{:S(2)}) collective-permute-start(bf16[128,4096]{1,0:T(8,128)(2,1)} %get-tuple-element.14), channel_id=1, source_target_pairs={{0,8},{8,0},{16,24},{24,16},{32,40},{40,32},{48,56},{56,48},{64,72... | collective-permute-start | bytes 3145736 | tf_op jit(solution)/shard_map/ppermute | solution.py:452
  17.6 5.7 %copy-start = (bf16[128,4096]{1,0:T(8,128)(2,1)S(1)}, bf16[128,4096]{1,0:T(8,128)(2,1)}, u32[]{:S(2)}) copy-start(bf16[128,4096]{1,0:T(8,128)(2,1)} %get-tuple-element.13.own_ref) | copy-start | bytes 3145732
  23.2 9.9 %copy-start.8 = (s32[8,1]{0,1:T(1,128)S(1)}, s32[8,1]{0,1:T(1,128)}, u32[]{:S(2)}) copy-start(s32[8,1]{0,1:T(1,128)} %param.16) | copy-start | bytes 100
  23.2 10.1 %copy-start.2 = (bf16[256,256]{1,0:T(8,128)(2,1)S(1)}, bf16[256,256]{1,0:T(8,128)(2,1)}, u32[]{:S(2)}) copy-start(bf16[256,256]{1,0:T(8,128)(2,1)} %constant.24.clone.table_ref) | copy-start | bytes 393220
  23.2 10.1 %copy-start.3 = (bf16[512,128]{1,0:T(8,128)(2,1)S(1)}, bf16[512,128]{1,0:T(8,128)(2,1)}, u32[]{:S(2)}) copy-start(bf16[512,128]{1,0:T(8,128)(2,1)} %constant.28.clone.wz_ref) | copy-start | bytes 393220
  23.2 10.1 %copy-start.5 = (f32[2,96,128]{2,1,0:T(8,128)S(1)}, f32[2,96,128]{2,1,0:T(8,128)}, u32[]{:S(2)}) copy-start(f32[2,96,128]{2,1,0:T(8,128)} %constant.26.clone.x_ref) | copy-start | bytes 294916
  23.2 10.1 %copy-start.6 = (bf16[16,40]{1,0:T(8,128)(2,1)S(1)}, bf16[16,40]{1,0:T(8,128)(2,1)}, u32[]{:S(2)}) copy-start(bf16[16,40]{1,0:T(8,128)(2,1)} %constant.27.clone.ex_ref) | copy-start | bytes 3844
  23.2 10.1 %copy-start.7 = (s32[4]{0:T(128)S(1)}, s32[4]{0:T(128)}, u32[]{:S(2)}) copy-start(s32[4]{0:T(128)} %get-tuple-element.11.slot_rot_ref) | copy-start | bytes 52
  27.2 6.1 %collective-permute-start.1 = (bf16[128,4096]{1,0:T(8,128)(2,1)S(1)}, bf16[128,4096]{1,0:T(8,128)(2,1)}, u32[]{:S(2)}, u32[]{:S(2)}) collective-permute-start(bf16[128,4096]{1,0:T(8,128)(2,1)S(1)} %bitcast.24), channel_id=1, source_target_pairs={{0,8},{8,0},{16,24},{24,16},{32,40},{40,32},{48,56},{56,48},{64,72... | collective-permute-start | bytes 3145736 | tf_op jit(solution)/shard_map/ppermute | solution.py:481
  29.4 21.0 %copy-start.4 = (bf16[256,256]{1,0:T(8,128)(2,1)S(1)}, bf16[256,256]{1,0:T(8,128)(2,1)}, u32[]{:S(2)}) copy-start(bf16[256,256]{1,0:T(8,128)(2,1)} %constant.29.clone.table_ref) | copy-start | bytes 393220
  29.4 21.0 %all-to-all-start.1 = ((bf16[8,16,4096]{2,1,0:T(8,128)(2,1)}), bf16[8,16,4096]{2,1,0:T(8,128)(2,1)S(1)}, u32[]{:S(2)}, u32[]{:S(2)}) async-start(bf16[8,16,4096]{2,1,0:T(8,128)(2,1)} %bitcast.10), calls=%async_computation.1 | async-start | bytes 2097152 | tf_op jit(solution)/shard_map/all_to_all | solution.py:480
  33.3 31.9 %copy-start.1 = (bf16[2,256,256]{2,1,0:T(8,128)(2,1)S(1)}, bf16[2,256,256]{2,1,0:T(8,128)(2,1)}, u32[]{:S(2)}) copy-start(bf16[2,256,256]{2,1,0:T(8,128)(2,1)} %constant.30.clone.table_ref) | copy-start | bytes 786436
  38.5 2.9 %collective-permute-start.2 = (f32[4,512]{1,0:T(4,128)S(1)}, f32[4,512]{1,0:T(4,128)S(1)}, u32[]{:S(2)}, u32[]{:S(2)}) collective-permute-start(f32[4,512]{1,0:T(4,128)S(1)} %reshape.72), channel_id=1, source_target_pairs={{0,1},{1,0},{2,3},{3,2},{4,5},{5,4},{6,7},{7,6},{8,9},{9,8},{10,11... | collective-permute-start | bytes 24584 | tf_op jit(solution)/shard_map/ppermute | solution.py:516
  41.4 14.6 %collective-permute-start.3 = (f32[8,512]{1,0:T(8,128)S(1)}, f32[8,512]{1,0:T(8,128)S(1)}, u32[]{:S(2)}, u32[]{:S(2)}) collective-permute-start(f32[8,512]{1,0:T(8,128)S(1)} %pad_maximum_fusion.2), channel_id=1, source_target_pairs={{0,2},{1,3},{2,0},{3,1},{4,6},{5,7},{6,4},{7,5},{8,10},{9,11},{10,... | collective-permute-start | bytes 49160 | tf_op jit(solution)/shard_map/ppermute | solution.py:516
  51.9 13.3 %all-to-all-start.2 = ((bf16[16,64,128]{2,1,0:T(8,128)(2,1)}), bf16[16,64,128]{2,1,0:T(8,128)(2,1)S(1)}, u32[]{:S(2)}, u32[]{:S(2)}) async-start(bf16[16,64,128]{2,1,0:T(8,128)(2,1)} %bitcast.12), calls=%async_computation.2 | async-start | bytes 524288 | tf_op jit(solution)/shard_map/all_to_all | solution.py:538
  56.1 8.4 %collective-permute-start.4 = (f32[16,512]{1,0:T(8,128)S(1)}, f32[16,512]{1,0:T(8,128)S(1)}, u32[]{:S(2)}, u32[]{:S(2)}) collective-permute-start(f32[16,512]{1,0:T(8,128)S(1)} %pad_maximum_fusion.1), channel_id=1, source_target_pairs={{0,4},{1,5},{2,6},{3,7},{4,0},{5,1},{6,2},{7,3},{8,12},{9,13},{10,... | collective-permute-start | bytes 98312 | tf_op jit(solution)/shard_map/ppermute | solution.py:516

commit v7 on v5

--- a/solution.py
+++ b/solution.py
@@ -264,11 +264,11 @@
             wanted = ref_rot == slot_rot_ref[to]
             pick_s[rows, :SEND] = jnp.where(wanted, x_ref[core], 0.0).astype(BF)
             pick_s[rows, SEND:] = jnp.where(wanted, x_ref[1 - core], 0.0).astype(BF)
-        for start in range(0, BOX * BOX, 512):
-            lanes = slice(start, start + 512)
+        for start in range(0, BOX * BOX, 1024):
+            lanes = slice(start, start + 1024)
             planes = jnp.concatenate([own_ref[:, lanes], other_ref[:, lanes]], axis=0)
             part = jnp.dot(pick_s[...], planes, preferred_element_type=F32)
-            x_s[:, :, lanes] = part.astype(BF).reshape(CAP, 2 * KXP, 512)
+            x_s[:, :, lanes] = part.astype(BF).reshape(CAP, 2 * KXP, 1024)
 
     def one_slot(slot, carry):
         pltpu.make_async_copy(zp_hbm.at[slot], zp_s.at[slot], sems.at[slot]).wait()

time: 66.6 us -> 67.2 us (level)
  starting transfers between devices: 23.1 us -> 26.7 us
  waiting for transfers between devices: 19.3 us -> 16.9 us
    ppermute x3, starting transfers between devices: 3.09 us -> 5.5 us  [shards(): lax.ppermute(everywhere, 'rot', [(i, i ^ bit) for i in range(8)])]
    ppermute x3, waiting for transfers between devices: 7.25 us -> 5.44 us  [shards(): lax.ppermute(everywhere, 'rot', [(i, i ^ bit) for i in range(8)])]
    all_to_all x1, waiting for transfers between devices: 6.19 us -> 4.86 us  [shards(): lax.all_to_all(pair_sum, 'dom', 0, 0, tiled=True, axis_index_groups=SAME_...]
    all_to_all x1, starting transfers between devices: 4.45 us -> 5.67 us  [shards(): by_rows = lax.all_to_all(grids, 'dom', 0, 0, tiled=True)]
    all_to_all x1, waiting for transfers between devices: 3.16 us -> 3.89 us  [shards(): by_rows = lax.all_to_all(grids, 'dom', 0, 0, tiled=True)]
where the time goes in v7:
time: 67.2 us; the launch traced here: 67.4 us
  starting transfers between devices  26.7 us (40%)
  Pallas kernels  21 us (31%)
  waiting for transfers between devices  16.9 us (25%)
  between operations  1.49 us (2%)
  other arithmetic  1.04 us (2%)
    all_to_all x1, starting transfers between devices, shards(): lax.all_to_all(mine_refs, 'dom', 0, 0, tiled=True, axis_index_groups=SAME...  8.51 us
    all_to_all x1, starting transfers between devices, shards(): by_rows = lax.all_to_all(grids, 'dom', 0, 0, tiled=True)  5.67 us
    pallas_call x1, Pallas kernels, shards(): pl.pallas_call(spectra_kernel, out_shape=jax.ShapeDtypeStruct((CAP, PAIRS...  5.58 us
    ppermute x3, starting transfers between devices, shards(): lax.ppermute(everywhere, 'rot', [(i, i ^ bit) for i in range(8)])  5.5 us
    ppermute x3, waiting for transfers between devices, shards(): lax.ppermute(everywhere, 'rot', [(i, i ^ bit) for i in range(8)])  5.44 us
    pallas_call x1, Pallas kernels, shards(): pl.pallas_call(score_kernel, out_shape=jax.ShapeDtypeStruct((CAP, SHIFTS...  4.96 us
    all_to_all x1, waiting for transfers between devices, shards(): lax.all_to_all(pair_sum, 'dom', 0, 0, tiled=True, axis_index_groups=SAME_...  4.86 us
    pallas_call x1, Pallas kernels, shards(): pl.pallas_call(send_kernel, out_shape=(jax.ShapeDtypeStruct((SEND, voxels...  4.5 us
  transfers between devices with their start and end apart: 8, of which 5 were waited for; matrix products, arithmetic and copies ran while one was open for 2% of the time, Pallas kernels for 20%

profile of v7, /device:TPU:1, one launch (start us, length us, event | category | flops | bytes accessed | tf_op | source)
XLA Modules:
  0.0 67.4 jit_solution(370197425994480864)
XLA Ops:
  0.6 2.1 %fan.1 = bf16[128,4096]{1,0:T(8,128)(2,1)} custom-call(bf16[4,4,4096]{2,1,0:T(4,128)(2,1)} %refs_ref.1), custom_call_target="tpu_custom_call" | custom-call | flops 1024 | bytes 1024 | tf_op jit(solution)/shard_map/fan/pallas_call | solution.py:401
  2.7 8.5 %all-to-all-start = ((bf16[8,16,4096]{2,1,0:T(8,128)(2,1)}), bf16[8,16,4096]{2,1,0:T(8,128)(2,1)S(1)}, u32[]{:S(2)}, u32[]{:S(2)}) async-start(bf16[8,16,4096]{2,1,0:T(8,128)(2,1)} %bitcast.28), calls=%async_computation | async-start | bytes 2097152 | tf_op jit(solution)/shard_map/all_to_all | solution.py:454
  11.9 4.5 %send.1 = (bf16[128,4096]{1,0:T(8,128)(2,1)}, bf16[128,4096]{1,0:T(8,128)(2,1)}, s32[1]{0:T(128)}, s32[4]{0:T(128)}, s32[4]{0:T(128)}) custom-call(s32[8]{0:T(128)} %bitcast.30, s32[8]{0:T(128)} %rot_ref.1, s32[8]{0:T(128)} %bucket_ref.1, s32[1]{0:T(128)} %copy.20.live_ref, bf16[1,8]{1,0:T(2,128)(2,1)} %bitcast.32, bf16[512,4096]{1,0:T(8,128)(2,1)} %bitcast.26), custom_call_target="tpu_custom_call" | custom-call | flops 1024 | bytes 1024 | tf_op jit(solution)/shard_map/send/pallas_call | solution.py:430
  16.4 1.2 %collective-permute-start = (bf16[128,4096]{1,0:T(8,128)(2,1)}, bf16[128,4096]{1,0:T(8,128)(2,1)S(1)}, u32[]{:S(2)}, u32[]{:S(2)}) collective-permute-start(bf16[128,4096]{1,0:T(8,128)(2,1)} %get-tuple-element.14), channel_id=1, source_target_pairs={{0,8},{8,0},{16,24},{24,16},{32,40},{40,32},{48,56},{56,48},{64,72... | collective-permute-start | bytes 3145736 | tf_op jit(solution)/shard_map/ppermute | solution.py:453
  17.6 5.6 %spectra.1.zp_hbm = bf16[4,1536,256]{2,1,0:T(8,128)(2,1)} custom-call(s32[4]{0:T(128)} %get-tuple-element.12.slot_row_ref, s32[1]{0:T(128)} %get-tuple-element.10.count_ref, bf16[96,64]{1,0:T(8,128)(2,1)} %constant.25.clone.x_ref, bf16[512,4096]{1,0:T(8,128)(2,1)} %bitcast.27, bf16[256,256]{1,0:T(8,128)(2,1)} %constant.24.clone.table_ref), custom_call_target="tpu_custom_call" | custom-call | flops 20000000000 | bytes 1024 | tf_op jit(solution)/shard_map/spectra/pallas_call | solution.py:468
  23.2 0.0 copy-start.8
  23.2 0.0 copy-start.2
  23.2 0.0 copy-start.3
  23.2 0.0 copy-start.5
  23.2 0.0 copy-start.6
  23.3 0.0 collective-permute-done.other_ref
  23.3 1.2 %pair.1 = bf16[128,4096]{1,0:T(8,128)(2,1)} custom-call(bf16[128,4096]{1,0:T(8,128)(2,1)S(1)} %copy-done, bf16[128,4096]{1,0:T(8,128)(2,1)S(1)} %collective-permute-done.other_ref), custom_call_target="tpu_custom_call" | custom-call | flops 1024 | bytes 1024 | tf_op jit(solution)/shard_map/pair/pallas_call | solution.py:457
  24.5 2.7 %all-to-all-done = bf16[8,16,4096]{2,1,0:T(8,128)(2,1)S(1)} async-done(((bf16[8,16,4096]{2,1,0:T(8,128)(2,1)}), bf16[8,16,4096]{2,1,0:T(8,128)(2,1)S(1)}, u32[]{:S(2)}, u32[]{:S(2)}) %all-to-all-start) | async-done | bytes 1048608 | tf_op jit(solution)/shard_map/all_to_all | solution.py:454
  27.2 2.2 %collective-permute-start.1 = (bf16[128,4096]{1,0:T(8,128)(2,1)S(1)}, bf16[128,4096]{1,0:T(8,128)(2,1)}, u32[]{:S(2)}, u32[]{:S(2)}) collective-permute-start(bf16[128,4096]{1,0:T(8,128)(2,1)S(1)} %bitcast.24), channel_id=1, source_target_pairs={{0,8},{8,0},{16,24},{24,16},{32,40},{40,32},{48,56},{56,48},{64,72... | collective-permute-start | bytes 3145736 | tf_op jit(solution)/shard_map/ppermute | solution.py:482
  29.4 3.7 %all-to-all-start.1 = ((bf16[8,16,4096]{2,1,0:T(8,128)(2,1)}), bf16[8,16,4096]{2,1,0:T(8,128)(2,1)S(1)}, u32[]{:S(2)}, u32[]{:S(2)}) async-start(bf16[8,16,4096]{2,1,0:T(8,128)(2,1)} %bitcast.10), calls=%async_computation.1 | async-start | bytes 2097152 | tf_op jit(solution)/shard_map/all_to_all | solution.py:481
  33.1 0.2 convert_reduce_fusion
  33.3 0.0 collective-permute-done.1.other_ref
  33.3 0.0 copy-start.1
  33.4 5.0 %slot_scores.1 = f32[4,64,128]{2,1,0:T(8,128)S(1)} custom-call(s32[1]{0:T(128)} %get-tuple-element.10.count_ref, s32[4]{0:T(128)S(1)} %copy-done.7, bf16[4,1536,256]{2,1,0:T(8,128)(2,1)} %spectra.1.zp_hbm, f32[2,96,128]{2,1,0:T(8,128)S(1)} %copy-done.5, bf16[128,4096]{1,0:T(8,128)(2,1)S(1)} %bitcast.25, bf16[128,4096]{1,0:T(8,128)(2,1)} %collective-permute-done.1.other_ref, ...), custom_call_target="tpu_custom_call" | custom-call | flops 1024 | bytes 1024 | tf_op jit(solution)/shard_map/slot_scores/pallas_call | solution.py:485
  38.4 0.1 reshape.72
  38.5 1.3 %collective-permute-start.2 = (f32[4,512]{1,0:T(4,128)S(1)}, f32[4,512]{1,0:T(4,128)S(1)}, u32[]{:S(2)}, u32[]{:S(2)}) collective-permute-start(f32[4,512]{1,0:T(4,128)S(1)} %reshape.72), channel_id=1, source_target_pairs={{0,1},{1,0},{2,3},{3,2},{4,5},{5,4},{6,7},{7,6},{8,9},{9,8},{10,11... | collective-permute-start | bytes 24584 | tf_op jit(solution)/shard_map/ppermute | solution.py:517
  39.8 1.6 %collective-permute-done.2 = f32[4,512]{1,0:T(4,128)S(1)} collective-permute-done((f32[4,512]{1,0:T(4,128)S(1)}, f32[4,512]{1,0:T(4,128)S(1)}, u32[]{:S(2)}, u32[]{:S(2)}) %collective-permute-start.2) | collective-permute-done | bytes 8224 | tf_op jit(solution)/shard_map/ppermute | solution.py:517
  41.4 4.1 %collective-permute-start.3 = (f32[8,512]{1,0:T(8,128)S(1)}, f32[8,512]{1,0:T(8,128)S(1)}, u32[]{:S(2)}, u32[]{:S(2)}) collective-permute-start(f32[8,512]{1,0:T(8,128)S(1)} %pad_maximum_fusion.2), channel_id=1, source_target_pairs={{0,2},{1,3},{2,0},{3,1},{4,6},{5,7},{6,4},{7,5},{8,10},{9,11},{10,... | collective-permute-start | bytes 49160 | tf_op jit(solution)/shard_map/ppermute | solution.py:517
  45.5 4.9 %all-to-all-done.1 = bf16[8,16,4096]{2,1,0:T(8,128)(2,1)S(1)} async-done(((bf16[8,16,4096]{2,1,0:T(8,128)(2,1)}), bf16[8,16,4096]{2,1,0:T(8,128)(2,1)S(1)}, u32[]{:S(2)}, u32[]{:S(2)}) %all-to-all-start.1) | async-done | bytes 1048608 | tf_op jit(solution)/shard_map/all_to_all | solution.py:481
  50.4 1.5 %yz_planes.1 = bf16[1024,128]{1,0:T(8,128)(2,1)} custom-call(bf16[128,4096]{1,0:T(8,128)(2,1)S(1)} %bitcast.23, bf16[256,256]{1,0:T(8,128)(2,1)S(1)} %copy-done.4), custom_call_target="tpu_custom_call" | custom-call | flops 1024 | bytes 1024 | tf_op jit(solution)/shard_map/yz_planes/pallas_call | solution.py:529
  51.9 5.7 %all-to-all-start.2 = ((bf16[16,64,128]{2,1,0:T(8,128)(2,1)}), bf16[16,64,128]{2,1,0:T(8,128)(2,1)S(1)}, u32[]{:S(2)}, u32[]{:S(2)}) async-start(bf16[16,64,128]{2,1,0:T(8,128)(2,1)} %bitcast.12), calls=%async_computation.2 | async-start | bytes 524288 | tf_op jit(solution)/shard_map/all_to_all | solution.py:539
  57.6 0.1 collective-permute-start.4
  57.7 0.1 fusion.1
  57.8 3.8 %collective-permute-done.4 = f32[16,512]{1,0:T(8,128)S(1)} collective-permute-done((f32[16,512]{1,0:T(8,128)S(1)}, f32[16,512]{1,0:T(8,128)S(1)}, u32[]{:S(2)}, u32[]{:S(2)}) %collective-permute-start.4) | collective-permute-done | bytes 32800 | tf_op jit(solution)/shard_map/ppermute | solution.py:517
  61.6 0.7 %select_reduce_fusion = f32[8,512]{1,0:T(8,128)} fusion(f32[32,512]{1,0:T(8,128)S(1)} %pad_maximum_fusion, pred[8,32]{1,0:T(8,128)(4,1)S(1)} %fusion.1), kind=kLoop, calls=%fused_computation | loop fusion | flops 258048 | bytes 82176 | tf_op jit(solution)/shard_map/reduce_sum | solution.py:524
  62.3 3.9 %all-to-all-done.2.rows_ref = bf16[16,64,128]{2,1,0:T(8,128)(2,1)S(1)} async-done(((bf16[16,64,128]{2,1,0:T(8,128)(2,1)}), bf16[16,64,128]{2,1,0:T(8,128)(2,1)S(1)}, u32[]{:S(2)}, u32[]{:S(2)}) %all-to-all-start.2) | async-done | bytes 262176 | tf_op jit(solution)/shard_map/all_to_all | solution.py:539
  66.2 1.2 %x_rows.1 = f32[4,4,64,128]{3,2,1,0:T(8,128)} custom-call(bf16[16,64,128]{2,1,0:T(8,128)(2,1)S(1)} %all-to-all-done.2.rows_ref, bf16[2,256,256]{2,1,0:T(8,128)(2,1)S(1)} %copy-done.1), custom_call_target="tpu_custom_call" | custom-call | tf_op jit(solution)/shard_map/x_rows/pallas_call | solution.py:540
  (20 shorter events, 0.1 us)
Async XLA Ops:
  2.7 24.5 %all-to-all-start = ((bf16[8,16,4096]{2,1,0:T(8,128)(2,1)}), bf16[8,16,4096]{2,1,0:T(8,128)(2,1)S(1)}, u32[]{:S(2)}, u32[]{:S(2)}) async-start(bf16[8,16,4096]{2,1,0:T(8,128)(2,1)} %bitcast.28), calls=%async_computation | async-start | bytes 2097152 | tf_op jit(solution)/shard_map/all_to_all | solution.py:454
  16.4 6.9 %collective-permute-start = (bf16[128,4096]{1,0:T(8,128)(2,1)}, bf16[128,4096]{1,0:T(8,128)(2,1)S(1)}, u32[]{:S(2)}, u32[]{:S(2)}) collective-permute-start(bf16[128,4096]{1,0:T(8,128)(2,1)} %get-tuple-element.14), channel_id=1, source_target_pairs={{0,8},{8,0},{16,24},{24,16},{32,40},{40,32},{48,56},{56,48},{64,72... | collective-permute-start | bytes 3145736 | tf_op jit(solution)/shard_map/ppermute | solution.py:453
  17.6 5.7 %copy-start = (bf16[128,4096]{1,0:T(8,128)(2,1)S(1)}, bf16[128,4096]{1,0:T(8,128)(2,1)}, u32[]{:S(2)}) copy-start(bf16[128,4096]{1,0:T(8,128)(2,1)} %get-tuple-element.13.own_ref) | copy-start | bytes 3145732
  23.2 9.9 %copy-start.8 = (s32[8,1]{0,1:T(1,128)S(1)}, s32[8,1]{0,1:T(1,128)}, u32[]{:S(2)}) copy-start(s32[8,1]{0,1:T(1,128)} %param.16) | copy-start | bytes 100
  23.2 10.1 %copy-start.2 = (bf16[256,256]{1,0:T(8,128)(2,1)S(1)}, bf16[256,256]{1,0:T(8,128)(2,1)}, u32[]{:S(2)}) copy-start(bf16[256,256]{1,0:T(8,128)(2,1)} %constant.24.clone.table_ref) | copy-start | bytes 393220
  23.2 10.1 %copy-start.3 = (bf16[512,128]{1,0:T(8,128)(2,1)S(1)}, bf16[512,128]{1,0:T(8,128)(2,1)}, u32[]{:S(2)}) copy-start(bf16[512,128]{1,0:T(8,128)(2,1)} %constant.28.clone.wz_ref) | copy-start | bytes 393220
  23.2 10.1 %copy-start.5 = (f32[2,96,128]{2,1,0:T(8,128)S(1)}, f32[2,96,128]{2,1,0:T(8,128)}, u32[]{:S(2)}) copy-start(f32[2,96,128]{2,1,0:T(8,128)} %constant.26.clone.x_ref) | copy-start | bytes 294916
  23.2 10.1 %copy-start.6 = (bf16[16,40]{1,0:T(8,128)(2,1)S(1)}, bf16[16,40]{1,0:T(8,128)(2,1)}, u32[]{:S(2)}) copy-start(bf16[16,40]{1,0:T(8,128)(2,1)} %constant.27.clone.ex_ref) | copy-start | bytes 3844
  23.2 10.1 %copy-start.7 = (s32[4]{0:T(128)S(1)}, s32[4]{0:T(128)}, u32[]{:S(2)}) copy-start(s32[4]{0:T(128)} %get-tuple-element.11.slot_rot_ref) | copy-start | bytes 52
  27.2 6.1 %collective-permute-start.1 = (bf16[128,4096]{1,0:T(8,128)(2,1)S(1)}, bf16[128,4096]{1,0:T(8,128)(2,1)}, u32[]{:S(2)}, u32[]{:S(2)}) collective-permute-start(bf16[128,4096]{1,0:T(8,128)(2,1)S(1)} %bitcast.24), channel_id=1, source_target_pairs={{0,8},{8,0},{16,24},{24,16},{32,40},{40,32},{48,56},{56,48},{64,72... | collective-permute-start | bytes 3145736 | tf_op jit(solution)/shard_map/ppermute | solution.py:482
  29.4 21.0 %copy-start.4 = (bf16[256,256]{1,0:T(8,128)(2,1)S(1)}, bf16[256,256]{1,0:T(8,128)(2,1)}, u32[]{:S(2)}) copy-start(bf16[256,256]{1,0:T(8,128)(2,1)} %constant.29.clone.table_ref) | copy-start | bytes 393220
  29.4 21.0 %all-to-all-start.1 = ((bf16[8,16,4096]{2,1,0:T(8,128)(2,1)}), bf16[8,16,4096]{2,1,0:T(8,128)(2,1)S(1)}, u32[]{:S(2)}, u32[]{:S(2)}) async-start(bf16[8,16,4096]{2,1,0:T(8,128)(2,1)} %bitcast.10), calls=%async_computation.1 | async-start | bytes 2097152 | tf_op jit(solution)/shard_map/all_to_all | solution.py:481
  33.3 32.9 %copy-start.1 = (bf16[2,256,256]{2,1,0:T(8,128)(2,1)S(1)}, bf16[2,256,256]{2,1,0:T(8,128)(2,1)}, u32[]{:S(2)}) copy-start(bf16[2,256,256]{2,1,0:T(8,128)(2,1)} %constant.30.clone.table_ref) | copy-start | bytes 786436
  38.5 2.9 %collective-permute-start.2 = (f32[4,512]{1,0:T(4,128)S(1)}, f32[4,512]{1,0:T(4,128)S(1)}, u32[]{:S(2)}, u32[]{:S(2)}) collective-permute-start(f32[4,512]{1,0:T(4,128)S(1)} %reshape.72), channel_id=1, source_target_pairs={{0,1},{1,0},{2,3},{3,2},{4,5},{5,4},{6,7},{7,6},{8,9},{9,8},{10,11... | collective-permute-start | bytes 24584 | tf_op jit(solution)/shard_map/ppermute | solution.py:517
  41.4 16.2 %collective-permute-start.3 = (f32[8,512]{1,0:T(8,128)S(1)}, f32[8,512]{1,0:T(8,128)S(1)}, u32[]{:S(2)}, u32[]{:S(2)}) collective-permute-start(f32[8,512]{1,0:T(8,128)S(1)} %pad_maximum_fusion.2), channel_id=1, source_target_pairs={{0,2},{1,3},{2,0},{3,1},{4,6},{5,7},{6,4},{7,5},{8,10},{9,11},{10,... | collective-permute-start | bytes 49160 | tf_op jit(solution)/shard_map/ppermute | solution.py:517
  51.9 14.3 %all-to-all-start.2 = ((bf16[16,64,128]{2,1,0:T(8,128)(2,1)}), bf16[16,64,128]{2,1,0:T(8,128)(2,1)S(1)}, u32[]{:S(2)}, u32[]{:S(2)}) async-start(bf16[16,64,128]{2,1,0:T(8,128)(2,1)} %bitcast.12), calls=%async_computation.2 | async-start | bytes 524288 | tf_op jit(solution)/shard_map/all_to_all | solution.py:539
  57.6 4.0 %collective-permute-start.4 = (f32[16,512]{1,0:T(8,128)S(1)}, f32[16,512]{1,0:T(8,128)S(1)}, u32[]{:S(2)}, u32[]{:S(2)}) collective-permute-start(f32[16,512]{1,0:T(8,128)S(1)} %pad_maximum_fusion.1), channel_id=1, source_target_pairs={{0,4},{1,5},{2,6},{3,7},{4,0},{5,1},{6,2},{7,3},{8,12},{9,13},{10,... | collective-permute-start | bytes 98312 | tf_op jit(solution)/shard_map/ppermute | solution.py:517
